TPU v7x, 32 devices: a whole 2x2x4 slice. The times are simulated.
32 devices in a mesh: slab: 8 (over y, x, core), buddy: 4 (over z).
Axes of the slice: x: 2, y: 2, z: 4, core: 2. Of those that a mesh axis runs over, the one named last changes fastest.
Arguments:
- checkpoint: float32 [32, 5, 64, 4, 256], P('buddy', None, 'slab'), may hold values from -6 to 6
- slot_block: int32 [4, 8], replicated, may hold values from 0 to 31, as said below
- live_state: float32 [4, 5, 64, 32, 256], P('buddy', None, 'slab'), may hold values from -6 to 6
- levels: int32 [2, 4, 3], P(None, 'buddy'), may hold values from 0 to 2
- coefficients: float32 [2, 4], P(None, 'buddy'), may hold values from 0.3 to 1
- tile_owner: int32 [8, 16], P('slab'), may hold values from 0 to 3, as said below
Outputs:
- recovered: float32 [4, 5, 64, 32, 256], P('buddy', None, 'slab')
- combined: float32 [32, 5, 64, 2, 256], P('buddy', None, 'slab')
Inputs may be any that keep to these rules, and one draw needn't show every extreme that they name: `slot_block`: row h lists the blocks in the 8 slots of holder h, block j of grid g written g * 8 + j. Every block is held exactly once, never by its own grid's holder; one holder keeps at most 3 blocks of one grid, and some holder keeps exactly 3 of some grid. `tile_owner`: no reader reads more than 8 tiles of one slab, and in every slab some reader reads exactly 8.
All inputs are finite; a program needn't handle non-finite values.
Results may differ from a plain program's by a relative error of at most 0.000096.
Values sent between devices are 32-bit elements; how exact they have to be, the bound alone decides.
No kernel may reach another device: no remote copies, remote signals or barrier semaphores. Data moves between devices by JAX's collectives and lax.ppermute only.
A program may use at most 192 MiB of HBM per device.

v0:
```python
import functools

import jax
import jax.numpy as jnp
from jax import lax
from jax.experimental import pallas as pl
from jax.experimental.pallas import tpu as pltpu
from jax.sharding import PartitionSpec as P

VELOCITY = (0.3, -0.2, 0.45)
COURANT = 1.0
TILE_LINES = 2
HELD_MOST = 3
DEPTH = 4
LANES = 128
ROWS = 8
VMEM_BYTES = 48 * 1024 * 1024


def spec_vmem():
    return pl.BlockSpec(memory_space=pltpu.VMEM)


def spec_smem():
    return pl.BlockSpec(memory_space=pltpu.SMEM)


def spec_any():
    return pl.BlockSpec(memory_space=pl.ANY)


def params():
    return pltpu.CompilerParams(vmem_limit_bytes=VMEM_BYTES)


def shape(*dims):
    return jax.ShapeDtypeStruct(dims, jnp.float32)


def add(*terms):
    total = None
    for term in terms:
        if term is not None:
            total = term if total is None else total + term
    return total


def sub(left, right):
    if right is None:
        return left
    return -right if left is None else left - right


def mul(factor, term):
    return None if term is None else factor * term


def lane_index():
    return lax.broadcasted_iota(jnp.int32, (ROWS, LANES), 1)


def turn_lanes(value, amount):
    return None if value is None else pltpu.roll(value, amount, 1)


def split_parity(left, right):
    lane = lane_index()
    even_at = (2 * lane) % LANES
    first = lane < LANES // 2
    pick = lambda array, at: jnp.take_along_axis(array, at, axis=1)
    even = jnp.where(first, pick(left, even_at), pick(right, even_at))
    odd = jnp.where(first, pick(left, even_at + 1), pick(right, even_at + 1))
    return even, odd


def join_parity(even, odd):
    lane = lane_index()
    half = lane // 2
    is_even = lane % 2 == 0
    pick = lambda array, at: jnp.take_along_axis(array, at, axis=1)
    left = jnp.where(is_even, pick(even, half), pick(odd, half))
    right = jnp.where(is_even, pick(even, half + LANES // 2), pick(odd, half + LANES // 2))
    return left, right


def pick_rows(array, at):
    return jnp.take_along_axis(array, at, axis=0)


def direction_factors(axis_number):
    drift = VELOCITY[axis_number]
    wave = abs(drift) + 1.0
    carried = (0.5 * (wave - drift), 0.5 * (wave + drift))
    if drift >= 0:
        rising = (0.0, 0.5 * wave)
        falling = (0.5, 0.5 * drift)
    else:
        rising = (-0.5 * drift, 0.5)
        falling = (0.5 * wave, 0.0)
    return carried, rising, falling


def factor_table(spacing, time_step, weight):
    sections = []
    for number, part in enumerate((4.0, 3.0, 2.0, 1.0)):
        scale = time_step / part
        if number == 3:
            scale = scale * weight
        rows = []
        centre = 0.0
        for axis_number in range(3):
            unit = scale * spacing[axis_number]
            centre = centre - unit * (abs(VELOCITY[axis_number]) + 1.0)
            carried, rising, falling = direction_factors(axis_number)
            one_sided = rising if 0.0 in rising else falling
            two_sided = falling if 0.0 in rising else rising
            rows += [
                unit * carried[0],
                unit * carried[1],
                unit * (one_sided[0] + one_sided[1]),
                unit * two_sided[0],
                unit * two_sided[1],
            ]
        sections.append(jnp.stack([centre] + rows + [weight * jnp.ones_like(scale)]))
    return jnp.stack(sections)


def acoustic(axis_number, factors, rising_next, rising_prev, falling_next, falling_prev):
    one, two_next, two_prev = factors
    if VELOCITY[axis_number] >= 0:
        rising = mul(one, rising_prev)
        falling = add(mul(two_next, falling_next), mul(two_prev, falling_prev))
    else:
        rising = add(mul(two_next, rising_next), mul(two_prev, rising_prev))
        falling = mul(one, falling_next)
    return add(rising, falling), sub(rising, falling)


def section(src, src_lines, src_at, state, state_at, dst, dst_lines, dst_at, count, factors, wrap, scaled):
    def layer(number, carry):
        cache = {}

        def cell(field, parity, line, step=0):
            low, high = src_lines
            key = (field, parity, line, step)
            if key in cache:
                return cache[key]
            if low <= line < high:
                value = src[field, src_at + number + step, parity, line - low]
            elif wrap and line < low:
                value = pltpu.roll(cell(field, parity, high - 1), 1, 0)
            elif wrap:
                value = pltpu.roll(cell(field, parity, low), ROWS - 1, 0)
            else:
                value = None
            cache[key] = value
            return value

        def pair(axis_number, parity, line, step=0):
            key = ("pair", axis_number, parity, line, step)
            if key not in cache:
                pressure = cell(4, parity, line, step)
                speed = cell(1 + axis_number, parity, line, step)
                cache[key] = (None, None) if pressure is None else (pressure + speed, pressure - speed)
            return cache[key]

        centre = factors[0]
        for line in range(*dst_lines):
            for parity in (0, 1):
                result = [None] * 5
                for field in range(5):
                    terms = mul(centre, cell(field, parity, line))
                    if 0 <= line < 4:
                        held = state[field, state_at + number, parity, line]
                        terms = add(mul(factors[16], held) if scaled else held, terms)
                    result[field] = terms
                for axis_number in range(3):
                    forward, backward, *sound = factors[1 + 5 * axis_number : 6 + 5 * axis_number]

                    def neighbours(read):
                        if axis_number == 0:
                            other = read(1 - parity, line, 0)
                            if parity == 0:
                                return other, [turn_lanes(part, 1) for part in other]
                            return [turn_lanes(part, LANES - 1) for part in other], other
                        if axis_number == 1:
                            return read(parity, line + 1, 0), read(parity, line - 1, 0)
                        return read(parity, line, 1), read(parity, line, -1)

                    for field in range(4):
                        if field != 1 + axis_number:
                            (after,), (before,) = neighbours(
                                lambda *where, field=field: [cell(field, *where)]
                            )
                            result[field] = add(result[field], add(mul(forward, after), mul(backward, before)))
                    after, before = neighbours(lambda *where: pair(axis_number, *where))
                    pressure, speed = acoustic(
                        axis_number, sound, after[0], before[0], after[1], before[1]
                    )
                    result[4] = add(result[4], pressure)
                    result[1 + axis_number] = add(result[1 + axis_number], speed)
                for field in range(5):
                    dst[field, dst_at + number, parity, line - dst_lines[0]] = result[field]
        return carry

    lax.fori_loop(0, count, layer, 0)


def gather_slots_kernel(others, at_ref, checkpoint, *rest):
    outs, sems = rest[:others], rest[others]
    copies = []
    for number in range(others):
        for slot in range(HELD_MOST):
            copies.append(
                pltpu.make_async_copy(
                    checkpoint.at[at_ref[number, slot]], outs[number].at[slot], sems.at[number, slot]
                )
            )
    for copy in copies:
        copy.start()
    for copy in copies:
        copy.wait()


def gather_slots(checkpoint, at):
    others = at.shape[0]
    piece = shape(HELD_MOST, *checkpoint.shape[1:])
    return pl.pallas_call(
        functools.partial(gather_slots_kernel, others),
        out_shape=[piece] * others,
        in_specs=[spec_smem(), spec_any()],
        out_specs=[spec_any()] * others,
        scratch_shapes=[pltpu.SemaphoreType.DMA((others, HELD_MOST))],
        compiler_params=params(),
        name="gather_slots",
    )(at, checkpoint)


def store_lines(lines, out, z):
    for line in range(4):
        rows = pl.ds(line * ROWS, ROWS)
        pressure = split_parity(lines[4, 0, rows, :], lines[4, 1, rows, :])
        for field in range(5):
            parts = pressure
            if field < 4:
                parts = split_parity(lines[field, 0, rows, :], lines[field, 1, rows, :])
            if field == 0:
                parts = (parts[0] - pressure[0], parts[1] - pressure[1])
            for parity in (0, 1):
                out[field, z, parity, line] = parts[parity]


def prepare_kernel(checkpoint, live, low, high, lines):
    slots = checkpoint.shape[0]
    for half, out in ((0, low), (1, high)):

        def held(z, carry, half=half, out=out):
            for field in range(5):
                for side in (0, 1):
                    for slot in range(slots):
                        lines[field, side, pl.ds(slot, 4, stride=ROWS), :] = checkpoint[
                            slot, field, half * DEPTH + z, :, pl.ds(side * LANES, LANES)
                        ]
            store_lines(lines, out.at[0], z)
            return carry

        def own(z, carry, half=half, out=out):
            for field in range(5):
                for side in (0, 1):
                    for group in range(4):
                        rows = live[field, half * DEPTH + z, pl.ds(group * ROWS, ROWS), pl.ds(side * LANES, LANES)]
                        for block in (0, 1):
                            lines[field, side, pl.ds(2 * group + block, 4, stride=ROWS), :] = rows[
                                4 * block : 4 * block + 4
                            ]
            store_lines(lines, out.at[1], z)
            return carry

        lax.fori_loop(0, DEPTH, held, 0)
        lax.fori_loop(0, DEPTH, own, 0)


def prepare(checkpoint, live):
    half = shape(2, 5, DEPTH, 2, 4, ROWS, LANES)
    return pl.pallas_call(
        prepare_kernel,
        out_shape=[half, half],
        in_specs=[spec_vmem(), spec_vmem()],
        out_specs=[spec_vmem(), spec_vmem()],
        scratch_shapes=[pltpu.VMEM((5, 2, 4 * ROWS, LANES), jnp.float32)],
        compiler_params=params(),
        name="prepare",
    )(checkpoint, live)


HELD_LINES = ((0, 4), (-1, 5), (-2, 6), (-3, 7), (-4, 8))
LIVE_LINES = ((0, 4),) * 5
CARRIES = ((0, 6), (0, 8), (0, 10), (1, 4), (1, 4), (1, 4))


def copy_all(pairs, sems):
    copies = [pltpu.make_async_copy(src, dst, sems.at[number]) for number, (src, dst) in enumerate(pairs)]
    for copy in copies:
        copy.start()
    for copy in copies:
        copy.wait()


def weigh_and_pack(others, held_out, live_out, rows_ref, mask_ref, tiles_ref, send, keep):
    def layer(z, carry):
        for field in (4, 0, 1, 2, 3):
            for parity in (0, 1):
                total = [live_out[field, z, parity, line] for line in range(4)]
                for other in range(others):
                    for place, first in ((0, 4), (1, 8), (2, 0)):
                        at = rows_ref[other, place]
                        mask = mask_ref[other, place]
                        for line in range(4):
                            image = held_out[field, z, parity, first + line]
                            total[line] = total[line] + mask * pick_rows(image, at)
                for number, out in ((0, send), (1, keep)):
                    at = tiles_ref[number, 0]
                    lower = tiles_ref[number, 1] == 0
                    for line in (0, 1):
                        value = jnp.where(lower, pick_rows(total[line], at), pick_rows(total[2 + line], at))
                        if field == 0:
                            value = value + out[4, z, parity, line]
                        out[field, z, parity, line] = value
        return carry

    lax.fori_loop(0, DEPTH, layer, 0)


def first_half_kernel(
    others, live_factors, held_factors, rows_ref, mask_ref, tiles_ref, before, low, high, *rest
):
    send, keep, *carries = rest[:8]
    held, live, h1, h2, h3, h4, l1, l2, l3, l4, sems = rest[8:]
    pairs = []
    for kind, state in ((0, held), (1, live)):
        for number, part in enumerate((before, low, high)):
            pairs.append((part.at[kind], state.at[:, pl.ds(number * DEPTH, DEPTH)]))
    copy_all(pairs, sems)
    run_sections(held, (h1, h2, h3, h4), HELD_LINES, False, held_factors, False)
    run_sections(live, (l1, l2, l3, l4), LIVE_LINES, True, live_factors, False)
    last = ((h1, 8), (h2, 6), (h3, 4), (l1, 8), (l2, 6), (l3, 4))
    copies = [
        pltpu.make_async_copy(src.at[:, pl.ds(at, 2)], out, sems.at[number])
        for number, ((src, at), out) in enumerate(zip(last, carries))
    ]
    for copy in copies:
        copy.start()
    weigh_and_pack(others, h4, l4, rows_ref, mask_ref, tiles_ref, send, keep)
    for copy in copies:
        copy.wait()


def second_half_kernel(
    others, live_factors, held_factors, rows_ref, mask_ref, tiles_ref, high, after, *rest
):
    carries, (send, keep) = rest[:6], rest[6:8]
    held, live, h1, h2, h3, h4, l1, l2, l3, l4, sems = rest[8:]
    pairs = []
    for kind, state in ((0, held), (1, live)):
        for number, part in enumerate((high, after)):
            pairs.append((part.at[kind], state.at[:, pl.ds(number * DEPTH, DEPTH)]))
    for carry, dst in zip(carries, (h1, h2, h3, l1, l2, l3)):
        pairs.append((carry, dst.at[:, pl.ds(0, 2)]))
    copy_all(pairs, sems)
    run_sections(held, (h1, h2, h3, h4), HELD_LINES, False, held_factors, True)
    run_sections(live, (l1, l2, l3, l4), LIVE_LINES, True, live_factors, True)
    weigh_and_pack(others, h4, l4, rows_ref, mask_ref, tiles_ref, send, keep)


def run_sections(state, stages, lines, wrap, factors, continued):
    for number in range(4):
        if wrap:
            row = [factors[number, i] for i in range(17)]
        else:
            row = [factors[number, i] for i in range(17)]
        src = state if number == 0 else stages[number - 1]
        if continued:
            src_at = 3 if number == 0 else 1
            state_at = 3 - number
            dst_at, count = (0 if number == 3 else 2), DEPTH
        else:
            src_at, state_at, dst_at, count = 1, 1 + number, 0, 3 * DEPTH - 2 * (number + 1)
        section(
            src, lines[number], src_at, state, state_at, stages[number], lines[number + 1], dst_at,
            count, row, wrap, number == 3,
        )


def half_step(kernel, parts, carries_in, tables, others, layers, last):
    live_factors, held_factors, rows, masks, tiles = tables
    packed = shape(5, DEPTH, 2, 2, ROWS, LANES)
    buffer = lambda count, lines: pltpu.VMEM((5, count, 2, lines, ROWS, LANES), jnp.float32)
    carry_shapes = [shape(5, 2, 2, lines, ROWS, LANES) for lines in (6, 8, 10, 4, 4, 4)]
    outs = [packed, packed] + ([] if last else carry_shapes)
    stage_layers = (6, 6, 6, DEPTH) if last else (10, 8, 6, DEPTH)
    return pl.pallas_call(
        functools.partial(kernel, others),
        out_shape=outs,
        in_specs=[spec_smem()] + [spec_vmem()] * 4 + [spec_any()] * (len(parts) + len(carries_in)),
        out_specs=[spec_vmem()] * 2 + [spec_any()] * (len(outs) - 2),
        scratch_shapes=[buffer(layers, 4), buffer(layers, 4)]
        + [buffer(count, lines) for count, lines in zip(stage_layers, (6, 8, 10, 12))]
        + [buffer(count, 4) for count in stage_layers]
        + [pltpu.SemaphoreType.DMA((10,))],
        compiler_params=params(),
        name="second_half" if last else "first_half",
    )(live_factors, held_factors, rows, masks, tiles, *parts, *carries_in)


def share_kernel(groups, at_ref, keep, arrived, *outs):
    def layer(z, carry):
        odd = lax.broadcasted_iota(jnp.int32, (ROWS, LANES), 0) % 2 == 1
        for field in range(5):
            for parity in (0, 1):
                first = keep[field, z, parity, 0] + arrived[field, z, parity, 0]
                second = keep[field, z, parity, 1] + arrived[field, z, parity, 1]
                for number in range(groups):
                    at = at_ref[number]
                    outs[number][field, z, parity] = jnp.where(
                        odd, pick_rows(second, at), pick_rows(first, at)
                    )
        return carry

    lax.fori_loop(0, DEPTH, layer, 0)


def share(keep, arrived, at):
    groups = at.shape[0]
    piece = shape(5, DEPTH, 2, ROWS, LANES)
    return pl.pallas_call(
        functools.partial(share_kernel, groups),
        out_shape=[piece] * groups,
        in_specs=[spec_vmem()] * 3,
        out_specs=[spec_vmem()] * groups,
        compiler_params=params(),
        name="share",
    )(at, keep, arrived)


def collect_kernel(groups, tile_most, swap_ref, mask_ref, *rest):
    pieces, out = rest[: 2 * groups], rest[2 * groups]
    swap = swap_ref[0] == 1
    for half in (0, 1):
        own = pieces[half * groups : (half + 1) * groups]

        def layer(z, carry, half=half, own=own):
            for field in range(5):
                sums = []
                for kind in (0, 1):
                    parts = []
                    for parity in (0, 1):
                        value = own[kind][field, z, parity]
                        for other in range(2 + kind, groups, 2):
                            value = value + own[other][field, z, parity]
                        parts.append(value)
                    sums.append(parts)
                for kind in (0, 1):
                    mask = mask_ref[kind]
                    parts = [
                        mask * jnp.where(swap, sums[1 - kind][parity], sums[kind][parity])
                        for parity in (0, 1)
                    ]
                    sides = join_parity(*parts)
                    for slot in range(tile_most // 2):
                        for side in (0, 1):
                            out[2 * slot + kind, field, half * DEPTH + z, :, pl.ds(side * LANES, LANES)] = sides[
                                side
                            ][2 * slot : 2 * slot + 2]
            return carry

        lax.fori_loop(0, DEPTH, layer, 0)


def collect(pieces, swap, masks, tile_most):
    groups = len(pieces) // 2
    return pl.pallas_call(
        functools.partial(collect_kernel, groups, tile_most),
        out_shape=shape(tile_most, 5, 2 * DEPTH, TILE_LINES, 2 * LANES),
        in_specs=[spec_smem()] + [spec_vmem()] * (1 + len(pieces)),
        out_specs=spec_vmem(),
        compiler_params=params(),
        name="collect",
    )(swap, masks, *pieces)


def place_kernel(others, block_ref, *rest):
    pieces, (low, high, lines) = rest[:others], rest[others:]
    for half, out in ((0, low), (1, high)):

        def layer(z, carry, half=half, out=out):
            for number in range(others):
                for slot in range(HELD_MOST):
                    block = block_ref[number, slot]

                    @pl.when(block >= 0)
                    def _():
                        for field in range(5):
                            for side in (0, 1):
                                lines[field, side, pl.ds(block, 4, stride=ROWS), :] = pieces[number][
                                    slot, field, half * DEPTH + z, :, pl.ds(side * LANES, LANES)
                                ]

            store_lines(lines, out, z)
            return carry

        lax.fori_loop(0, DEPTH, layer, 0)


def place(pieces, blocks):
    half = shape(5, DEPTH, 2, 4, ROWS, LANES)
    return pl.pallas_call(
        functools.partial(place_kernel, len(pieces)),
        out_shape=[half, half],
        in_specs=[spec_smem()] + [spec_vmem()] * len(pieces),
        out_specs=[spec_vmem()] * 2,
        scratch_shapes=[pltpu.VMEM((5, 2, 4 * ROWS, LANES), jnp.float32)],
        compiler_params=params(),
        name="place",
    )(blocks, *pieces)


def recover_kernel(factors, before, low, high, after, out, state, s1, s2, s3, s4, lines, sems):
    copy_all(
        [(part, state.at[:, pl.ds(number * DEPTH, DEPTH)]) for number, part in enumerate((before, low, high, after))],
        sems,
    )
    for number, dst in enumerate((s1, s2, s3, s4)):
        src = state if number == 0 else (s1, s2, s3)[number - 1]
        row = [factors[number, i] for i in range(17)]
        section(src, (0, 4), 1, state, 1 + number, dst, (0, 4), 0, 4 * DEPTH - 2 * (number + 1), row, True, False)

    def layer(z, carry):
        for line in range(4):
            pressure = [s4[4, z, parity, line] for parity in (0, 1)]
            for field in range(5):
                parts = pressure if field == 4 else [s4[field, z, parity, line] for parity in (0, 1)]
                if field == 0:
                    parts = [parts[parity] + pressure[parity] for parity in (0, 1)]
                for side, value in enumerate(join_parity(*parts)):
                    lines[field, side, pl.ds(line, ROWS, stride=4), :] = value
        for field in range(5):
            for side in (0, 1):
                out[field, z, :, pl.ds(side * LANES, LANES)] = lines[field, side]
        return carry

    lax.fori_loop(0, 2 * DEPTH, layer, 0)


def recover(factors, parts):
    buffer = lambda count: pltpu.VMEM((5, count, 2, 4, ROWS, LANES), jnp.float32)
    return pl.pallas_call(
        recover_kernel,
        out_shape=shape(5, 2 * DEPTH, 4 * ROWS, 2 * LANES),
        in_specs=[spec_smem()] + [spec_any()] * 4,
        out_specs=spec_vmem(),
        scratch_shapes=[buffer(count) for count in (16, 14, 12, 10, 8)]
        + [pltpu.VMEM((5, 2, 4 * ROWS, LANES), jnp.float32), pltpu.SemaphoreType.DMA((4,))],
        compiler_params=params(),
        name="recover",
    )(factors, *parts)


def rows_of(table):
    return jnp.broadcast_to(table[..., None], (*table.shape, LANES))


def body(checkpoint, slot_block, live_state, levels, coefficients, tile_owner):
    groups = lax.axis_size("buddy")
    slabs = lax.axis_size("slab")
    myself = lax.axis_index("buddy")
    others = groups - 1
    blocks = checkpoint.shape[0]
    partners = [jnp.bitwise_xor(myself, d) for d in range(groups)]
    distances = jnp.arange(1, groups, dtype=jnp.int32)
    other_grids = jnp.bitwise_xor(myself, distances)
    trade = lambda array, d: lax.ppermute(array, "buddy", [(i, i ^ d) for i in range(groups)])
    upward = lambda array: lax.ppermute(array, "slab", [(i, (i + 1) % slabs) for i in range(slabs)])
    downward = lambda array: lax.ppermute(array, "slab", [((i + 1) % slabs, i) for i in range(slabs)])

    slot_grid, slot_place = slot_block // blocks, slot_block % blocks
    earlier = jnp.tril(jnp.ones((blocks, blocks), jnp.int32), -1)
    same = (slot_grid[:, :, None] == slot_grid[:, None, :]).astype(jnp.int32)
    slot_rank = jnp.sum(same * earlier[None], axis=2)
    held_grid = lax.dynamic_index_in_dim(slot_grid, myself, 0, keepdims=False)
    held_place = lax.dynamic_index_in_dim(slot_place, myself, 0, keepdims=False)
    held_rank = lax.dynamic_index_in_dim(slot_rank, myself, 0, keepdims=False)
    slots = jnp.arange(blocks, dtype=jnp.int32)
    wanted = (held_grid[None, None, :] == other_grids[:, None, None]) & (
        held_rank[None, None, :] == jnp.arange(HELD_MOST, dtype=jnp.int32)[None, :, None]
    )
    send_at = jnp.sum(jnp.where(wanted, slots, 0), axis=2).astype(jnp.int32)
    sent = gather_slots(checkpoint, send_at)
    received = [trade(array, d) for d, array in enumerate(sent, 1)]

    low, high = prepare(checkpoint, live_state[0])
    before = upward(high)
    after = downward(low)

    inverse = jnp.exp2(levels[:, 0, :].astype(jnp.float32))
    facts = lax.all_gather(jnp.concatenate([inverse[0], coefficients[0]]), "buddy", axis=0)
    waves = [abs(drift) + 1.0 for drift in VELOCITY]

    def factors_of(spacing, weight):
        spread = waves[0] * spacing[0] + waves[1] * spacing[1] + waves[2] * spacing[2]
        return factor_table(spacing, COURANT / spread, weight)

    recover_factors = factors_of([inverse[0, a] for a in range(3)], jnp.float32(1.0))
    live_factors = factors_of([inverse[1, a] for a in range(3)], coefficients[1, 0])
    of_slot = (held_grid[:, None] == jnp.arange(groups, dtype=jnp.int32)[None, :])
    slot_facts = jnp.sum(jnp.where(of_slot[:, :, None], facts[None], 0.0), axis=1)
    held_factors = rows_of(factors_of([slot_facts[:, a] for a in range(3)], slot_facts[:, 3]))

    rows, masks = [], []
    for shift in (0, 1, -1):
        place_wanted = (slots - shift) % blocks
        hit = (held_grid[None, None, :] == other_grids[:, None, None]) & (
            held_place[None, None, :] == place_wanted[None, :, None]
        )
        rows.append(jnp.sum(jnp.where(hit, slots, 0), axis=2).astype(jnp.int32))
        masks.append(jnp.sum(hit.astype(jnp.float32), axis=2))
    rows = rows_of(jnp.stack(rows, 1))
    masks = rows_of(jnp.stack(masks, 1))

    own_tiles = tile_owner[0]
    tile_count = own_tiles.shape[0]
    tile_most = 2 * tile_count // groups
    numbers = jnp.arange(tile_count, dtype=jnp.int32)
    ahead = (own_tiles[None, :] < own_tiles[:, None]) | (
        (own_tiles[None, :] == own_tiles[:, None]) & (numbers[None, :] < numbers[:, None])
    )
    position = jnp.sum(ahead.astype(jnp.int32), axis=1)
    readers = jnp.arange(groups, dtype=jnp.int32)
    start = jnp.sum((own_tiles[None, :] < readers[:, None]).astype(jnp.int32), axis=1)
    amount = jnp.sum((own_tiles[None, :] == readers[:, None]).astype(jnp.int32), axis=1)
    kind = myself % 2
    order = jnp.stack([2 * slots + 1 - kind, 2 * slots + kind])
    listed = jnp.sum(jnp.where(position[None, None, :] == order[:, :, None], numbers, 0), axis=2)
    tiles = rows_of(jnp.stack([listed // 2, listed % 2], 1).astype(jnp.int32))
    first_slot = (start + 1 - kind) // 2
    partner_first = jnp.sum(
        jnp.where(jnp.stack(partners)[:, None] == readers[None, :], first_slot[None, :], 0), axis=1
    )
    share_at = rows_of(jnp.minimum(partner_first[:, None] + slots[None, :] // 2, ROWS - 1))
    my_start = jnp.sum(jnp.where(readers == myself, start, 0))
    my_amount = jnp.sum(jnp.where(readers == myself, amount, 0))
    swap = ((my_start % 2) != kind).astype(jnp.int32).reshape(1)
    tile_ranks = 2 * (slots[None, :] // 2) + jnp.arange(2, dtype=jnp.int32)[:, None]
    tile_masks = rows_of((tile_ranks < my_amount).astype(jnp.float32))

    tables = (live_factors, held_factors, rows, masks, tiles)
    send_low, keep_low, *carries = half_step(
        first_half_kernel, (before, low, high), (), tables, others, 3 * DEPTH, False
    )
    arrived_low = trade(send_low, 1)
    send_high, keep_high = half_step(
        second_half_kernel, (high, after), carries, tables, others, 2 * DEPTH, True
    )
    arrived_high = trade(send_high, 1)

    shares_low = share(keep_low, arrived_low, share_at)
    pieces_low = [shares_low[0]] + [trade(shares_low[d], d) for d in range(1, groups)]
    shares_high = share(keep_high, arrived_high, share_at)
    pieces_high = [shares_high[0]] + [trade(shares_high[d], d) for d in range(1, groups)]

    received_blocks = []
    for d in range(1, groups):
        holder_grid = lax.dynamic_index_in_dim(slot_grid, partners[d], 0, keepdims=False)
        holder_place = lax.dynamic_index_in_dim(slot_place, partners[d], 0, keepdims=False)
        holder_rank = lax.dynamic_index_in_dim(slot_rank, partners[d], 0, keepdims=False)
        hit = (holder_grid[None, :] == myself) & (
            holder_rank[None, :] == jnp.arange(HELD_MOST, dtype=jnp.int32)[:, None]
        )
        received_blocks.append(jnp.sum(jnp.where(hit, holder_place[None, :] + 1, 0), axis=1) - 1)
    restored_low, restored_high = place(received, jnp.stack(received_blocks).astype(jnp.int32))
    restored_before = upward(restored_high)
    restored_after = downward(restored_low)
    recovered = recover(recover_factors, (restored_before, restored_low, restored_high, restored_after))
    combined = collect(pieces_low + pieces_high, swap, tile_masks, tile_most)
    return recovered[None], combined


def solution(mesh):
    return jax.shard_map(
        body,
        mesh=mesh,
        in_specs=(
            P("buddy", None, "slab", None, None),
            P(),
            P("buddy", None, "slab", None, None),
            P(None, "buddy", None),
            P(None, "buddy"),
            P("slab", None),
        ),
        out_specs=(P("buddy", None, "slab", None, None), P("buddy", None, "slab", None, None)),
        check_vma=False,
    )
```

profile of v0, /device:TPU:0, one launch (start us, length us, event | category | flops | bytes accessed | tf_op | source)
XLA Modules:
  0.0 167.6 jit_solution(11613099004984445721)
XLA Ops:
  0.6 1.3 copy-done
  1.9 1.3 copy-done.4
  3.3 5.3 %prepare.1 = (f32[2,5,4,2,4,8,128]{6,5,4,3,2,1,0:T(8,128)}, f32[2,5,4,2,4,8,128]{6,5,4,3,2,1,0:T(8,128)S(1)}) custom-call(f32[8,5,8,4,256]{4,3,2,1,0:T(4,128)S(1)} %copy-done, f32[5,8,32,256]{3,2,1,0:T(8,128)S(1)} %bitcast.243), custom_call_target="tpu_custom_call" | custom-call | tf_op jit(solution)/shard_map/prepare/pallas_call | solution.py:285
  8.6 0.5 collective-permute-start.5
  9.1 2.9 %collective-permute-start.10 = (f32[2,5,4,2,4,8,128]{6,5,4,3,2,1,0:T(8,128)}, f32[2,5,4,2,4,8,128]{6,5,4,3,2,1,0:T(8,128)}, u32[]{:S(2)}, u32[]{:S(2)}) collective-permute-start(f32[2,5,4,2,4,8,128]{6,5,4,3,2,1,0:T(8,128)} %get-tuple-element.33.low), channel_id=1, source_target_pairs={{4,0},{8,4},{12,8},{16,12},{20,16},{24,20},{28,24},{0,28},{5,1},{9... | collective-permute-start | bytes 3932168 | tf_op jit(solution)/shard_map/ppermute | solution.py:583
  12.2 0.2 select_reduce_fusion
  12.5 0.2 select_reduce_fusion.3.at_ref
  12.6 1.7 %gather_slots.1 = (f32[3,5,8,4,256]{4,3,2,1,0:T(4,128)}, f32[3,5,8,4,256]{4,3,2,1,0:T(4,128)}, f32[3,5,8,4,256]{4,3,2,1,0:T(4,128)}) custom-call(s32[3,3]{1,0:T(4,128)S(1)} %select_reduce_fusion.3.at_ref, f32[8,5,8,4,256]{4,3,2,1,0:T(4,128)S(1)} %copy-done.1), custom_call_target="tpu_custom_call" | custom-call | tf_op jit(solution)/shard_map/gather_slots/pallas_call | solution.py:228
  14.4 2.3 %collective-permute-start = (f32[3,5,8,4,256]{4,3,2,1,0:T(4,128)}, f32[3,5,8,4,256]{4,3,2,1,0:T(4,128)S(1)}, u32[]{:S(2)}, u32[]{:S(2)}) collective-permute-start(f32[3,5,8,4,256]{4,3,2,1,0:T(4,128)} %get-tuple-element.27), channel_id=1, source_target_pairs={{0,1},{1,0},{2,3},{3,2},{4,5},{5,4},{6,7},{7,6},{8,9},{9,8},{10,11... | collective-permute-start | bytes 1474568 | tf_op jit(solution)/shard_map/ppermute | solution.py:581
  16.7 2.6 %collective-permute-start.1 = (f32[3,5,8,4,256]{4,3,2,1,0:T(4,128)}, f32[3,5,8,4,256]{4,3,2,1,0:T(4,128)S(1)}, u32[]{:S(2)}, u32[]{:S(2)}) collective-permute-start(f32[3,5,8,4,256]{4,3,2,1,0:T(4,128)} %get-tuple-element.28), channel_id=1, source_target_pairs={{0,2},{1,3},{2,0},{3,1},{4,6},{5,7},{6,4},{7,5},{8,10},{9,11},{10,... | collective-permute-start | bytes 1474568 | tf_op jit(solution)/shard_map/ppermute | solution.py:581
  19.4 0.6 fusion.36
  20.0 0.7 dynamic-slice
  21.4 0.7 maximum_dynamic-update-slice_fusion
  22.1 31.7 %all-reduce = f32[16]{0:T(128)S(1)} all-reduce(f32[16]{0:T(128)S(1)} %maximum_dynamic-update-slice_fusion), channel_id=2, replica_groups=mesh['slab'=8,'buddy'=4] {'buddy'}, use_global_device_ids=true, to_apply=%add | all-reduce | flops 16 | bytes 128
  54.1 0.3 fusion
  54.5 0.2 convert_reduce_fusion
  54.7 0.1 convert_reduce_fusion.1
  54.9 0.2 select_reduce_fusion.1
  55.2 0.1 select_reduce_fusion.5
  60.2 0.7 fusion.35
  60.9 0.7 and_select_fusion.8
  61.6 0.8 copy-done.5
  62.4 0.8 copy-done.7
  63.2 1.0 copy-done.6
  64.2 1.0 copy-done.8
  65.2 3.2 %place.1 = (f32[5,4,2,4,8,128]{5,4,3,2,1,0:T(8,128)S(1)}, f32[5,4,2,4,8,128]{5,4,3,2,1,0:T(8,128)S(1)}) custom-call(s32[3,3]{1,0:T(4,128)S(1)} %pad_add_fusion.1.block_ref, f32[3,5,8,4,256]{4,3,2,1,0:T(4,128)S(1)} %collective-permute-done.rest_0_, f32[3,5,8,4,256]{4,3,2,1,0:T(4,128)S(1)} %copy-done.6, f32[3,5,8,4,256]{4,3,2,1,0:T(4,128)S(1)} %copy-done.8), custom_call_target="tpu_custom_call" | custom-call | tf_op jit(solution)/shard_map/place/pallas_call | solution.py:516
  68.6 2.6 %collective-permute-start.4 = (f32[5,4,2,4,8,128]{5,4,3,2,1,0:T(8,128)S(1)}, f32[5,4,2,4,8,128]{5,4,3,2,1,0:T(8,128)}, u32[]{:S(2)}, u32[]{:S(2)}) collective-permute-start(f32[5,4,2,4,8,128]{5,4,3,2,1,0:T(8,128)S(1)} %get-tuple-element.31.low), channel_id=1, source_target_pairs={{4,0},{8,4},{12,8},{16,12},{20,16},{24,20},{28,24},{0,28},{5,1},{9... | collective-permute-start | bytes 1966088 | tf_op jit(solution)/shard_map/ppermute | solution.py:583
  81.7 0.7 stack.661
  82.4 0.7 stack.631
  83.1 0.7 stack.646
  83.8 0.7 stack.616
  84.6 0.1 broadcast_in_dim.213.held_factors
  84.9 11.6 %first_half.1 = (f32[5,4,2,2,8,128]{5,4,3,2,1,0:T(8,128)S(1)}, f32[5,4,2,2,8,128]{5,4,3,2,1,0:T(8,128)S(1)}, f32[5,2,2,6,8,128]{5,4,3,2,1,0:T(8,128)S(1)}, f32[5...) custom-call(f32[4,17]{1,0:T(4,128)S(1)} %pad_maximum_fusion.3.live_f, ...), custom_call_target="tpu_custom_call" | custom-call | tf_op jit(solution)/shard_map/first_half/pallas_call | solution.py:401
  96.5 7.4 %second_half.1 = (f32[5,4,2,2,8,128]{5,4,3,2,1,0:T(8,128)S(1)}, f32[5,4,2,2,8,128]{5,4,3,2,1,0:T(8,128)S(1)}) custom-call(f32[4,17]{1,0:T(4,128)S(1)} %pad_maximum_fusion.3.live_factors, f32[4,17,8,128]{3,2,1,0:T(8,128)S(1)} %broadcast_in_dim.213.held_factors, s32[3,3,8,128]{3,2,1,0:T(8,128)S(1)} %broadcast_in_dim.218.rows_ref, ...), custom_call_target="tpu_custom_call" | custom-call | tf_op jit(solution)/shard_map/second_half/pallas_call | solution.py:401
  104.0 9.7 %collective-permute-start.11 = (f32[5,4,2,2,8,128]{5,4,3,2,1,0:T(8,128)S(1)}, f32[5,4,2,2,8,128]{5,4,3,2,1,0:T(8,128)S(1)}, u32[]{:S(2)}, u32[]{:S(2)}) collective-permute-start(f32[5,4,2,2,8,128]{5,4,3,2,1,0:T(8,128)S(1)} %get-tuple-element.47), channel_id=1, source_target_pairs={{0,1},{1,0},{2,3},{3,2},{4,5},{5,4},{6,7},{7,6},{8,9},{9,8},{10,11... | collective-permute-start | bytes 983048 | tf_op jit(solution)/shard_map/ppermute | solution.py:581
  113.7 0.2 select_reduce_fusion.4
  114.0 8.3 %collective-permute-done.11.arrived = f32[5,4,2,2,8,128]{5,4,3,2,1,0:T(8,128)S(1)} collective-permute-done((f32[5,4,2,2,8,128]{5,4,3,2,1,0:T(8,128)S(1)}, f32[5,4,2,2,8,128]{5,4,3,2,1,0:T(8,128)S(1)}, u32[]{:S(2)}, u32[]{:S(2)}) %collective-permute-start.11) | collective-permute-done | bytes 327712 | tf_op jit(solution)/shard_map/ppermute | solution.py:581
  122.4 0.8 share.3
  123.2 2.0 %collective-permute-start.12 = (f32[5,4,2,8,128]{4,3,2,1,0:T(8,128)S(1)}, f32[5,4,2,8,128]{4,3,2,1,0:T(8,128)S(1)}, u32[]{:S(2)}, u32[]{:S(2)}) collective-permute-start(f32[5,4,2,8,128]{4,3,2,1,0:T(8,128)S(1)} %get-tuple-element.49), channel_id=1, source_target_pairs={{0,1},{1,0},{2,3},{3,2},{4,5},{5,4},{6,7},{7,6},{8,9},{9,8},{10,11... | collective-permute-start | bytes 491528 | tf_op jit(solution)/shard_map/ppermute | solution.py:581
  125.2 3.2 %collective-permute-start.13 = (f32[5,4,2,8,128]{4,3,2,1,0:T(8,128)}, f32[5,4,2,8,128]{4,3,2,1,0:T(8,128)S(1)}, u32[]{:S(2)}, u32[]{:S(2)}) collective-permute-start(f32[5,4,2,8,128]{4,3,2,1,0:T(8,128)} %get-tuple-element.50), channel_id=1, source_target_pairs={{0,2},{1,3},{2,0},{3,1},{4,6},{5,7},{6,4},{7,5},{8,10},{9,11},{10,... | collective-permute-start | bytes 491528 | tf_op jit(solution)/shard_map/ppermute | solution.py:581
  128.4 3.7 %collective-permute-done.6.arrived = f32[5,4,2,2,8,128]{5,4,3,2,1,0:T(8,128)S(1)} collective-permute-done((f32[5,4,2,2,8,128]{5,4,3,2,1,0:T(8,128)S(1)}, f32[5,4,2,2,8,128]{5,4,3,2,1,0:T(8,128)S(1)}, u32[]{:S(2)}, u32[]{:S(2)}) %collective-permute-start.6) | collective-permute-done | bytes 327712 | tf_op jit(solution)/shard_map/ppermute | solution.py:581
  132.1 5.2 %collective-permute-start.14 = (f32[5,4,2,8,128]{4,3,2,1,0:T(8,128)S(1)}, f32[5,4,2,8,128]{4,3,2,1,0:T(8,128)S(1)}, u32[]{:S(2)}, u32[]{:S(2)}) collective-permute-start(f32[5,4,2,8,128]{4,3,2,1,0:T(8,128)S(1)} %get-tuple-element.51), channel_id=1, source_target_pairs={{0,3},{1,2},{2,1},{3,0},{4,7},{5,6},{6,5},{7,4},{8,11},{9,10},{10,... | collective-permute-start | bytes 491528 | tf_op jit(solution)/shard_map/ppermute | solution.py:581
  137.4 0.9 share.2
  138.3 0.6 collective-permute-start.8
  138.8 3.8 %collective-permute-start.9 = (f32[5,4,2,8,128]{4,3,2,1,0:T(8,128)}, f32[5,4,2,8,128]{4,3,2,1,0:T(8,128)S(1)}, u32[]{:S(2)}, u32[]{:S(2)}) collective-permute-start(f32[5,4,2,8,128]{4,3,2,1,0:T(8,128)} %get-tuple-element.39), channel_id=1, source_target_pairs={{0,3},{1,2},{2,1},{3,0},{4,7},{5,6},{6,5},{7,4},{8,11},{9,10},{10,... | collective-permute-start | bytes 491528 | tf_op jit(solution)/shard_map/ppermute | solution.py:581
  142.6 0.6 compare_convert_fusion
  155.0 10.3 %recover.1 = f32[5,8,32,256]{3,2,1,0:T(8,128)} custom-call(f32[4,17]{1,0:T(4,128)S(1)} %pad_maximum_fusion.2.factors, f32[5,4,2,4,8,128]{5,4,3,2,1,0:T(8,128)S(1)} %collective-permute-done.3.before, f32[5,4,2,4,8,128]{5,4,3,2,1,0:T(8,128)S(1)} %get-tuple-element.31.low, f32[5,4,2,4,8,128]{5,4,3,2,1,0:T(8,128)S(1)} %get-tuple-element.30.high, ...), custom_call_target="tpu_custom_call" | custom-call | tf_op jit(solution)/shard_map/recover/pallas_call | solution.py:556
  165.4 2.1 %collect.1 = f32[8,5,8,2,256]{4,3,2,1,0:T(2,128)} custom-call(s32[1]{0:T(128)} %bitcast.76.swap_ref, f32[2,8,128]{2,1,0:T(8,128)S(1)} %broadcast_in_dim.206.mask_ref, f32[5,4,2,8,128]{4,3,2,1,0:T(8,128)S(1)} %get-tuple-element.36.rest_0_, f32[5,4,2,8,128]{4,3,2,1,0:T(8,128)S(1)} %collective-permute-done.7.rest_1_, ...), custom_call_target="tpu_custom_call" | custom-call | tf_op jit(solution)/shard_map/collect/pallas_call | solution.py:481
  (150 shorter events, 6.7 us)
Async XLA Ops:
  0.6 1.3 copy-start
  1.9 1.3 copy-start.4
  3.3 8.8 %copy-start.9 = (s32[4,8]{1,0:T(4,128)S(1)}, s32[4,8]{1,0:T(4,128)}, u32[]{:S(2)}) copy-start(s32[4,8]{1,0:T(4,128)} %param.7) | copy-start | bytes 388
  3.3 9.4 %copy-start.1 = (f32[8,5,8,4,256]{4,3,2,1,0:T(4,128)S(1)}, f32[8,5,8,4,256]{4,3,2,1,0:T(4,128)}, u32[]{:S(2)}) copy-start(f32[8,5,8,4,256]{4,3,2,1,0:T(4,128)} %checkpoint.3) | copy-start | bytes 3932164
  8.6 59.9 %copy-start.2 = (f32[2,5,4,2,4,8,128]{6,5,4,3,2,1,0:T(8,128)}, f32[2,5,4,2,4,8,128]{6,5,4,3,2,1,0:T(8,128)S(1)}, u32[]{:S(2)}) copy-start(f32[2,5,4,2,4,8,128]{6,5,4,3,2,1,0:T(8,128)S(1)} %get-tuple-element.32.high) | copy-start | bytes 3932164
  8.6 10.8 %copy-start.11 = (s32[2,1,3]{2,1,0:T(1,128)S(1)}, s32[2,1,3]{2,1,0:T(1,128)}, u32[]{:S(2)}) copy-start(s32[2,1,3]{2,1,0:T(1,128)} %param.9) | copy-start | bytes 76
  8.6 10.8 %copy-start.10 = (f32[2,1]{0,1:T(1,128)S(1)}, f32[2,1]{0,1:T(1,128)}, u32[]{:S(2)}) copy-start(f32[2,1]{0,1:T(1,128)} %param.10) | copy-start | bytes 28
  8.6 11.4 %copy-start.13 = (u32[32]{0:T(128)S(1)}, u32[32]{0:T(128)}, u32[]{:S(2)}) copy-start(u32[32]{0:T(128)} %constant.229) | copy-start | bytes 388
  8.6 45.9 %copy-start.12 = (s32[1,16]{1,0:T(1,128)S(1)}, s32[1,16]{1,0:T(1,128)}, u32[]{:S(2)}) copy-start(s32[1,16]{1,0:T(1,128)} %param.11) | copy-start | bytes 196
  8.6 76.0 %collective-permute-start.5 = (f32[2,5,4,2,4,8,128]{6,5,4,3,2,1,0:T(8,128)S(1)}, f32[2,5,4,2,4,8,128]{6,5,4,3,2,1,0:T(8,128)}, u32[]{:S(2)}, u32[]{:S(2)}) collective-permute-start(f32[2,5,4,2,4,8,128]{6,5,4,3,2,1,0:T(8,128)S(1)} %get-tuple-element.32.high), channel_id=1, source_target_pairs={{0,4},{4,8},{8,12},{12,16},{16,20},{20,24},{24,28},{28,0},{1,5},{5... | collective-permute-start | bytes 3932168 | tf_op jit(solution)/shard_map/ppermute | solution.py:582
  9.1 87.4 %collective-permute-start.10 = (f32[2,5,4,2,4,8,128]{6,5,4,3,2,1,0:T(8,128)}, f32[2,5,4,2,4,8,128]{6,5,4,3,2,1,0:T(8,128)}, u32[]{:S(2)}, u32[]{:S(2)}) collective-permute-start(f32[2,5,4,2,4,8,128]{6,5,4,3,2,1,0:T(8,128)} %get-tuple-element.33.low), channel_id=1, source_target_pairs={{4,0},{8,4},{12,8},{16,12},{20,16},{24,20},{28,24},{0,28},{5,1},{9... | collective-permute-start | bytes 3932168 | tf_op jit(solution)/shard_map/ppermute | solution.py:583
  14.4 47.2 %collective-permute-start = (f32[3,5,8,4,256]{4,3,2,1,0:T(4,128)}, f32[3,5,8,4,256]{4,3,2,1,0:T(4,128)S(1)}, u32[]{:S(2)}, u32[]{:S(2)}) collective-permute-start(f32[3,5,8,4,256]{4,3,2,1,0:T(4,128)} %get-tuple-element.27), channel_id=1, source_target_pairs={{0,1},{1,0},{2,3},{3,2},{4,5},{5,4},{6,7},{7,6},{8,9},{9,8},{10,11... | collective-permute-start | bytes 1474568 | tf_op jit(solution)/shard_map/ppermute | solution.py:581
  16.7 44.9 %collective-permute-start.1 = (f32[3,5,8,4,256]{4,3,2,1,0:T(4,128)}, f32[3,5,8,4,256]{4,3,2,1,0:T(4,128)S(1)}, u32[]{:S(2)}, u32[]{:S(2)}) collective-permute-start(f32[3,5,8,4,256]{4,3,2,1,0:T(4,128)} %get-tuple-element.28), channel_id=1, source_target_pairs={{0,2},{1,3},{2,0},{3,1},{4,6},{5,7},{6,4},{7,5},{8,10},{9,11},{10,... | collective-permute-start | bytes 1474568 | tf_op jit(solution)/shard_map/ppermute | solution.py:581
  19.3 43.1 %collective-permute-start.2 = (f32[3,5,8,4,256]{4,3,2,1,0:T(4,128)}, f32[3,5,8,4,256]{4,3,2,1,0:T(4,128)S(1)}, u32[]{:S(2)}, u32[]{:S(2)}) collective-permute-start(f32[3,5,8,4,256]{4,3,2,1,0:T(4,128)} %get-tuple-element.29), channel_id=1, source_target_pairs={{0,3},{1,2},{2,1},{3,0},{4,7},{5,6},{6,5},{7,4},{8,11},{9,10},{10,... | collective-permute-start | bytes 1474568 | tf_op jit(solution)/shard_map/ppermute | solution.py:581
  61.6 0.8 copy-start.5
  62.4 0.8 copy-start.7
  63.2 1.0 copy-start.6
  64.2 1.0 copy-start.8
  68.5 69.8 %collective-permute-start.3 = (f32[5,4,2,4,8,128]{5,4,3,2,1,0:T(8,128)S(1)}, f32[5,4,2,4,8,128]{5,4,3,2,1,0:T(8,128)S(1)}, u32[]{:S(2)}, u32[]{:S(2)}) collective-permute-start(f32[5,4,2,4,8,128]{5,4,3,2,1,0:T(8,128)S(1)} %get-tuple-element.30.high), channel_id=1, source_target_pairs={{0,4},{4,8},{8,12},{12,16},{16,20},{20,24},{24,28},{28,0},{1,5},{5... | collective-permute-start | bytes 1966088 | tf_op jit(solution)/shard_map/ppermute | solution.py:582
  68.6 69.7 %collective-permute-start.4 = (f32[5,4,2,4,8,128]{5,4,3,2,1,0:T(8,128)S(1)}, f32[5,4,2,4,8,128]{5,4,3,2,1,0:T(8,128)}, u32[]{:S(2)}, u32[]{:S(2)}) collective-permute-start(f32[5,4,2,4,8,128]{5,4,3,2,1,0:T(8,128)S(1)} %get-tuple-element.31.low), channel_id=1, source_target_pairs={{4,0},{8,4},{12,8},{16,12},{20,16},{24,20},{28,24},{0,28},{5,1},{9... | collective-permute-start | bytes 1966088 | tf_op jit(solution)/shard_map/ppermute | solution.py:583
  84.9 11.6 %copy-start.3 = (f32[2,5,4,2,4,8,128]{6,5,4,3,2,1,0:T(8,128)S(1)}, f32[2,5,4,2,4,8,128]{6,5,4,3,2,1,0:T(8,128)}, u32[]{:S(2)}) copy-start(f32[2,5,4,2,4,8,128]{6,5,4,3,2,1,0:T(8,128)} %copy-done.2) | copy-start | bytes 3932164
  104.0 18.3 %collective-permute-start.11 = (f32[5,4,2,2,8,128]{5,4,3,2,1,0:T(8,128)S(1)}, f32[5,4,2,2,8,128]{5,4,3,2,1,0:T(8,128)S(1)}, u32[]{:S(2)}, u32[]{:S(2)}) collective-permute-start(f32[5,4,2,2,8,128]{5,4,3,2,1,0:T(8,128)S(1)} %get-tuple-element.47), channel_id=1, source_target_pairs={{0,1},{1,0},{2,3},{3,2},{4,5},{5,4},{6,7},{7,6},{8,9},{9,8},{10,11... | collective-permute-start | bytes 983048 | tf_op jit(solution)/shard_map/ppermute | solution.py:581
  113.9 18.3 %collective-permute-start.6 = (f32[5,4,2,2,8,128]{5,4,3,2,1,0:T(8,128)S(1)}, f32[5,4,2,2,8,128]{5,4,3,2,1,0:T(8,128)S(1)}, u32[]{:S(2)}, u32[]{:S(2)}) collective-permute-start(f32[5,4,2,2,8,128]{5,4,3,2,1,0:T(8,128)S(1)} %get-tuple-element.35), channel_id=1, source_target_pairs={{0,1},{1,0},{2,3},{3,2},{4,5},{5,4},{6,7},{7,6},{8,9},{9,8},{10,11... | collective-permute-start | bytes 983048 | tf_op jit(solution)/shard_map/ppermute | solution.py:581
  123.2 15.7 %collective-permute-start.12 = (f32[5,4,2,8,128]{4,3,2,1,0:T(8,128)S(1)}, f32[5,4,2,8,128]{4,3,2,1,0:T(8,128)S(1)}, u32[]{:S(2)}, u32[]{:S(2)}) collective-permute-start(f32[5,4,2,8,128]{4,3,2,1,0:T(8,128)S(1)} %get-tuple-element.49), channel_id=1, source_target_pairs={{0,1},{1,0},{2,3},{3,2},{4,5},{5,4},{6,7},{7,6},{8,9},{9,8},{10,11... | collective-permute-start | bytes 491528 | tf_op jit(solution)/shard_map/ppermute | solution.py:581
  125.2 40.1 %collective-permute-start.13 = (f32[5,4,2,8,128]{4,3,2,1,0:T(8,128)}, f32[5,4,2,8,128]{4,3,2,1,0:T(8,128)S(1)}, u32[]{:S(2)}, u32[]{:S(2)}) collective-permute-start(f32[5,4,2,8,128]{4,3,2,1,0:T(8,128)} %get-tuple-element.50), channel_id=1, source_target_pairs={{0,2},{1,3},{2,0},{3,1},{4,6},{5,7},{6,4},{7,5},{8,10},{9,11},{10,... | collective-permute-start | bytes 491528 | tf_op jit(solution)/shard_map/ppermute | solution.py:581
  132.1 33.2 %collective-permute-start.14 = (f32[5,4,2,8,128]{4,3,2,1,0:T(8,128)S(1)}, f32[5,4,2,8,128]{4,3,2,1,0:T(8,128)S(1)}, u32[]{:S(2)}, u32[]{:S(2)}) collective-permute-start(f32[5,4,2,8,128]{4,3,2,1,0:T(8,128)S(1)} %get-tuple-element.51), channel_id=1, source_target_pairs={{0,3},{1,2},{2,1},{3,0},{4,7},{5,6},{6,5},{7,4},{8,11},{9,10},{10,... | collective-permute-start | bytes 491528 | tf_op jit(solution)/shard_map/ppermute | solution.py:581
  138.3 27.1 %collective-permute-start.7 = (f32[5,4,2,8,128]{4,3,2,1,0:T(8,128)}, f32[5,4,2,8,128]{4,3,2,1,0:T(8,128)S(1)}, u32[]{:S(2)}, u32[]{:S(2)}) collective-permute-start(f32[5,4,2,8,128]{4,3,2,1,0:T(8,128)} %get-tuple-element.37), channel_id=1, source_target_pairs={{0,1},{1,0},{2,3},{3,2},{4,5},{5,4},{6,7},{7,6},{8,9},{9,8},{10,11... | collective-permute-start | bytes 491528 | tf_op jit(solution)/shard_map/ppermute | solution.py:581
  138.3 27.1 %collective-permute-start.8 = (f32[5,4,2,8,128]{4,3,2,1,0:T(8,128)}, f32[5,4,2,8,128]{4,3,2,1,0:T(8,128)S(1)}, u32[]{:S(2)}, u32[]{:S(2)}) collective-permute-start(f32[5,4,2,8,128]{4,3,2,1,0:T(8,128)} %get-tuple-element.38), channel_id=1, source_target_pairs={{0,2},{1,3},{2,0},{3,1},{4,6},{5,7},{6,4},{7,5},{8,10},{9,11},{10,... | collective-permute-start | bytes 491528 | tf_op jit(solution)/shard_map/ppermute | solution.py:581
  138.8 26.5 %collective-permute-start.9 = (f32[5,4,2,8,128]{4,3,2,1,0:T(8,128)}, f32[5,4,2,8,128]{4,3,2,1,0:T(8,128)S(1)}, u32[]{:S(2)}, u32[]{:S(2)}) collective-permute-start(f32[5,4,2,8,128]{4,3,2,1,0:T(8,128)} %get-tuple-element.39), channel_id=1, source_target_pairs={{0,3},{1,2},{2,1},{3,0},{4,7},{5,6},{6,5},{7,4},{8,11},{9,10},{10,... | collective-permute-start | bytes 491528 | tf_op jit(solution)/shard_map/ppermute | solution.py:581
where the time goes:
time: 168 us
  Pallas kernels  43.3 us (26%)
  starting transfers between devices  35.7 us (21%)
  blocking collectives  31.7 us (19%)
  between operations  23.4 us (14%)
  local copies, waits for them, and re-layouts  16.8 us (10%)
  waiting for transfers between devices  12 us (7%)
  other arithmetic  4.43 us (3%)
    unnamed x1, blocking collectives  31.7 us
    ppermute x11, starting transfers between devices, body(): lax.ppermute(array, 'buddy', [(i, i ^ d) for i in range(groups)])  29.6 us
    pallas_call x2, Pallas kernels, half_step(): pl.pallas_call(functools.partial(kernel, others), out_shape=outs, in_spec...  19 us
    ppermute x11, waiting for transfers between devices, body(): lax.ppermute(array, 'buddy', [(i, i ^ d) for i in range(groups)])  12 us
    pallas_call x1, Pallas kernels, recover(): pl.pallas_call(recover_kernel, out_shape=shape(5, 2 * DEPTH, 4 * ROWS, 2...  10.3 us
    unnamed x30, local copies, waits for them, and re-layouts  6.94 us
    ppermute x2, starting transfers between devices, body(): lax.ppermute(array, 'slab', [((i + 1) % slabs, i) for i in range(slabs)])  5.58 us
    pallas_call x1, Pallas kernels, prepare(): pl.pallas_call(prepare_kernel, out_shape=[half, half], in_specs=[spec_vme...  5.31 us
  transfers between devices with their start and end apart: 15, of which 2 were waited for; matrix products, arithmetic and copies ran while one was open for 9% of the time, Pallas kernels for 21%

commit v1 on v0

v1 whole, which is shorter than its diff:
```python
import functools

import jax
import jax.numpy as jnp
from jax import lax
from jax.experimental import pallas as pl
from jax.experimental.pallas import tpu as pltpu
from jax.sharding import PartitionSpec as P

VELOCITY = (0.3, -0.2, 0.45)
COURANT = 1.0
TILE_LINES = 2
HELD_MOST = 3
DEPTH = 4
LANES = 128
ROWS = 8
VMEM_BYTES = 32 * 1024 * 1024


def spec_vmem():
    return pl.BlockSpec(memory_space=pltpu.VMEM)


def spec_smem():
    return pl.BlockSpec(memory_space=pltpu.SMEM)


def spec_any():
    return pl.BlockSpec(memory_space=pl.ANY)


def spec_hbm():
    return pl.BlockSpec(memory_space=pltpu.HBM)


def params():
    return pltpu.CompilerParams(vmem_limit_bytes=VMEM_BYTES)


def cost(microseconds, flops=0):
    return pl.CostEstimate(flops=flops, bytes_accessed=microseconds, transcendentals=0)


def shape(*dims):
    return jax.ShapeDtypeStruct(dims, jnp.float32)


def add(*terms):
    total = None
    for term in terms:
        if term is not None:
            total = term if total is None else total + term
    return total


def sub(left, right):
    if right is None:
        return left
    return -right if left is None else left - right


def mul(factor, term):
    return None if term is None else factor * term


def lane_index():
    return lax.broadcasted_iota(jnp.int32, (ROWS, LANES), 1)


def turn_lanes(value, amount):
    return None if value is None else pltpu.roll(value, amount, 1)


def one_hot(out, join):
    row = lax.broadcasted_iota(jnp.int32, (LANES, 2 * LANES), 0)
    column = lax.broadcasted_iota(jnp.int32, (LANES, 2 * LANES), 1)
    for part in (0, 1):
        if join:
            target = 2 * row + part
        else:
            cell = row + part * LANES
            target = cell // 2 + LANES * (cell % 2)
        out[part] = (column == target).astype(jnp.float32).astype(jnp.bfloat16)


def move_lanes(rows, matrix):
    top = rows.astype(jnp.bfloat16)
    rest = rows - top.astype(jnp.float32)
    middle = rest.astype(jnp.bfloat16)
    low = (rest - middle.astype(jnp.float32)).astype(jnp.bfloat16)
    product = lambda part: jnp.dot(part, matrix, preferred_element_type=jnp.float32)
    return (product(top) + product(middle)) + product(low)


def one_hot_scratch():
    return pltpu.VMEM((2, LANES, 2 * LANES), jnp.bfloat16)


def pick_rows(array, at):
    return jnp.take_along_axis(array, at, axis=0)


def direction_factors(axis_number):
    drift = VELOCITY[axis_number]
    wave = abs(drift) + 1.0
    carried = (0.5 * (wave - drift), 0.5 * (wave + drift))
    if drift >= 0:
        rising = (0.0, 0.5 * wave)
        falling = (0.5, 0.5 * drift)
    else:
        rising = (-0.5 * drift, 0.5)
        falling = (0.5 * wave, 0.0)
    return carried, rising, falling


def store_factors(out, spacing, weight):
    waves = [abs(drift) + 1.0 for drift in VELOCITY]
    spread = (waves[0] * spacing[0] + waves[1] * spacing[1]) + waves[2] * spacing[2]
    time_step = COURANT / spread
    for number, part in enumerate((4.0, 3.0, 2.0, 1.0)):
        scale = time_step * (1.0 / part)
        if number == 3:
            scale = scale * weight
        out[number, 0] = -(scale * spread)
        for axis_number in range(3):
            unit = scale * spacing[axis_number]
            carried, rising, falling = direction_factors(axis_number)
            one_sided = rising if 0.0 in rising else falling
            two_sided = falling if 0.0 in rising else rising
            for place, factor in enumerate((*carried, one_sided[0] + one_sided[1], *two_sided)):
                out[number, 1 + 5 * axis_number + place] = unit * factor
        out[number, 16] = weight


def splat(scalar):
    return jnp.full((ROWS, LANES), scalar, jnp.float32)


def spacing_of(level):
    return lax.shift_left(jnp.int32(1), level).astype(jnp.float32)


def own_factors(out, levels_ref, kind, weight):
    store_factors(out, [splat(spacing_of(levels_ref[kind, 0, axis])) for axis in range(3)], splat(weight))


def row_index():
    return lax.broadcasted_iota(jnp.int32, (ROWS, LANES), 0)


def by_slot(scalars):
    value = splat(scalars[0])
    for slot, scalar in enumerate(scalars[1:], 1):
        value = jnp.where(row_index() == slot, scalar, value)
    return value


def held_tables(me, block_ref, fact_refs, facts, factors, rows, masks):
    slots = block_ref.shape[1]
    for number, ref in enumerate(fact_refs):
        for item in range(3):
            facts[number, item] = spacing_of(ref[item].astype(jnp.int32))
        facts[number, 3] = ref[6]
    grids = [block_ref[me, slot] // slots for slot in range(slots)]
    places = [block_ref[me, slot] % slots for slot in range(slots)]
    numbers = [jnp.bitwise_xor(grid, me) - 1 for grid in grids]
    columns = [by_slot([facts[number, item] for number in numbers]) for item in range(4)]
    store_factors(factors, columns[:3], columns[3])
    for other in range(len(fact_refs)):
        for place, shift in enumerate((0, 1, -1)):
            at = jnp.zeros((ROWS, LANES), jnp.int32)
            mask = jnp.zeros((ROWS, LANES), jnp.float32)
            for slot in range(slots):
                target = jnp.where(numbers[slot] == other, (places[slot] + shift) % slots, -1)
                hit = row_index() == target
                at = jnp.where(hit, slot, at)
                mask = jnp.where(hit, 1.0, mask)
            rows[other, place] = at
            masks[other, place] = mask


def count_tiles(owner_ref, groups, start, amount, rank):
    for reader in range(groups):
        amount[reader] = 0
    for tile in range(owner_ref.shape[1]):
        reader = owner_ref[0, tile]
        rank[tile] = amount[reader]
        amount[reader] = amount[reader] + 1
    total = jnp.int32(0)
    for reader in range(groups):
        start[reader] = total
        total = total + amount[reader]


def tile_scratch(groups, tiles):
    return [pltpu.SMEM((groups,), jnp.int32), pltpu.SMEM((groups,), jnp.int32), pltpu.SMEM((tiles,), jnp.int32)]


def first_slot(start, kind):
    return (start + 1 - kind) // 2


def tile_tables(me, owner_ref, groups, counts, table):
    start, amount, rank = counts
    count_tiles(owner_ref, groups, start, amount, rank)
    kind = me % 2
    lists = [[jnp.zeros((ROWS, LANES), jnp.int32) for _ in range(2)] for _ in range(2)]
    for tile in range(owner_ref.shape[1]):
        position = start[owner_ref[0, tile]] + rank[tile]
        for number in (0, 1):
            mine = position % 2 == (kind if number == 1 else 1 - kind)
            hit = row_index() == jnp.where(mine, position // 2, -1)
            lists[number][0] = jnp.where(hit, tile // 2, lists[number][0])
            lists[number][1] = jnp.where(hit, tile % 2, lists[number][1])
    for number in (0, 1):
        for item in (0, 1):
            table[number, item] = lists[number][item]


def acoustic(axis_number, factors, rising_next, rising_prev, falling_next, falling_prev):
    one, two_next, two_prev = factors
    if VELOCITY[axis_number] >= 0:
        rising = mul(one, rising_prev)
        falling = add(mul(two_next, falling_next), mul(two_prev, falling_prev))
    else:
        rising = add(mul(two_next, rising_next), mul(two_prev, rising_prev))
        falling = mul(one, falling_next)
    return add(rising, falling), sub(rising, falling)


def section(src, src_lines, src_at, state, state_at, dst, dst_lines, dst_at, count, factors, wrap, scaled):
    def layer(number, carry):
        cache = {}

        def cell(field, parity, line, step=0):
            low, high = src_lines
            key = (field, parity, line, step)
            if key in cache:
                return cache[key]
            if low <= line < high:
                value = src[field, src_at + number + step, parity, line - low]
            elif wrap and line < low:
                value = pltpu.roll(cell(field, parity, high - 1), 1, 0)
            elif wrap:
                value = pltpu.roll(cell(field, parity, low), ROWS - 1, 0)
            else:
                value = None
            cache[key] = value
            return value

        def pair(axis_number, parity, line, step=0):
            key = ("pair", axis_number, parity, line, step)
            if key not in cache:
                pressure = cell(4, parity, line, step)
                speed = cell(1 + axis_number, parity, line, step)
                cache[key] = (None, None) if pressure is None else (pressure + speed, pressure - speed)
            return cache[key]

        centre = factors[0]
        for line in range(*dst_lines):
            for parity in (0, 1):
                result = [None] * 5
                for field in range(5):
                    terms = mul(centre, cell(field, parity, line))
                    if 0 <= line < 4:
                        held = state[field, state_at + number, parity, line]
                        terms = add(mul(factors[16], held) if scaled else held, terms)
                    result[field] = terms
                for axis_number in range(3):
                    forward, backward, *sound = factors[1 + 5 * axis_number : 6 + 5 * axis_number]

                    def neighbours(read):
                        if axis_number == 0:
                            other = read(1 - parity, line, 0)
                            if parity == 0:
                                return other, [turn_lanes(part, 1) for part in other]
                            return [turn_lanes(part, LANES - 1) for part in other], other
                        if axis_number == 1:
                            return read(parity, line + 1, 0), read(parity, line - 1, 0)
                        return read(parity, line, 1), read(parity, line, -1)

                    for field in range(4):
                        if field != 1 + axis_number:
                            (after,), (before,) = neighbours(
                                lambda *where, field=field: [cell(field, *where)]
                            )
                            result[field] = add(result[field], add(mul(forward, after), mul(backward, before)))
                    after, before = neighbours(lambda *where: pair(axis_number, *where))
                    pressure, speed = acoustic(
                        axis_number, sound, after[0], before[0], after[1], before[1]
                    )
                    result[4] = add(result[4], pressure)
                    result[1 + axis_number] = add(result[1 + axis_number], speed)
                for field in range(5):
                    dst[field, dst_at + number, parity, line - dst_lines[0]] = result[field]
        return carry

    lax.fori_loop(0, count, layer, 0)


def gather_slots_kernel(others, me_ref, block_ref, checkpoint, *outs):
    me = me_ref[0]
    slots = checkpoint.shape[0]
    grids = [block_ref[me, slot] // slots for slot in range(slots)]
    for slot in range(slots):
        rank = jnp.int32(0)
        for earlier in range(slot):
            rank = rank + (grids[earlier] == grids[slot]).astype(jnp.int32)
        for number in range(others):

            @pl.when(grids[slot] == jnp.bitwise_xor(me, number + 1))
            def _(slot=slot, number=number, rank=rank):
                def layer(z, carry):
                    for field in range(5):
                        outs[number][rank, field, z] = checkpoint[slot, field, z]
                    return carry

                lax.fori_loop(0, checkpoint.shape[2], layer, 0)


def gather_slots(me, slot_block, checkpoint, others):
    piece = shape(HELD_MOST, *checkpoint.shape[1:])
    return pl.pallas_call(
        functools.partial(gather_slots_kernel, others),
        out_shape=[piece] * others,
        in_specs=[spec_smem(), spec_smem(), spec_vmem()],
        out_specs=[spec_vmem()] * others,
        compiler_params=params(),
        cost_estimate=cost(1),
        name="gather_slots",
    )(me, slot_block, checkpoint)


def store_lines(lines, matrix, out, z):
    halves = [lines[:, side].reshape(5 * 4 * ROWS, LANES) for side in (0, 1)]
    moved = move_lanes(halves[0], matrix[0]) + move_lanes(halves[1], matrix[1])
    moved = moved.reshape(5, 4, ROWS, 2 * LANES)
    for parity in (0, 1):
        lanes = slice(parity * LANES, (parity + 1) * LANES)
        out[0, z, parity] = moved[0, :, :, lanes] - moved[4, :, :, lanes]
        for field in range(1, 5):
            out[field, z, parity] = moved[field, :, :, lanes]


def prepare_kernel(checkpoint, live, low, high, held_lines, own_lines, matrix):
    slots = checkpoint.shape[0]
    one_hot(matrix, False)

    for half, out in ((1, high), (0, low)):

        def layer(z, carry, half=half, out=out):
            for field in range(5):
                for side in (0, 1):
                    lanes = pl.ds(side * LANES, LANES)
                    for slot in range(slots):
                        held_lines[field, side, pl.ds(slot, 4, stride=ROWS), :] = checkpoint[
                            slot, field, half * DEPTH + z, :, lanes
                        ]
                    for group in range(4):
                        rows = live[field, half * DEPTH + z, pl.ds(group * ROWS, ROWS), lanes]
                        for block in (0, 1):
                            own_lines[field, side, pl.ds(2 * group + block, 4, stride=ROWS), :] = rows[
                                4 * block : 4 * block + 4
                            ]
            store_lines(held_lines, matrix, out.at[0], z)
            store_lines(own_lines, matrix, out.at[1], z)
            return carry

        lax.fori_loop(0, DEPTH, layer, 0)


def prepare(checkpoint, live):
    lines = pltpu.VMEM((5, 2, 4 * ROWS, LANES), jnp.float32)
    half = shape(2, 5, DEPTH, 2, 4, ROWS, LANES)
    return pl.pallas_call(
        prepare_kernel,
        out_shape=[half, half],
        in_specs=[spec_vmem(), spec_vmem()],
        out_specs=[spec_vmem(), spec_vmem()],
        scratch_shapes=[lines, lines, one_hot_scratch()],
        compiler_params=params(),
        cost_estimate=cost(1),
        name="prepare",
    )(checkpoint, live)


HELD_LINES = ((0, 4), (-1, 5), (-2, 6), (-3, 7), (-4, 8))
LIVE_LINES = ((0, 4),) * 5
CARRIES = ((0, 6), (0, 8), (0, 10), (1, 4), (1, 4), (1, 4))


def copy_layers(src, src_at, dst, dst_at, count):
    def layer(z, carry):
        dst[:, dst_at + z] = src[:, src_at + z]
        return carry

    lax.fori_loop(0, count, layer, 0)


def weigh_and_pack(others, held_out, live_out, rows_ref, mask_ref, tiles_ref, send, keep):
    def layer(z, carry):
        for field in (4, 0, 1, 2, 3):
            for parity in (0, 1):
                total = [live_out[field, z, parity, line] for line in range(4)]
                for other in range(others):
                    for place, first in ((0, 4), (1, 8), (2, 0)):
                        at = rows_ref[other, place]
                        mask = mask_ref[other, place]
                        for line in range(4):
                            image = held_out[field, z, parity, first + line]
                            total[line] = total[line] + mask * pick_rows(image, at)
                for number, out in ((0, send), (1, keep)):
                    at = tiles_ref[number, 0]
                    lower = tiles_ref[number, 1] == 0
                    for line in (0, 1):
                        value = jnp.where(lower, pick_rows(total[line], at), pick_rows(total[2 + line], at))
                        if field == 0:
                            value = value + out[4, z, parity, line]
                        out[field, z, parity, line] = value
        return carry

    lax.fori_loop(0, DEPTH, layer, 0)


def half_tables(others, scalars, scratch):
    me_ref, block_ref, owner_ref, levels_ref, weights_ref, *fact_refs = scalars
    live_factors, held_factors, rows, masks, tiles, facts, *counts = scratch
    me = me_ref[0]
    own_factors(live_factors, levels_ref, 1, weights_ref[1, 0])
    held_tables(me, block_ref, fact_refs, facts, held_factors, rows, masks)
    tile_tables(me, owner_ref, others + 1, counts, tiles)
    return live_factors, held_factors, rows, masks, tiles


def start_halo(part, held, live, at, sems):
    copies = [
        pltpu.make_async_copy(part.at[kind], state.at[:, pl.ds(at, DEPTH)], sems.at[kind])
        for kind, state in ((0, held), (1, live))
    ]
    for copy in copies:
        copy.start()
    return copies


def first_half_kernel(others, *refs):
    scalars, refs = refs[: 5 + others], refs[5 + others :]
    before, low, high, send, keep, *refs = refs
    carries, refs = refs[:6], refs[6:]
    held, live, h1, h2, h3, h4, l1, l2, l3, l4, sems, *scratch = refs
    waiting = start_halo(before, held, live, 0, sems)
    for kind, state in ((0, held), (1, live)):
        for number, part in ((1, low), (2, high)):
            copy_layers(part.at[kind], 0, state, number * DEPTH, DEPTH)
    live_factors, held_factors, rows, masks, tiles = half_tables(others, scalars, scratch)
    waiting[0].wait()
    run_sections(held, (h1, h2, h3, h4), HELD_LINES, False, held_factors, False)
    waiting[1].wait()
    run_sections(live, (l1, l2, l3, l4), LIVE_LINES, True, live_factors, False)
    last = ((h1, 8), (h2, 6), (h3, 4), (l1, 8), (l2, 6), (l3, 4))
    for (src, at), out in zip(last, carries):
        copy_layers(src, at, out, 0, 2)
    weigh_and_pack(others, h4, l4, rows, masks, tiles, send, keep)


def second_half_kernel(others, *refs):
    scalars, refs = refs[: 5 + others], refs[5 + others :]
    after, high, *refs = refs
    carries, (send, keep, *refs) = refs[:6], refs[6:]
    held, live, h1, h2, h3, h4, l1, l2, l3, l4, sems, *scratch = refs
    waiting = start_halo(after, held, live, DEPTH, sems)
    for kind, state in ((0, held), (1, live)):
        copy_layers(high.at[kind], 0, state, 0, DEPTH)
    for carry, dst in zip(carries, (h1, h2, h3, l1, l2, l3)):
        copy_layers(carry, 0, dst, 0, 2)
    live_factors, held_factors, rows, masks, tiles = half_tables(others, scalars, scratch)
    waiting[0].wait()
    run_sections(held, (h1, h2, h3, h4), HELD_LINES, False, held_factors, True)
    waiting[1].wait()
    run_sections(live, (l1, l2, l3, l4), LIVE_LINES, True, live_factors, True)
    weigh_and_pack(others, h4, l4, rows, masks, tiles, send, keep)


def run_sections(state, stages, lines, wrap, factors, continued):
    for number in range(4):
        row = [factors[number, i] for i in range(17)]
        src = state if number == 0 else stages[number - 1]
        if continued:
            src_at = 3 if number == 0 else 1
            state_at = 3 - number
            dst_at, count = (0 if number == 3 else 2), DEPTH
        else:
            src_at, state_at, dst_at, count = 1, 1 + number, 0, 3 * DEPTH - 2 * (number + 1)
        section(
            src, lines[number], src_at, state, state_at, stages[number], lines[number + 1], dst_at,
            count, row, wrap, number == 3,
        )


def half_step(kernel, scalars, parts, carries_in, layers, last):
    others = len(scalars) - 5
    tiles = scalars[2].shape[1]
    packed = shape(5, DEPTH, 2, 2, ROWS, LANES)
    buffer = lambda count, lines: pltpu.VMEM((5, count, 2, lines, ROWS, LANES), jnp.float32)
    table = lambda *dims, kind=jnp.float32: pltpu.VMEM((*dims, ROWS, LANES), kind)
    carry_shapes = [shape(5, 2, 2, lines, ROWS, LANES) for lines in (6, 8, 10, 4, 4, 4)]
    outs = [packed, packed] + ([] if last else carry_shapes)
    stage_layers = (6, 6, 6, DEPTH) if last else (10, 8, 6, DEPTH)
    return pl.pallas_call(
        functools.partial(kernel, others),
        out_shape=outs,
        in_specs=[spec_smem()] * len(scalars) + [spec_any()] + [spec_vmem()] * (len(parts) - 1 + len(carries_in)),
        out_specs=[spec_vmem()] * len(outs),
        scratch_shapes=[buffer(layers, 4), buffer(layers, 4)]
        + [buffer(count, lines) for count, lines in zip(stage_layers, (6, 8, 10, 12))]
        + [buffer(count, 4) for count in stage_layers]
        + [pltpu.SemaphoreType.DMA((2,))]
        + [table(4, 17), table(4, 17), table(others, 3, kind=jnp.int32), table(others, 3), table(2, 2, kind=jnp.int32)]
        + [pltpu.SMEM((others, 4), jnp.float32)]
        + tile_scratch(others + 1, tiles),
        compiler_params=params(),
        cost_estimate=cost(8 if last else 12),
        name="second_half" if last else "first_half",
    )(*scalars, *parts, *carries_in)


def share_kernel(groups, me_ref, owner_ref, keep_low, arrived_low, keep_high, arrived_high, *refs):
    outs, (table, *counts) = refs[:groups], refs[groups:]
    start = counts[0]
    count_tiles(owner_ref, groups, *counts)
    me = me_ref[0]
    for number in range(groups):
        first = first_slot(start[jnp.bitwise_xor(me, number)], me % 2)
        table[number] = jnp.minimum(first + row_index() // 2, ROWS - 1)

    for half, keep, arrived in ((0, keep_low, arrived_low), (1, keep_high, arrived_high)):

        def layer(z, carry, half=half, keep=keep, arrived=arrived):
            odd = row_index() % 2 == 1
            for field in range(5):
                for parity in (0, 1):
                    first = keep[field, z, parity, 0] + arrived[field, z, parity, 0]
                    second = keep[field, z, parity, 1] + arrived[field, z, parity, 1]
                    for number in range(groups):
                        at = table[number]
                        outs[number][field, half * DEPTH + z, parity] = jnp.where(
                            odd, pick_rows(second, at), pick_rows(first, at)
                        )
            return carry

        lax.fori_loop(0, DEPTH, layer, 0)


def share(me, owner, halves, groups):
    piece = shape(5, 2 * DEPTH, 2, ROWS, LANES)
    return pl.pallas_call(
        functools.partial(share_kernel, groups),
        out_shape=[piece] * groups,
        in_specs=[spec_smem()] * 2 + [spec_vmem()] * len(halves),
        out_specs=[spec_vmem()] * groups,
        scratch_shapes=[pltpu.VMEM((groups, ROWS, LANES), jnp.int32)] + tile_scratch(groups, owner.shape[1]),
        compiler_params=params(),
        cost_estimate=cost(1),
        name="share",
    )(me, owner, *halves)


def collect_kernel(groups, tile_most, me_ref, owner_ref, *rest):
    pieces, (out, matrix, *counts) = rest[:groups], rest[groups:]
    count_tiles(owner_ref, groups, *counts)
    one_hot(matrix, True)
    me = me_ref[0]
    mine = counts[1][me]
    swap = counts[0][me] % 2 != me % 2

    def layer(z, carry):
        even = 2 * (row_index() // 2) < mine
        odd = 2 * (row_index() // 2) + 1 < mine
        moved = None
        for parity in (0, 1):
            sums = []
            for kind in (0, 1):
                value = pieces[kind][:, z, parity]
                for other in range(2 + kind, groups, 2):
                    value = value + pieces[other][:, z, parity]
                sums.append(value)
            rows = jnp.concatenate(
                [
                    jnp.where(even, jnp.where(swap, sums[1], sums[0]), 0.0),
                    jnp.where(odd, jnp.where(swap, sums[0], sums[1]), 0.0),
                ]
            )
            part = move_lanes(rows.reshape(10 * ROWS, LANES), matrix[parity])
            moved = part if moved is None else moved + part
        moved = moved.reshape(2, 5, ROWS, 2 * LANES)
        for kind in (0, 1):
            for field in range(5):
                for slot in range(tile_most // 2):
                    out[2 * slot + kind, field, z] = moved[kind, field, 2 * slot : 2 * slot + 2]
        return carry

    lax.fori_loop(0, 2 * DEPTH, layer, 0)


def collect(me, owner, pieces, tile_most):
    groups = len(pieces)
    return pl.pallas_call(
        functools.partial(collect_kernel, groups, tile_most),
        out_shape=shape(tile_most, 5, 2 * DEPTH, TILE_LINES, 2 * LANES),
        in_specs=[spec_smem()] * 2 + [spec_vmem()] * len(pieces),
        out_specs=spec_vmem(),
        scratch_shapes=[one_hot_scratch()] + tile_scratch(groups, owner.shape[1]),
        compiler_params=params(),
        cost_estimate=cost(2),
        name="collect",
    )(me, owner, *pieces)


def place_kernel(others, me_ref, block_ref, *rest):
    pieces, (low, high, lines, matrix, table) = rest[:others], rest[others:]
    one_hot(matrix, False)
    me = me_ref[0]
    slots = block_ref.shape[1]
    groups = block_ref.shape[0]
    inner = (me == groups // 2 - 1) | (me == groups // 2)
    for number in range(others):
        for slot in range(HELD_MOST):
            table[number, slot] = -1
        holder = jnp.bitwise_xor(me, min(number + 1, groups - 1))
        rank = jnp.int32(0)
        for slot in range(slots):
            block = block_ref[holder, slot]
            mine = block // slots == me
            if number >= groups - 2:
                mine = mine & (inner if number == groups - 1 else jnp.logical_not(inner))
            table[number, jnp.where(mine, rank, HELD_MOST)] = block % slots
            rank = rank + mine.astype(jnp.int32)
    for half, out in ((0, low), (1, high)):

        def layer(z, carry, half=half, out=out):
            for number in range(others):
                for slot in range(HELD_MOST):
                    block = table[number, slot]

                    @pl.when(block >= 0)
                    def _(number=number, slot=slot, block=block):
                        for field in range(5):
                            for side in (0, 1):
                                lines[field, side, pl.ds(block, 4, stride=ROWS), :] = pieces[number][
                                    slot, field, half * DEPTH + z, :, pl.ds(side * LANES, LANES)
                                ]

            store_lines(lines, matrix, out, z)
            return carry

        lax.fori_loop(0, DEPTH, layer, 0)


def place(me, slot_block, pieces):
    half = shape(5, DEPTH, 2, 4, ROWS, LANES)
    return pl.pallas_call(
        functools.partial(place_kernel, len(pieces)),
        out_shape=[half, half],
        in_specs=[spec_smem()] * 2 + [spec_vmem()] * len(pieces),
        out_specs=[spec_vmem()] * 2,
        scratch_shapes=[
            pltpu.VMEM((5, 2, 4 * ROWS, LANES), jnp.float32),
            one_hot_scratch(),
            pltpu.SMEM((len(pieces), HELD_MOST + 1), jnp.int32),
        ],
        compiler_params=params(),
        cost_estimate=cost(3),
        name="place",
    )(me, slot_block, *pieces)


def recover_kernel(levels_ref, before, low, high, after, out, state, s1, s2, s3, s4, lines, factors, matrix):
    one_hot(matrix, True)
    own_factors(factors, levels_ref, 0, 1.0)
    for number, part in enumerate((before, low, high, after)):
        copy_layers(part, 0, state, number * DEPTH, DEPTH)
    for number, dst in enumerate((s1, s2, s3, s4)):
        src = state if number == 0 else (s1, s2, s3)[number - 1]
        row = [factors[number, i] for i in range(17)]
        section(src, (0, 4), 1, state, 1 + number, dst, (0, 4), 0, 4 * DEPTH - 2 * (number + 1), row, True, False)

    def layer(z, carry):
        moved = None
        for parity in (0, 1):
            rows = s4[:, z, parity]
            rows = jnp.concatenate([rows[:1] + rows[4:], rows[1:]]).reshape(5 * 4 * ROWS, LANES)
            part = move_lanes(rows, matrix[parity])
            moved = part if moved is None else moved + part
        moved = moved.reshape(5, 4, ROWS, 2 * LANES)
        for field in range(5):
            for side in (0, 1):
                for line in range(4):
                    lines[field, side, pl.ds(line, ROWS, stride=4), :] = moved[
                        field, line, :, side * LANES : (side + 1) * LANES
                    ]
                out[field, z, :, pl.ds(side * LANES, LANES)] = lines[field, side]
        return carry

    lax.fori_loop(0, 2 * DEPTH, layer, 0)


def recover(levels, parts):
    buffer = lambda count: pltpu.VMEM((5, count, 2, 4, ROWS, LANES), jnp.float32)
    return pl.pallas_call(
        recover_kernel,
        out_shape=shape(5, 2 * DEPTH, 4 * ROWS, 2 * LANES),
        in_specs=[spec_smem()] + [spec_vmem()] * 4,
        out_specs=spec_vmem(),
        scratch_shapes=[buffer(count) for count in (16, 14, 12, 10, 8)]
        + [
            pltpu.VMEM((5, 2, 4 * ROWS, LANES), jnp.float32),
            pltpu.VMEM((4, 17, ROWS, LANES), jnp.float32),
            one_hot_scratch(),
        ],
        compiler_params=params(),
        cost_estimate=cost(10),
        name="recover",
    )(levels, *parts)


def after_all(*arrays):
    return lax.optimization_barrier(arrays)


def body(checkpoint, slot_block, live_state, levels, coefficients, tile_owner):
    groups = lax.axis_size("buddy")
    slabs = lax.axis_size("slab")
    me = lax.axis_index("buddy").astype(jnp.int32).reshape(1)
    tile_most = 2 * tile_owner.shape[1] // groups
    trade = lambda array, d: lax.ppermute(array, "buddy", [(i, i ^ d) for i in range(groups)])
    upward = lambda array: lax.ppermute(array, "slab", [(i, (i + 1) % slabs) for i in range(slabs)])
    downward = lambda array: lax.ppermute(array, "slab", [((i + 1) % slabs, i) for i in range(slabs)])

    facts = jnp.concatenate([levels.astype(jnp.float32).reshape(-1), coefficients.reshape(-1)])
    other_facts = [trade(facts, d) for d in range(1, groups)]
    low, high = prepare(checkpoint, live_state[0])
    before = upward(high)
    sent = gather_slots(me, slot_block, checkpoint, groups - 1)
    low, sent, other_facts = after_all(low, sent, other_facts)
    after = downward(low)
    middle = (groups // 2 - 1, groups // 2)
    received = [trade(sent[d - 1], d) for d in range(1, groups - 1)]
    received.append(
        lax.ppermute(sent[-1], "buddy", [(i, i ^ (groups - 1)) for i in range(groups) if i not in middle])
    )

    scalars = (me, slot_block, tile_owner, levels, coefficients, *other_facts)
    send_low, keep_low, *carries = half_step(first_half_kernel, scalars, (before, low, high), (), 3 * DEPTH, False)
    send_low, late, carries[0] = after_all(send_low, sent[-1], carries[0])
    arrived_low = trade(send_low, 1)
    received.append(lax.ppermute(late, "buddy", [middle, middle[::-1]]))
    send_high, keep_high = half_step(second_half_kernel, scalars, (after, high), carries, 2 * DEPTH, True)
    arrived_high = trade(send_high, 1)

    keep_high, received = after_all(keep_high, received)
    restored_low, restored_high = place(me, slot_block, received)
    restored_before = upward(restored_high)
    restored_after = downward(restored_low)
    shares = share(me, tile_owner, (keep_low, arrived_low, keep_high, arrived_high), groups)
    pieces = [shares[0]] + [trade(shares[d], d) for d in range(1, groups)]
    recovered = recover(levels, (restored_before, restored_low, restored_high, restored_after))
    recovered, pieces[0] = after_all(recovered, pieces[0])
    combined = collect(me, tile_owner, pieces, tile_most)
    return recovered[None], combined


def solution(mesh):
    return jax.shard_map(
        body,
        mesh=mesh,
        in_specs=(
            P("buddy", None, "slab", None, None),
            P(),
            P("buddy", None, "slab", None, None),
            P(None, "buddy", None),
            P(None, "buddy"),
            P("slab", None),
        ),
        out_specs=(P("buddy", None, "slab", None, None), P("buddy", None, "slab", None, None)),
        check_vma=False,
    )
```

time: 168 us -> 108 us (0.64)
  the two profiles are of different devices: /device:TPU:0 before, /device:TPU:12 now
where the time goes in v1:
time: 108 us; the launch traced here: 107 us
  Pallas kernels  46.1 us (43%)
  waiting for transfers between devices  33.6 us (31%)
  starting transfers between devices  22.5 us (21%)
  local copies, waits for them, and re-layouts  4.38 us (4%)
    pallas_call x2, Pallas kernels, half_step(): pl.pallas_call(functools.partial(kernel, others), out_shape=outs, in_spec...  21.7 us
    ppermute x10, starting transfers between devices, body(): lax.ppermute(array, 'buddy', [(i, i ^ d) for i in range(groups)])  15.7 us
    ppermute x2, waiting for transfers between devices, body(): lax.ppermute(array, 'slab', [(i, (i + 1) % slabs) for i in range(slabs)])  10.8 us
    pallas_call x1, Pallas kernels, recover(): pl.pallas_call(recover_kernel, out_shape=shape(5, 2 * DEPTH, 4 * ROWS, 2...  10.7 us
    ppermute x2, waiting for transfers between devices, body(): lax.ppermute(array, 'slab', [((i + 1) % slabs, i) for i in range(slabs)])  10.7 us
    ppermute x10, waiting for transfers between devices, body(): lax.ppermute(array, 'buddy', [(i, i ^ d) for i in range(groups)])  7.1 us
    ppermute x1, waiting for transfers between devices, body(): received.append(lax.ppermute(late, 'buddy', [middle, middle[::-1]]))  5.03 us
    pallas_call x1, Pallas kernels, prepare(): pl.pallas_call(prepare_kernel, out_shape=[half, half], in_specs=[spec_vme...  4.54 us
  transfers between devices with their start and end apart: 16, of which 6 were waited for; matrix products, arithmetic and copies ran while one was open for 0% of the time, Pallas kernels for 36%

profile of v1, /device:TPU:12, one launch (start us, length us, event | category | flops | bytes accessed | tf_op | source)
XLA Modules:
  0.0 107.4 jit_solution(6305307703288838850)
XLA Ops:
  0.6 1.3 %copy-done = f32[8,5,8,4,256]{4,3,2,1,0:T(4,128)S(1)} copy-done((f32[8,5,8,4,256]{4,3,2,1,0:T(4,128)S(1)}, f32[8,5,8,4,256]{4,3,2,1,0:T(4,128)}, u32[]{:S(2)}) %copy-start) | copy-done | bytes 1310744
  2.0 1.3 %copy-done.2 = f32[1,5,8,32,256]{4,3,2,1,0:T(8,128)S(1)} copy-done((f32[1,5,8,32,256]{4,3,2,1,0:T(8,128)S(1)}, f32[1,5,8,32,256]{4,3,2,1,0:T(8,128)}, u32[]{:S(2)}) %copy-start.2) | copy-done | bytes 1310744
  3.3 4.5 %prepare.1 = (f32[2,5,4,2,4,8,128]{6,5,4,3,2,1,0:T(8,128)}, f32[2,5,4,2,4,8,128]{6,5,4,3,2,1,0:T(8,128)S(1)}) custom-call(f32[8,5,8,4,256]{4,3,2,1,0:T(4,128)S(1)} %copy-done, f32[5,8,32,256]{3,2,1,0:T(8,128)S(1)} %bitcast.4), custom_call_target="tpu_custom_call" | custom-call | bytes 1 | tf_op jit(solution)/shard_map/prepare/pallas_call | solution.py:375
  7.8 0.0 collective-permute-start.4
  7.8 0.0 copy-done.4
  7.8 0.1 reshape.14
  7.9 0.1 pad_maximum_fusion
  8.0 0.4 collective-permute-start
  8.5 2.6 %collective-permute-start.1 = (f32[8]{0:T(128)S(1)}, f32[8]{0:T(128)S(1)}, u32[]{:S(2)}, u32[]{:S(2)}) collective-permute-start(f32[8]{0:T(128)S(1)} %pad_maximum_fusion), channel_id=1, source_target_pairs={{0,2},{1,3},{2,0},{3,1},{4,6},{5,7},{6,4},{7,5},{8,10},{9,11},{10,... | collective-permute-start | bytes 104 | tf_op jit(solution)/shard_map/ppermute | solution.py:734
  11.0 0.4 collective-permute-start.2
  11.5 1.1 %gather_slots.1 = (f32[3,5,8,4,256]{4,3,2,1,0:T(4,128)S(1)}, f32[3,5,8,4,256]{4,3,2,1,0:T(4,128)S(1)}, f32[3,5,8,4,256]{4,3,2,1,0:T(4,128)S(1)}) custom-call(s32[1]{0:T(128)} %bitcast.me_ref.refs_0_, s32[4,8]{1,0:T(4,128)S(1)} %copy-done.3, f32[8,5,8,4,256]{4,3,2,1,0:T(4,128)S(1)} %copy-done.1), custom_call_target="tpu_custom_call" | custom-call | bytes 1 | tf_op jit(solution)/shard_map/gather_slots/pallas_call | solution.py:323
  12.6 0.8 copy-done.6
  13.4 0.8 copy-done.7
  14.2 0.0 collective-permute-done.refs_5_
  14.2 0.0 collective-permute-done.1.refs_6_
  14.2 0.4 collective-permute-done.2.refs_7_
  14.6 1.5 %collective-permute-start.3 = (f32[2,5,4,2,4,8,128]{6,5,4,3,2,1,0:T(8,128)}, f32[2,5,4,2,4,8,128]{6,5,4,3,2,1,0:T(8,128)S(1)}, u32[]{:S(2)}, u32[]{:S(2)}) collective-permute-start(f32[2,5,4,2,4,8,128]{6,5,4,3,2,1,0:T(8,128)} %get-tuple-element.47.refs_9_), channel_id=1, source_target_pairs={{4,0},{8,4},{12,8},{16,12},{20,16},{24,20},{28,24},{0,28},{5,1},{9... | collective-permute-start | bytes 3932168 | tf_op jit(solution)/shard_map/ppermute | solution.py:736
  16.1 0.1 copy.9.refs_4_
  16.2 0.7 collective-permute-start.7
  16.8 6.2 %collective-permute-start.5 = (f32[3,5,8,4,256]{4,3,2,1,0:T(4,128)}, f32[3,5,8,4,256]{4,3,2,1,0:T(4,128)S(1)}, u32[]{:S(2)}, u32[]{:S(2)}) collective-permute-start(f32[3,5,8,4,256]{4,3,2,1,0:T(4,128)} %copy-done.7), channel_id=1, source_target_pairs={{0,1},{1,0},{2,3},{3,2},{4,5},{5,4},{6,7},{7,6},{8,9},{9,8},{10,11... | collective-permute-start | bytes 1474568 | tf_op jit(solution)/shard_map/ppermute | solution.py:734
  23.1 0.3 collective-permute-start.6
  23.4 9.8 %collective-permute-done.4.refs_8_ = f32[2,5,4,2,4,8,128]{6,5,4,3,2,1,0:T(8,128)} collective-permute-done((f32[2,5,4,2,4,8,128]{6,5,4,3,2,1,0:T(8,128)S(1)}, f32[2,5,4,2,4,8,128]{6,5,4,3,2,1,0:T(8,128)}, u32[]{:S(2)}, u32[]{:S(2)}) %collective-permute-start.4) | collective-permute-done | bytes 1310752 | tf_op jit(solution)/shard_map/ppermute | solution.py:735
  33.2 13.5 %first_half.1 = (f32[5,4,2,2,8,128]{5,4,3,2,1,0:T(8,128)S(1)}, f32[5,4,2,2,8,128]{5,4,3,2,1,0:T(8,128)S(1)}, f32[5,2,2,6,8,128]{5,4,3,2,1,0:T(8,128)S(1)}, f32[5...) custom-call(s32[1]{0:T(128)} %bitcast.me_ref.refs_0_, ...), custom_call_target="tpu_custom_call" | custom-call | bytes 12 | tf_op jit(solution)/shard_map/first_half/pallas_call | solution.py:508
  46.7 3.5 %collective-permute-start.8 = (f32[3,5,8,4,256]{4,3,2,1,0:T(4,128)S(1)}, f32[3,5,8,4,256]{4,3,2,1,0:T(4,128)S(1)}, u32[]{:S(2)}, u32[]{:S(2)}) collective-permute-start(f32[3,5,8,4,256]{4,3,2,1,0:T(4,128)S(1)} %get-tuple-element.61), channel_id=1, source_target_pairs={{1,2},{2,1},{5,6},{6,5},{9,10},{10,9},{13,14},{14,13},{17,18},{18,... | collective-permute-start | bytes 1474568 | tf_op jit(solution)/shard_map/ppermute | solution.py:755
  50.2 0.0 collective-permute-done.3.refs_8_
  50.2 0.1 collective-permute-start.11
  50.3 8.2 %second_half.1 = (f32[5,4,2,2,8,128]{5,4,3,2,1,0:T(8,128)S(1)}, f32[5,4,2,2,8,128]{5,4,3,2,1,0:T(8,128)S(1)}) custom-call(s32[1]{0:T(128)} %bitcast.me_ref.refs_0_, s32[4,8]{1,0:T(4,128)S(1)} %copy-done.3, s32[1,16]{1,0:T(1,128)S(1)} %copy-done.5, s32[2,1,3]{2,1,0:T(1,128)S(1)} %copy-done.4, f32[2,1]{1,0:T(2,128)S(1)} %copy.9.refs_4_, ...), custom_call_target="tpu_custom_call" | custom-call | bytes 8 | tf_op jit(solution)/shard_map/second_half/pallas_call | solution.py:508
  58.5 0.0 collective-permute-done.7.rest_2_
  58.5 2.1 %collective-permute-start.12 = (f32[5,4,2,2,8,128]{5,4,3,2,1,0:T(8,128)S(1)}, f32[5,4,2,2,8,128]{5,4,3,2,1,0:T(8,128)S(1)}, u32[]{:S(2)}, u32[]{:S(2)}) collective-permute-start(f32[5,4,2,2,8,128]{5,4,3,2,1,0:T(8,128)S(1)} %get-tuple-element.71), channel_id=1, source_target_pairs={{0,1},{1,0},{2,3},{3,2},{4,5},{5,4},{6,7},{7,6},{8,9},{9,8},{10,11... | collective-permute-start | bytes 983048 | tf_op jit(solution)/shard_map/ppermute | solution.py:734
  60.6 0.0 collective-permute-done.5.rest_0_
  60.6 0.0 collective-permute-done.6.rest_1_
  60.6 5.0 %collective-permute-done.8.rest_3_ = f32[3,5,8,4,256]{4,3,2,1,0:T(4,128)S(1)} collective-permute-done((f32[3,5,8,4,256]{4,3,2,1,0:T(4,128)S(1)}, f32[3,5,8,4,256]{4,3,2,1,0:T(4,128)S(1)}, u32[]{:S(2)}, u32[]{:S(2)}) %collective-permute-start.8) | collective-permute-done | bytes 491552 | tf_op jit(solution)/shard_map/ppermute | solution.py:755
  65.6 3.9 %place.1 = (f32[5,4,2,4,8,128]{5,4,3,2,1,0:T(8,128)S(1)}, f32[5,4,2,4,8,128]{5,4,3,2,1,0:T(8,128)S(1)}) custom-call(s32[1]{0:T(128)} %bitcast.me_ref.refs_0_, s32[4,8]{1,0:T(4,128)S(1)} %copy-done.3, f32[3,5,8,4,256]{4,3,2,1,0:T(4,128)S(1)} %collective-permute-done.5.rest_0_, f32[3,5,8,4,256]{4,3,2,1,0:T(4,128)S(1)} %collective-permute-done.6.rest_1_, ...), custom_call_target="tpu_custom_call" | custom-call | bytes 3 | tf_op jit(solution)/shard_map/place/pallas_call | solution.py:660
  69.5 1.1 %collective-permute-start.10 = (f32[5,4,2,4,8,128]{5,4,3,2,1,0:T(8,128)S(1)}, f32[5,4,2,4,8,128]{5,4,3,2,1,0:T(8,128)S(1)}, u32[]{:S(2)}, u32[]{:S(2)}) collective-permute-start(f32[5,4,2,4,8,128]{5,4,3,2,1,0:T(8,128)S(1)} %get-tuple-element.67.low), channel_id=1, source_target_pairs={{4,0},{8,4},{12,8},{16,12},{20,16},{24,20},{28,24},{0,28},{5,1},{9... | collective-permute-start | bytes 1966088 | tf_op jit(solution)/shard_map/ppermute | solution.py:736
  70.6 0.0 collective-permute-start.9
  70.7 0.0 collective-permute-done.11.arrived_low
  70.7 0.0 collective-permute-done.12.arrived_high
  70.7 0.8 share.1
  71.5 0.1 collective-permute-start.13
  71.6 2.1 %collective-permute-start.14 = (f32[5,8,2,8,128]{4,3,2,1,0:T(8,128)S(1)}, f32[5,8,2,8,128]{4,3,2,1,0:T(8,128)S(1)}, u32[]{:S(2)}, u32[]{:S(2)}) collective-permute-start(f32[5,8,2,8,128]{4,3,2,1,0:T(8,128)S(1)} %get-tuple-element.76), channel_id=1, source_target_pairs={{0,2},{1,3},{2,0},{3,1},{4,6},{5,7},{6,4},{7,5},{8,10},{9,11},{10,... | collective-permute-start | bytes 983048 | tf_op jit(solution)/shard_map/ppermute | solution.py:734
  73.7 1.4 %collective-permute-start.15 = (f32[5,8,2,8,128]{4,3,2,1,0:T(8,128)S(1)}, f32[5,8,2,8,128]{4,3,2,1,0:T(8,128)S(1)}, u32[]{:S(2)}, u32[]{:S(2)}) collective-permute-start(f32[5,8,2,8,128]{4,3,2,1,0:T(8,128)S(1)} %get-tuple-element.77), channel_id=1, source_target_pairs={{0,3},{1,2},{2,1},{3,0},{4,7},{5,6},{6,5},{7,4},{8,11},{9,10},{10,... | collective-permute-start | bytes 983048 | tf_op jit(solution)/shard_map/ppermute | solution.py:734
  75.1 10.7 %collective-permute-done.10.after = f32[5,4,2,4,8,128]{5,4,3,2,1,0:T(8,128)S(1)} collective-permute-done((f32[5,4,2,4,8,128]{5,4,3,2,1,0:T(8,128)S(1)}, f32[5,4,2,4,8,128]{5,4,3,2,1,0:T(8,128)S(1)}, u32[]{:S(2)}, u32[]{:S(2)}) %collective-permute-start.10) | collective-permute-done | bytes 655392 | tf_op jit(solution)/shard_map/ppermute | solution.py:736
  85.7 1.0 collective-permute-done.9.before
  86.8 10.7 %recover.1 = f32[5,8,32,256]{3,2,1,0:T(8,128)} custom-call(s32[2,1,3]{2,1,0:T(1,128)S(1)} %copy-done.4, f32[5,4,2,4,8,128]{5,4,3,2,1,0:T(8,128)S(1)} %collective-permute-done.9.before, f32[5,4,2,4,8,128]{5,4,3,2,1,0:T(8,128)S(1)} %get-tuple-element.67.low, f32[5,4,2,4,8,128]{5,4,3,2,1,0:T(8,128)S(1)} %get-tuple-element.66.high, ...), custom_call_target="tpu_custom_call" | custom-call | bytes 10 | tf_op jit(solution)/shard_map/recover/pallas_call | solution.py:708
  97.5 0.0 collective-permute-done.13.rest_1_
  97.5 0.0 collective-permute-done.14.rest_2_
  97.5 6.7 %collective-permute-done.15.rest_3_ = f32[5,8,2,8,128]{4,3,2,1,0:T(8,128)S(1)} collective-permute-done((f32[5,8,2,8,128]{4,3,2,1,0:T(8,128)S(1)}, f32[5,8,2,8,128]{4,3,2,1,0:T(8,128)S(1)}, u32[]{:S(2)}, u32[]{:S(2)}) %collective-permute-start.15) | collective-permute-done | bytes 327712 | tf_op jit(solution)/shard_map/ppermute | solution.py:734
  104.2 3.2 %collect.1 = f32[8,5,8,2,256]{4,3,2,1,0:T(2,128)} custom-call(s32[1]{0:T(128)} %bitcast.me_ref.refs_0_, s32[1,16]{1,0:T(1,128)S(1)} %copy-done.5, f32[5,8,2,8,128]{4,3,2,1,0:T(8,128)S(1)} %get-tuple-element.74.rest_0_, f32[5,8,2,8,128]{4,3,2,1,0:T(8,128)S(1)} %collective-permute-done.13.rest_1_, f32[5,8,2,8,128]{4,3,2,1,0:T(8,128)S(1)} %collective-permute-done.14.rest_2_, ...), custom_call_target="tpu_custom_call" | custom-call | bytes 2 | tf_op jit(solution)/shard_map/collect/pallas_call | solution.py:606
  (14 shorter events, 0.0 us)
Async XLA Ops:
  0.6 1.3 %copy-start = (f32[8,5,8,4,256]{4,3,2,1,0:T(4,128)S(1)}, f32[8,5,8,4,256]{4,3,2,1,0:T(4,128)}, u32[]{:S(2)}) copy-start(f32[8,5,8,4,256]{4,3,2,1,0:T(4,128)} %checkpoint.3) | copy-start | bytes 3932164
  1.9 1.3 %copy-start.2 = (f32[1,5,8,32,256]{4,3,2,1,0:T(8,128)S(1)}, f32[1,5,8,32,256]{4,3,2,1,0:T(8,128)}, u32[]{:S(2)}) copy-start(f32[1,5,8,32,256]{4,3,2,1,0:T(8,128)} %param.8) | copy-start | bytes 3932164
  3.3 4.6 %copy-start.4 = (s32[2,1,3]{2,1,0:T(1,128)S(1)}, s32[2,1,3]{2,1,0:T(1,128)}, u32[]{:S(2)}) copy-start(s32[2,1,3]{2,1,0:T(1,128)} %levels_ref.1) | copy-start | bytes 76
  3.3 4.7 %copy-start.8 = (f32[2,1]{0,1:T(1,128)S(1)}, f32[2,1]{0,1:T(1,128)}, u32[]{:S(2)}) copy-start(f32[2,1]{0,1:T(1,128)} %param.10) | copy-start | bytes 28
  3.3 8.2 %copy-start.1 = (f32[8,5,8,4,256]{4,3,2,1,0:T(4,128)S(1)}, f32[8,5,8,4,256]{4,3,2,1,0:T(4,128)}, u32[]{:S(2)}) copy-start(f32[8,5,8,4,256]{4,3,2,1,0:T(4,128)} %checkpoint.3) | copy-start | bytes 3932164
  3.3 8.2 %copy-start.3 = (s32[4,8]{1,0:T(4,128)S(1)}, s32[4,8]{1,0:T(4,128)}, u32[]{:S(2)}) copy-start(s32[4,8]{1,0:T(4,128)} %block_ref.3) | copy-start | bytes 388
  7.8 25.4 %copy-start.5 = (s32[1,16]{1,0:T(1,128)S(1)}, s32[1,16]{1,0:T(1,128)}, u32[]{:S(2)}) copy-start(s32[1,16]{1,0:T(1,128)} %owner_ref.3) | copy-start | bytes 196
  7.8 25.4 %collective-permute-start.4 = (f32[2,5,4,2,4,8,128]{6,5,4,3,2,1,0:T(8,128)S(1)}, f32[2,5,4,2,4,8,128]{6,5,4,3,2,1,0:T(8,128)}, u32[]{:S(2)}, u32[]{:S(2)}) collective-permute-start(f32[2,5,4,2,4,8,128]{6,5,4,3,2,1,0:T(8,128)S(1)} %get-tuple-element.48.refs_10_.refs_9_), channel_id=1, source_target_pairs={{0,4},{4,8},{8,12},{12,16},{16,20},{20,24},{24,28},{28,0},{1,5},{5... | collective-permute-start | bytes 3932168 | tf_op jit(solution)/shard_map/ppermute | solution.py:735
  8.0 6.2 %collective-permute-start = (f32[8]{0:T(128)S(1)}, f32[8]{0:T(128)S(1)}, u32[]{:S(2)}, u32[]{:S(2)}) collective-permute-start(f32[8]{0:T(128)S(1)} %pad_maximum_fusion), channel_id=1, source_target_pairs={{0,1},{1,0},{2,3},{3,2},{4,5},{5,4},{6,7},{7,6},{8,9},{9,8},{10,11... | collective-permute-start | bytes 104 | tf_op jit(solution)/shard_map/ppermute | solution.py:734
  8.5 5.8 %collective-permute-start.1 = (f32[8]{0:T(128)S(1)}, f32[8]{0:T(128)S(1)}, u32[]{:S(2)}, u32[]{:S(2)}) collective-permute-start(f32[8]{0:T(128)S(1)} %pad_maximum_fusion), channel_id=1, source_target_pairs={{0,2},{1,3},{2,0},{3,1},{4,6},{5,7},{6,4},{7,5},{8,10},{9,11},{10,... | collective-permute-start | bytes 104 | tf_op jit(solution)/shard_map/ppermute | solution.py:734
  11.0 3.5 %collective-permute-start.2 = (f32[8]{0:T(128)S(1)}, f32[8]{0:T(128)S(1)}, u32[]{:S(2)}, u32[]{:S(2)}) collective-permute-start(f32[8]{0:T(128)S(1)} %pad_maximum_fusion), channel_id=1, source_target_pairs={{0,3},{1,2},{2,1},{3,0},{4,7},{5,6},{6,5},{7,4},{8,11},{9,10},{10,... | collective-permute-start | bytes 104 | tf_op jit(solution)/shard_map/ppermute | solution.py:734
  12.6 0.8 copy-start.6
  13.4 0.8 copy-start.7
  14.6 35.6 %collective-permute-start.3 = (f32[2,5,4,2,4,8,128]{6,5,4,3,2,1,0:T(8,128)}, f32[2,5,4,2,4,8,128]{6,5,4,3,2,1,0:T(8,128)S(1)}, u32[]{:S(2)}, u32[]{:S(2)}) collective-permute-start(f32[2,5,4,2,4,8,128]{6,5,4,3,2,1,0:T(8,128)} %get-tuple-element.47.refs_9_), channel_id=1, source_target_pairs={{4,0},{8,4},{12,8},{16,12},{20,16},{24,20},{28,24},{0,28},{5,1},{9... | collective-permute-start | bytes 3932168 | tf_op jit(solution)/shard_map/ppermute | solution.py:736
  16.2 42.3 %collective-permute-start.7 = (f32[3,5,8,4,256]{4,3,2,1,0:T(4,128)S(1)}, f32[3,5,8,4,256]{4,3,2,1,0:T(4,128)S(1)}, u32[]{:S(2)}, u32[]{:S(2)}) collective-permute-start(f32[3,5,8,4,256]{4,3,2,1,0:T(4,128)S(1)} %get-tuple-element.61), channel_id=1, source_target_pairs={{0,3},{3,0},{4,7},{7,4},{8,11},{11,8},{12,15},{15,12},{16,19},{19,... | collective-permute-start | bytes 1474568 | tf_op jit(solution)/shard_map/ppermute | solution.py:748
  16.8 43.7 %collective-permute-start.5 = (f32[3,5,8,4,256]{4,3,2,1,0:T(4,128)}, f32[3,5,8,4,256]{4,3,2,1,0:T(4,128)S(1)}, u32[]{:S(2)}, u32[]{:S(2)}) collective-permute-start(f32[3,5,8,4,256]{4,3,2,1,0:T(4,128)} %copy-done.7), channel_id=1, source_target_pairs={{0,1},{1,0},{2,3},{3,2},{4,5},{5,4},{6,7},{7,6},{8,9},{9,8},{10,11... | collective-permute-start | bytes 1474568 | tf_op jit(solution)/shard_map/ppermute | solution.py:734
  23.1 37.5 %collective-permute-start.6 = (f32[3,5,8,4,256]{4,3,2,1,0:T(4,128)}, f32[3,5,8,4,256]{4,3,2,1,0:T(4,128)S(1)}, u32[]{:S(2)}, u32[]{:S(2)}) collective-permute-start(f32[3,5,8,4,256]{4,3,2,1,0:T(4,128)} %copy-done.6), channel_id=1, source_target_pairs={{0,2},{1,3},{2,0},{3,1},{4,6},{5,7},{6,4},{7,5},{8,10},{9,11},{10,... | collective-permute-start | bytes 1474568 | tf_op jit(solution)/shard_map/ppermute | solution.py:734
  46.7 18.9 %collective-permute-start.8 = (f32[3,5,8,4,256]{4,3,2,1,0:T(4,128)S(1)}, f32[3,5,8,4,256]{4,3,2,1,0:T(4,128)S(1)}, u32[]{:S(2)}, u32[]{:S(2)}) collective-permute-start(f32[3,5,8,4,256]{4,3,2,1,0:T(4,128)S(1)} %get-tuple-element.61), channel_id=1, source_target_pairs={{1,2},{2,1},{5,6},{6,5},{9,10},{10,9},{13,14},{14,13},{17,18},{18,... | collective-permute-start | bytes 1474568 | tf_op jit(solution)/shard_map/ppermute | solution.py:755
  50.2 20.5 %collective-permute-start.11 = (f32[5,4,2,2,8,128]{5,4,3,2,1,0:T(8,128)S(1)}, f32[5,4,2,2,8,128]{5,4,3,2,1,0:T(8,128)S(1)}, u32[]{:S(2)}, u32[]{:S(2)}) collective-permute-start(f32[5,4,2,2,8,128]{5,4,3,2,1,0:T(8,128)S(1)} %get-tuple-element.69), channel_id=1, source_target_pairs={{0,1},{1,0},{2,3},{3,2},{4,5},{5,4},{6,7},{7,6},{8,9},{9,8},{10,11... | collective-permute-start | bytes 983048 | tf_op jit(solution)/shard_map/ppermute | solution.py:734
  58.5 12.2 %collective-permute-start.12 = (f32[5,4,2,2,8,128]{5,4,3,2,1,0:T(8,128)S(1)}, f32[5,4,2,2,8,128]{5,4,3,2,1,0:T(8,128)S(1)}, u32[]{:S(2)}, u32[]{:S(2)}) collective-permute-start(f32[5,4,2,2,8,128]{5,4,3,2,1,0:T(8,128)S(1)} %get-tuple-element.71), channel_id=1, source_target_pairs={{0,1},{1,0},{2,3},{3,2},{4,5},{5,4},{6,7},{7,6},{8,9},{9,8},{10,11... | collective-permute-start | bytes 983048 | tf_op jit(solution)/shard_map/ppermute | solution.py:734
  69.5 16.2 %collective-permute-start.10 = (f32[5,4,2,4,8,128]{5,4,3,2,1,0:T(8,128)S(1)}, f32[5,4,2,4,8,128]{5,4,3,2,1,0:T(8,128)S(1)}, u32[]{:S(2)}, u32[]{:S(2)}) collective-permute-start(f32[5,4,2,4,8,128]{5,4,3,2,1,0:T(8,128)S(1)} %get-tuple-element.67.low), channel_id=1, source_target_pairs={{4,0},{8,4},{12,8},{16,12},{20,16},{24,20},{28,24},{0,28},{5,1},{9... | collective-permute-start | bytes 1966088 | tf_op jit(solution)/shard_map/ppermute | solution.py:736
  70.6 16.1 %collective-permute-start.9 = (f32[5,4,2,4,8,128]{5,4,3,2,1,0:T(8,128)S(1)}, f32[5,4,2,4,8,128]{5,4,3,2,1,0:T(8,128)S(1)}, u32[]{:S(2)}, u32[]{:S(2)}) collective-permute-start(f32[5,4,2,4,8,128]{5,4,3,2,1,0:T(8,128)S(1)} %get-tuple-element.66.high), channel_id=1, source_target_pairs={{0,4},{4,8},{8,12},{12,16},{16,20},{20,24},{24,28},{28,0},{1,5},{5... | collective-permute-start | bytes 1966088 | tf_op jit(solution)/shard_map/ppermute | solution.py:735
  71.5 26.0 %collective-permute-start.13 = (f32[5,8,2,8,128]{4,3,2,1,0:T(8,128)S(1)}, f32[5,8,2,8,128]{4,3,2,1,0:T(8,128)S(1)}, u32[]{:S(2)}, u32[]{:S(2)}) collective-permute-start(f32[5,8,2,8,128]{4,3,2,1,0:T(8,128)S(1)} %get-tuple-element.75), channel_id=1, source_target_pairs={{0,1},{1,0},{2,3},{3,2},{4,5},{5,4},{6,7},{7,6},{8,9},{9,8},{10,11... | collective-permute-start | bytes 983048 | tf_op jit(solution)/shard_map/ppermute | solution.py:734
  71.6 25.9 %collective-permute-start.14 = (f32[5,8,2,8,128]{4,3,2,1,0:T(8,128)S(1)}, f32[5,8,2,8,128]{4,3,2,1,0:T(8,128)S(1)}, u32[]{:S(2)}, u32[]{:S(2)}) collective-permute-start(f32[5,8,2,8,128]{4,3,2,1,0:T(8,128)S(1)} %get-tuple-element.76), channel_id=1, source_target_pairs={{0,2},{1,3},{2,0},{3,1},{4,6},{5,7},{6,4},{7,5},{8,10},{9,11},{10,... | collective-permute-start | bytes 983048 | tf_op jit(solution)/shard_map/ppermute | solution.py:734
  73.7 30.5 %collective-permute-start.15 = (f32[5,8,2,8,128]{4,3,2,1,0:T(8,128)S(1)}, f32[5,8,2,8,128]{4,3,2,1,0:T(8,128)S(1)}, u32[]{:S(2)}, u32[]{:S(2)}) collective-permute-start(f32[5,8,2,8,128]{4,3,2,1,0:T(8,128)S(1)} %get-tuple-element.77), channel_id=1, source_target_pairs={{0,3},{1,2},{2,1},{3,0},{4,7},{5,6},{6,5},{7,4},{8,11},{9,10},{10,... | collective-permute-start | bytes 983048 | tf_op jit(solution)/shard_map/ppermute | solution.py:734

commit v2 on v1

--- a/solution.py
+++ b/solution.py
@@ -14,7 +14,6 @@
 DEPTH = 4
 LANES = 128
 ROWS = 8
-VMEM_BYTES = 32 * 1024 * 1024
 
 
 def spec_vmem():
@@ -33,8 +32,8 @@
     return pl.BlockSpec(memory_space=pltpu.HBM)
 
 
-def params():
-    return pltpu.CompilerParams(vmem_limit_bytes=VMEM_BYTES)
+def params(mebibytes):
+    return pltpu.CompilerParams(vmem_limit_bytes=mebibytes * 1024 * 1024)
 
 
 def cost(microseconds, flops=0):
@@ -72,15 +71,11 @@
 
 
 def one_hot(out, join):
-    row = lax.broadcasted_iota(jnp.int32, (LANES, 2 * LANES), 0)
-    column = lax.broadcasted_iota(jnp.int32, (LANES, 2 * LANES), 1)
-    for part in (0, 1):
-        if join:
-            target = 2 * row + part
-        else:
-            cell = row + part * LANES
-            target = cell // 2 + LANES * (cell % 2)
-        out[part] = (column == target).astype(jnp.float32).astype(jnp.bfloat16)
+    row = lax.broadcasted_iota(jnp.int32, out.shape, 0)
+    column = lax.broadcasted_iota(jnp.int32, out.shape, 1)
+    if join:
+        row, column = column, row
+    out[...] = (column == row // 2 + LANES * (row % 2)).astype(jnp.float32).astype(jnp.bfloat16)
 
 
 def move_lanes(rows, matrix):
@@ -93,7 +88,7 @@
 
 
 def one_hot_scratch():
-    return pltpu.VMEM((2, LANES, 2 * LANES), jnp.bfloat16)
+    return pltpu.VMEM((2 * LANES, 2 * LANES), jnp.bfloat16)
 
 
 def pick_rows(array, at):
@@ -325,7 +320,7 @@
         out_shape=[piece] * others,
         in_specs=[spec_smem(), spec_smem(), spec_vmem()],
         out_specs=[spec_vmem()] * others,
-        compiler_params=params(),
+        compiler_params=params(8),
         cost_estimate=cost(1),
         name="gather_slots",
     )(me, slot_block, checkpoint)
@@ -333,8 +328,7 @@
 
 def store_lines(lines, matrix, out, z):
     halves = [lines[:, side].reshape(5 * 4 * ROWS, LANES) for side in (0, 1)]
-    moved = move_lanes(halves[0], matrix[0]) + move_lanes(halves[1], matrix[1])
-    moved = moved.reshape(5, 4, ROWS, 2 * LANES)
+    moved = move_lanes(jnp.concatenate(halves, axis=1), matrix[...]).reshape(5, 4, ROWS, 2 * LANES)
     for parity in (0, 1):
         lanes = slice(parity * LANES, (parity + 1) * LANES)
         out[0, z, parity] = moved[0, :, :, lanes] - moved[4, :, :, lanes]
@@ -342,46 +336,44 @@
             out[field, z, parity] = moved[field, :, :, lanes]
 
 
-def prepare_kernel(checkpoint, live, low, high, held_lines, own_lines, matrix):
+def prepare_kernel(half, firsts, checkpoint, live, *refs):
+    out, held_lines, own_lines, matrix = refs[firsts:]
     slots = checkpoint.shape[0]
     one_hot(matrix, False)
 
-    for half, out in ((1, high), (0, low)):
-
-        def layer(z, carry, half=half, out=out):
-            for field in range(5):
-                for side in (0, 1):
-                    lanes = pl.ds(side * LANES, LANES)
-                    for slot in range(slots):
-                        held_lines[field, side, pl.ds(slot, 4, stride=ROWS), :] = checkpoint[
-                            slot, field, half * DEPTH + z, :, lanes
+    def layer(z, carry):
+        for field in range(5):
+            for side in (0, 1):
+                lanes = pl.ds(side * LANES, LANES)
+                for slot in range(slots):
+                    held_lines[field, side, pl.ds(slot, 4, stride=ROWS), :] = checkpoint[
+                        slot, field, half * DEPTH + z, :, lanes
+                    ]
+                for group in range(4):
+                    rows = live[field, half * DEPTH + z, pl.ds(group * ROWS, ROWS), lanes]
+                    for block in (0, 1):
+                        own_lines[field, side, pl.ds(2 * group + block, 4, stride=ROWS), :] = rows[
+                            4 * block : 4 * block + 4
                         ]
-                    for group in range(4):
-                        rows = live[field, half * DEPTH + z, pl.ds(group * ROWS, ROWS), lanes]
-                        for block in (0, 1):
-                            own_lines[field, side, pl.ds(2 * group + block, 4, stride=ROWS), :] = rows[
-                                4 * block : 4 * block + 4
-                            ]
-            store_lines(held_lines, matrix, out.at[0], z)
-            store_lines(own_lines, matrix, out.at[1], z)
-            return carry
-
-        lax.fori_loop(0, DEPTH, layer, 0)
-
-
-def prepare(checkpoint, live):
+        store_lines(held_lines, matrix, out.at[0], z)
+        store_lines(own_lines, matrix, out.at[1], z)
+        return carry
+
+    lax.fori_loop(0, DEPTH, layer, 0)
+
+
+def prepare(half, checkpoint, live, firsts):
     lines = pltpu.VMEM((5, 2, 4 * ROWS, LANES), jnp.float32)
-    half = shape(2, 5, DEPTH, 2, 4, ROWS, LANES)
     return pl.pallas_call(
-        prepare_kernel,
-        out_shape=[half, half],
-        in_specs=[spec_vmem(), spec_vmem()],
-        out_specs=[spec_vmem(), spec_vmem()],
+        functools.partial(prepare_kernel, half, len(firsts)),
+        out_shape=shape(2, 5, DEPTH, 2, 4, ROWS, LANES),
+        in_specs=[spec_vmem(), spec_vmem()] + [spec_any()] * len(firsts),
+        out_specs=spec_vmem(),
         scratch_shapes=[lines, lines, one_hot_scratch()],
-        compiler_params=params(),
+        compiler_params=params(8),
         cost_estimate=cost(1),
         name="prepare",
-    )(checkpoint, live)
+    )(checkpoint, live, *firsts)
 
 
 HELD_LINES = ((0, 4), (-1, 5), (-2, 6), (-3, 7), (-4, 8))
@@ -464,7 +456,7 @@
 
 def second_half_kernel(others, *refs):
     scalars, refs = refs[: 5 + others], refs[5 + others :]
-    after, high, *refs = refs
+    after, high, _, *refs = refs
     carries, (send, keep, *refs) = refs[:6], refs[6:]
     held, live, h1, h2, h3, h4, l1, l2, l3, l4, sems, *scratch = refs
     waiting = start_halo(after, held, live, DEPTH, sems)
@@ -517,10 +509,26 @@
         + [table(4, 17), table(4, 17), table(others, 3, kind=jnp.int32), table(others, 3), table(2, 2, kind=jnp.int32)]
         + [pltpu.SMEM((others, 4), jnp.float32)]
         + tile_scratch(others + 1, tiles),
-        compiler_params=params(),
+        compiler_params=params(24),
         cost_estimate=cost(8 if last else 12),
         name="second_half" if last else "first_half",
     )(*scalars, *parts, *carries_in)
+
+
+def after_kernel(count, *refs):
+    refs[count][...] = jnp.zeros((ROWS, LANES), jnp.float32)
+
+
+def there(arrays):
+    return pl.pallas_call(
+        functools.partial(after_kernel, len(arrays)),
+        out_shape=shape(ROWS, LANES),
+        in_specs=[spec_any()] * len(arrays),
+        out_specs=spec_vmem(),
+        compiler_params=params(1),
+        cost_estimate=cost(1, 10**12),
+        name="there",
+    )(*arrays)
 
 
 def share_kernel(groups, me_ref, owner_ref, keep_low, arrived_low, keep_high, arrived_high, *refs):
@@ -558,14 +566,14 @@
         in_specs=[spec_smem()] * 2 + [spec_vmem()] * len(halves),
         out_specs=[spec_vmem()] * groups,
         scratch_shapes=[pltpu.VMEM((groups, ROWS, LANES), jnp.int32)] + tile_scratch(groups, owner.shape[1]),
-        compiler_params=params(),
+        compiler_params=params(8),
         cost_estimate=cost(1),
         name="share",
     )(me, owner, *halves)
 
 
 def collect_kernel(groups, tile_most, me_ref, owner_ref, *rest):
-    pieces, (out, matrix, *counts) = rest[:groups], rest[groups:]
+    pieces, (result, out, sems, matrix, *counts) = rest[:groups], rest[groups:]
     count_tiles(owner_ref, groups, *counts)
     one_hot(matrix, True)
     me = me_ref[0]
@@ -575,7 +583,7 @@
     def layer(z, carry):
         even = 2 * (row_index() // 2) < mine
         odd = 2 * (row_index() // 2) + 1 < mine
-        moved = None
+        halves = []
         for parity in (0, 1):
             sums = []
             for kind in (0, 1):
@@ -589,27 +597,35 @@
                     jnp.where(odd, jnp.where(swap, sums[0], sums[1]), 0.0),
                 ]
             )
-            part = move_lanes(rows.reshape(10 * ROWS, LANES), matrix[parity])
-            moved = part if moved is None else moved + part
-        moved = moved.reshape(2, 5, ROWS, 2 * LANES)
+            halves.append(rows.reshape(10 * ROWS, LANES))
+        moved = move_lanes(jnp.concatenate(halves, axis=1), matrix[...]).reshape(2, 5, ROWS, 2 * LANES)
         for kind in (0, 1):
             for field in range(5):
                 for slot in range(tile_most // 2):
                     out[2 * slot + kind, field, z] = moved[kind, field, 2 * slot : 2 * slot + 2]
         return carry
 
-    lax.fori_loop(0, 2 * DEPTH, layer, 0)
+    copies = []
+    for part in range(4):
+        lax.fori_loop(2 * part, 2 * part + 2, layer, 0)
+        layers = pl.ds(2 * part, 2)
+        copies.append(pltpu.make_async_copy(out.at[:, :, layers], result.at[:, :, layers], sems.at[part]))
+        copies[part].start()
+    for copy in copies:
+        copy.wait()
 
 
 def collect(me, owner, pieces, tile_most):
     groups = len(pieces)
+    dims = (tile_most, 5, 2 * DEPTH, TILE_LINES, 2 * LANES)
     return pl.pallas_call(
         functools.partial(collect_kernel, groups, tile_most),
-        out_shape=shape(tile_most, 5, 2 * DEPTH, TILE_LINES, 2 * LANES),
+        out_shape=shape(*dims),
         in_specs=[spec_smem()] * 2 + [spec_vmem()] * len(pieces),
-        out_specs=spec_vmem(),
-        scratch_shapes=[one_hot_scratch()] + tile_scratch(groups, owner.shape[1]),
-        compiler_params=params(),
+        out_specs=spec_any(),
+        scratch_shapes=[pltpu.VMEM(dims, jnp.float32), pltpu.SemaphoreType.DMA((4,)), one_hot_scratch()]
+        + tile_scratch(groups, owner.shape[1]),
+        compiler_params=params(8),
         cost_estimate=cost(2),
         name="collect",
     )(me, owner, *pieces)
@@ -667,13 +683,13 @@
             one_hot_scratch(),
             pltpu.SMEM((len(pieces), HELD_MOST + 1), jnp.int32),
         ],
-        compiler_params=params(),
+        compiler_params=params(8),
         cost_estimate=cost(3),
         name="place",
     )(me, slot_block, *pieces)
 
 
-def recover_kernel(levels_ref, before, low, high, after, out, state, s1, s2, s3, s4, lines, factors, matrix):
+def recover_kernel(levels_ref, before, low, high, after, result, state, s1, s2, s3, s4, out, lines, factors, matrix, sems):
     one_hot(matrix, True)
     own_factors(factors, levels_ref, 0, 1.0)
     for number, part in enumerate((before, low, high, after)):
@@ -684,13 +700,11 @@
         section(src, (0, 4), 1, state, 1 + number, dst, (0, 4), 0, 4 * DEPTH - 2 * (number + 1), row, True, False)
 
     def layer(z, carry):
-        moved = None
+        halves = []
         for parity in (0, 1):
             rows = s4[:, z, parity]
-            rows = jnp.concatenate([rows[:1] + rows[4:], rows[1:]]).reshape(5 * 4 * ROWS, LANES)
-            part = move_lanes(rows, matrix[parity])
-            moved = part if moved is None else moved + part
-        moved = moved.reshape(5, 4, ROWS, 2 * LANES)
+            halves.append(jnp.concatenate([rows[:1] + rows[4:], rows[1:]]).reshape(5 * 4 * ROWS, LANES))
+        moved = move_lanes(jnp.concatenate(halves, axis=1), matrix[...]).reshape(5, 4, ROWS, 2 * LANES)
         for field in range(5):
             for side in (0, 1):
                 for line in range(4):
@@ -698,9 +712,12 @@
                         field, line, :, side * LANES : (side + 1) * LANES
                     ]
                 out[field, z, :, pl.ds(side * LANES, LANES)] = lines[field, side]
+        pltpu.make_async_copy(out.at[:, z], result.at[:, z], sems.at[z]).start()
         return carry
 
     lax.fori_loop(0, 2 * DEPTH, layer, 0)
+    for z in range(2 * DEPTH):
+        pltpu.make_async_copy(out.at[:, z], result.at[:, z], sems.at[z]).wait()
 
 
 def recover(levels, parts):
@@ -709,14 +726,16 @@
         recover_kernel,
         out_shape=shape(5, 2 * DEPTH, 4 * ROWS, 2 * LANES),
         in_specs=[spec_smem()] + [spec_vmem()] * 4,
-        out_specs=spec_vmem(),
+        out_specs=spec_any(),
         scratch_shapes=[buffer(count) for count in (16, 14, 12, 10, 8)]
         + [
+            pltpu.VMEM((5, 2 * DEPTH, 4 * ROWS, 2 * LANES), jnp.float32),
             pltpu.VMEM((5, 2, 4 * ROWS, LANES), jnp.float32),
             pltpu.VMEM((4, 17, ROWS, LANES), jnp.float32),
             one_hot_scratch(),
+            pltpu.SemaphoreType.DMA((2 * DEPTH,)),
         ],
-        compiler_params=params(),
+        compiler_params=params(20),
         cost_estimate=cost(10),
         name="recover",
     )(levels, *parts)
@@ -737,10 +756,11 @@
 
     facts = jnp.concatenate([levels.astype(jnp.float32).reshape(-1), coefficients.reshape(-1)])
     other_facts = [trade(facts, d) for d in range(1, groups)]
-    low, high = prepare(checkpoint, live_state[0])
+    high = prepare(1, checkpoint, live_state[0], ())
     before = upward(high)
     sent = gather_slots(me, slot_block, checkpoint, groups - 1)
-    low, sent, other_facts = after_all(low, sent, other_facts)
+    sent, other_facts = after_all(sent, other_facts)
+    low = prepare(0, checkpoint, live_state[0], other_facts)
     after = downward(low)
     middle = (groups // 2 - 1, groups // 2)
     received = [trade(sent[d - 1], d) for d in range(1, groups - 1)]
@@ -753,7 +773,7 @@
     send_low, late, carries[0] = after_all(send_low, sent[-1], carries[0])
     arrived_low = trade(send_low, 1)
     received.append(lax.ppermute(late, "buddy", [middle, middle[::-1]]))
-    send_high, keep_high = half_step(second_half_kernel, scalars, (after, high), carries, 2 * DEPTH, True)
+    send_high, keep_high = half_step(second_half_kernel, scalars, (after, high, there(received[:-1])), carries, 2 * DEPTH, True)
     arrived_high = trade(send_high, 1)
 
     keep_high, received = after_all(keep_high, received)
@@ -761,7 +781,7 @@
     restored_before = upward(restored_high)
     restored_after = downward(restored_low)
     shares = share(me, tile_owner, (keep_low, arrived_low, keep_high, arrived_high), groups)
-    pieces = [shares[0]] + [trade(shares[d], d) for d in range(1, groups)]
+    pieces = [shares[0]] + [trade(shares[d], d) for d in range(groups - 1, 0, -1)][::-1]
     recovered = recover(levels, (restored_before, restored_low, restored_high, restored_after))
     recovered, pieces[0] = after_all(recovered, pieces[0])
     combined = collect(me, tile_owner, pieces, tile_most)

time: 108 us -> 105 us (0.972)
  the two profiles are of different devices: /device:TPU:12 before, /device:TPU:10 now
where the time goes in v2:
time: 105 us
  Pallas kernels  42.9 us (41%)
  waiting for transfers between devices  37.2 us (35%)
  starting transfers between devices  19.9 us (19%)
  local copies, waits for them, and re-layouts  4.14 us (4%)
    ppermute x10, waiting for transfers between devices, body(): lax.ppermute(array, 'buddy', [(i, i ^ d) for i in range(groups)])  26.5 us
    pallas_call x2, Pallas kernels, half_step(): pl.pallas_call(functools.partial(kernel, others), out_shape=outs, in_spec...  19.6 us
    ppermute x10, starting transfers between devices, body(): lax.ppermute(array, 'buddy', [(i, i ^ d) for i in range(groups)])  16.2 us
    pallas_call x1, Pallas kernels, recover(): pl.pallas_call(recover_kernel, out_shape=shape(5, 2 * DEPTH, 4 * ROWS, 2...  9 us
    ppermute x2, waiting for transfers between devices, body(): lax.ppermute(array, 'slab', [((i + 1) % slabs, i) for i in range(slabs)])  6.21 us
    pallas_call x1, Pallas kernels, place(): pl.pallas_call(functools.partial(place_kernel, len(pieces)), out_shape=[h...  4.37 us
    unnamed x17, local copies, waits for them, and re-layouts  4.05 us
    pallas_call x2, Pallas kernels, prepare(): pl.pallas_call(functools.partial(prepare_kernel, half, len(firsts)), out_...  3.81 us
  transfers between devices with their start and end apart: 16, of which 9 were waited for; matrix products, arithmetic and copies ran while one was open for 0% of the time, Pallas kernels for 37%

profile of v2, /device:TPU:10, one launch (start us, length us, event | category | flops | bytes accessed | tf_op | source)
XLA Modules:
  0.0 105.1 jit_solution(8537853545489352393)
XLA Ops:
  0.6 1.3 %copy-done = f32[8,5,8,4,256]{4,3,2,1,0:T(4,128)S(1)} copy-done((f32[8,5,8,4,256]{4,3,2,1,0:T(4,128)S(1)}, f32[8,5,8,4,256]{4,3,2,1,0:T(4,128)}, u32[]{:S(2)}) %copy-start) | copy-done | bytes 1310744
  1.9 1.3 %copy-done.2 = f32[1,5,8,32,256]{4,3,2,1,0:T(8,128)S(1)} copy-done((f32[1,5,8,32,256]{4,3,2,1,0:T(8,128)S(1)}, f32[1,5,8,32,256]{4,3,2,1,0:T(8,128)}, u32[]{:S(2)}) %copy-start.2) | copy-done | bytes 1310744
  3.3 1.4 %prepare.3.refs_10_.refs_9_ = f32[2,5,4,2,4,8,128]{6,5,4,3,2,1,0:T(8,128)S(1)} custom-call(f32[8,5,8,4,256]{4,3,2,1,0:T(4,128)S(1)} %copy-done, f32[5,8,32,256]{3,2,1,0:T(8,128)S(1)} %bitcast.4), custom_call_target="tpu_custom_call" | custom-call | bytes 1 | tf_op jit(solution)/shard_map/prepare/pallas_call | solution.py:367
  4.7 0.1 collective-permute-start.7
  4.8 0.1 reshape.14
  4.8 0.1 pad_maximum_fusion
  4.9 0.5 collective-permute-start
  5.4 2.6 %collective-permute-start.1 = (f32[8]{0:T(128)S(1)}, f32[8]{0:T(128)S(1)}, u32[]{:S(2)}, u32[]{:S(2)}) collective-permute-start(f32[8]{0:T(128)S(1)} %pad_maximum_fusion), channel_id=1, source_target_pairs={{0,2},{1,3},{2,0},{3,1},{4,6},{5,7},{6,4},{7,5},{8,10},{9,11},{10,... | collective-permute-start | bytes 104 | tf_op jit(solution)/shard_map/ppermute | solution.py:753
  8.0 0.5 collective-permute-start.2
  8.4 0.0 copy-done.1
  8.4 2.2 %gather_slots.1 = (f32[3,5,8,4,256]{4,3,2,1,0:T(4,128)}, f32[3,5,8,4,256]{4,3,2,1,0:T(4,128)}, f32[3,5,8,4,256]{4,3,2,1,0:T(4,128)}) custom-call(s32[1]{0:T(128)} %bitcast.me_ref.refs_0_, s32[4,8]{1,0:T(4,128)S(1)} %copy-done.4, f32[8,5,8,4,256]{4,3,2,1,0:T(4,128)S(1)} %copy-done.1), custom_call_target="tpu_custom_call" | custom-call | bytes 1 | tf_op jit(solution)/shard_map/gather_slots/pallas_call | solution.py:318
  10.7 0.0 collective-permute-done.refs_0_.refs_5_
  10.7 0.0 collective-permute-done.1.refs_1_.refs_6_
  10.7 0.8 collective-permute-done.2.refs_2_.refs_7_
  11.5 0.7 collective-permute-start.6
  12.2 5.4 %collective-permute-start.4 = (f32[3,5,8,4,256]{4,3,2,1,0:T(4,128)}, f32[3,5,8,4,256]{4,3,2,1,0:T(4,128)}, u32[]{:S(2)}, u32[]{:S(2)}) collective-permute-start(f32[3,5,8,4,256]{4,3,2,1,0:T(4,128)} %get-tuple-element.43), channel_id=1, source_target_pairs={{0,1},{1,0},{2,3},{3,2},{4,5},{5,4},{6,7},{7,6},{8,9},{9,8},{10,11... | collective-permute-start | bytes 1474568 | tf_op jit(solution)/shard_map/ppermute | solution.py:753
  17.6 1.7 %collective-permute-start.5 = (f32[3,5,8,4,256]{4,3,2,1,0:T(4,128)}, f32[3,5,8,4,256]{4,3,2,1,0:T(4,128)}, u32[]{:S(2)}, u32[]{:S(2)}) collective-permute-start(f32[3,5,8,4,256]{4,3,2,1,0:T(4,128)} %get-tuple-element.44), channel_id=1, source_target_pairs={{0,2},{1,3},{2,0},{3,1},{4,6},{5,7},{6,4},{7,5},{8,10},{9,11},{10,... | collective-permute-start | bytes 1474568 | tf_op jit(solution)/shard_map/ppermute | solution.py:753
  19.3 0.1 copy.9.refs_4_
  19.4 1.3 %copy-done.3 = f32[1,5,8,32,256]{4,3,2,1,0:T(8,128)S(1)} copy-done((f32[1,5,8,32,256]{4,3,2,1,0:T(8,128)S(1)}, f32[1,5,8,32,256]{4,3,2,1,0:T(8,128)}, u32[]{:S(2)}) %copy-start.3) | copy-done | bytes 1310744
  20.7 2.4 %prepare.2.refs_9_ = f32[2,5,4,2,4,8,128]{6,5,4,3,2,1,0:T(8,128)} custom-call(f32[8,5,8,4,256]{4,3,2,1,0:T(4,128)S(1)} %copy-done.1, f32[5,8,32,256]{3,2,1,0:T(8,128)S(1)} %bitcast.5, f32[8]{0:T(128)S(1)} %collective-permute-done.refs_0_.refs_5_, f32[8]{0:T(128)S(1)} %collective-permute-done.1.refs_1_.refs_6_, f32[8]{0:T(128)S(1)} %collective-permute-done.2.refs_2_.refs_7_), custom_call_target="tpu_custom_call" | custom-call | bytes 1 | tf_op jit(solution)/shard_map/prepare/pallas_call | solution.py:367
  23.1 0.0 collective-permute-start.3
  23.1 0.0 collective-permute-done.7.refs_8_
  23.1 12.0 %first_half.1 = (f32[5,4,2,2,8,128]{5,4,3,2,1,0:T(8,128)S(1)}, f32[5,4,2,2,8,128]{5,4,3,2,1,0:T(8,128)S(1)}, f32[5,2,2,6,8,128]{5,4,3,2,1,0:T(8,128)S(1)}, f32[5...) custom-call(s32[1]{0:T(128)} %bitcast.me_ref.refs_0_, ...), custom_call_target="tpu_custom_call" | custom-call | bytes 12 | tf_op jit(solution)/shard_map/first_half/pallas_call | solution.py:500
  35.1 2.4 %collective-permute-start.8 = (f32[3,5,8,4,256]{4,3,2,1,0:T(4,128)}, f32[3,5,8,4,256]{4,3,2,1,0:T(4,128)}, u32[]{:S(2)}, u32[]{:S(2)}) collective-permute-start(f32[3,5,8,4,256]{4,3,2,1,0:T(4,128)} %get-tuple-element.55), channel_id=1, source_target_pairs={{1,2},{2,1},{5,6},{6,5},{9,10},{10,9},{13,14},{14,13},{17,18},{18,... | collective-permute-start | bytes 1474568 | tf_op jit(solution)/shard_map/ppermute | solution.py:775
  37.6 0.0 collective-permute-done.6.refs_2_.rest_2_
  37.6 12.5 %collective-permute-done.4.refs_0_.rest_0_ = f32[3,5,8,4,256]{4,3,2,1,0:T(4,128)} collective-permute-done((f32[3,5,8,4,256]{4,3,2,1,0:T(4,128)}, f32[3,5,8,4,256]{4,3,2,1,0:T(4,128)}, u32[]{:S(2)}, u32[]{:S(2)}) %collective-permute-start.4) | collective-permute-done | bytes 491552 | tf_op jit(solution)/shard_map/ppermute | solution.py:753
  50.1 1.6 %collective-permute-done.5.refs_1_.rest_1_ = f32[3,5,8,4,256]{4,3,2,1,0:T(4,128)} collective-permute-done((f32[3,5,8,4,256]{4,3,2,1,0:T(4,128)}, f32[3,5,8,4,256]{4,3,2,1,0:T(4,128)}, u32[]{:S(2)}, u32[]{:S(2)}) %collective-permute-start.5) | collective-permute-done | bytes 491552 | tf_op jit(solution)/shard_map/ppermute | solution.py:753
  51.7 0.9 collective-permute-start.11
  52.6 0.0 collective-permute-done.3.refs_8_
  52.6 7.6 %second_half.1 = (f32[5,4,2,2,8,128]{5,4,3,2,1,0:T(8,128)S(1)}, f32[5,4,2,2,8,128]{5,4,3,2,1,0:T(8,128)S(1)}) custom-call(s32[1]{0:T(128)} %bitcast.me_ref.refs_0_, s32[4,8]{1,0:T(4,128)S(1)} %copy-done.4, s32[1,16]{1,0:T(1,128)S(1)} %copy-done.6, s32[2,1,3]{2,1,0:T(1,128)S(1)} %copy-done.5, f32[2,1]{1,0:T(2,128)S(1)} %copy.9.refs_4_, ...), custom_call_target="tpu_custom_call" | custom-call | bytes 8 | tf_op jit(solution)/shard_map/second_half/pallas_call | solution.py:500
  60.2 1.2 %collective-permute-start.12 = (f32[5,4,2,2,8,128]{5,4,3,2,1,0:T(8,128)S(1)}, f32[5,4,2,2,8,128]{5,4,3,2,1,0:T(8,128)S(1)}, u32[]{:S(2)}, u32[]{:S(2)}) collective-permute-start(f32[5,4,2,2,8,128]{5,4,3,2,1,0:T(8,128)S(1)} %get-tuple-element.65), channel_id=1, source_target_pairs={{0,1},{1,0},{2,3},{3,2},{4,5},{5,4},{6,7},{7,6},{8,9},{9,8},{10,11... | collective-permute-start | bytes 983048 | tf_op jit(solution)/shard_map/ppermute | solution.py:753
  61.3 0.7 collective-permute-done.8.rest_3_
  62.1 4.4 %place.1 = (f32[5,4,2,4,8,128]{5,4,3,2,1,0:T(8,128)S(1)}, f32[5,4,2,4,8,128]{5,4,3,2,1,0:T(8,128)S(1)}) custom-call(s32[1]{0:T(128)} %bitcast.me_ref.refs_0_, s32[4,8]{1,0:T(4,128)S(1)} %copy-done.4, f32[3,5,8,4,256]{4,3,2,1,0:T(4,128)} %collective-permute-done.4.refs_0_.rest_0_, f32[3,5,8,4,256]{4,3,2,1,0:T(4,128)} %collective-permute-done.5.refs_1_.rest_1_, ...), custom_call_target="tpu_custom_call" | custom-call | bytes 3 | tf_op jit(solution)/shard_map/place/pallas_call | solution.py:676
  66.4 0.2 collective-permute-start.10
  66.6 0.4 collective-permute-start.9
  67.0 0.0 collective-permute-done.11.arrived_low
  67.0 2.3 %collective-permute-done.12.arrived_high = f32[5,4,2,2,8,128]{5,4,3,2,1,0:T(8,128)S(1)} collective-permute-done((f32[5,4,2,2,8,128]{5,4,3,2,1,0:T(8,128)S(1)}, f32[5,4,2,2,8,128]{5,4,3,2,1,0:T(8,128)S(1)}, u32[]{:S(2)}, u32[]{:S(2)}) %collective-permute-start.12) | collective-permute-done | bytes 327712 | tf_op jit(solution)/shard_map/ppermute | solution.py:753
  69.3 0.8 share.1
  70.1 0.4 collective-permute-start.13
  70.5 2.5 %collective-permute-start.14 = (f32[5,8,2,8,128]{4,3,2,1,0:T(8,128)S(1)}, f32[5,8,2,8,128]{4,3,2,1,0:T(8,128)S(1)}, u32[]{:S(2)}, u32[]{:S(2)}) collective-permute-start(f32[5,8,2,8,128]{4,3,2,1,0:T(8,128)S(1)} %get-tuple-element.70), channel_id=1, source_target_pairs={{0,2},{1,3},{2,0},{3,1},{4,6},{5,7},{6,4},{7,5},{8,10},{9,11},{10,... | collective-permute-start | bytes 983048 | tf_op jit(solution)/shard_map/ppermute | solution.py:753
  73.0 0.6 collective-permute-start.15
  73.7 6.2 %collective-permute-done.10.after = f32[5,4,2,4,8,128]{5,4,3,2,1,0:T(8,128)S(1)} collective-permute-done((f32[5,4,2,4,8,128]{5,4,3,2,1,0:T(8,128)S(1)}, f32[5,4,2,4,8,128]{5,4,3,2,1,0:T(8,128)S(1)}, u32[]{:S(2)}, u32[]{:S(2)}) %collective-permute-start.10) | collective-permute-done | bytes 655392 | tf_op jit(solution)/shard_map/ppermute | solution.py:755
  79.9 3.8 %collective-permute-done.9.before = f32[5,4,2,4,8,128]{5,4,3,2,1,0:T(8,128)S(1)} collective-permute-done((f32[5,4,2,4,8,128]{5,4,3,2,1,0:T(8,128)S(1)}, f32[5,4,2,4,8,128]{5,4,3,2,1,0:T(8,128)S(1)}, u32[]{:S(2)}, u32[]{:S(2)}) %collective-permute-start.9) | collective-permute-done | bytes 655392 | tf_op jit(solution)/shard_map/ppermute | solution.py:754
  83.7 9.0 %recover.1 = f32[5,8,32,256]{3,2,1,0:T(8,128)} custom-call(s32[2,1,3]{2,1,0:T(1,128)S(1)} %copy-done.5, f32[5,4,2,4,8,128]{5,4,3,2,1,0:T(8,128)S(1)} %collective-permute-done.9.before, f32[5,4,2,4,8,128]{5,4,3,2,1,0:T(8,128)S(1)} %get-tuple-element.61.low, f32[5,4,2,4,8,128]{5,4,3,2,1,0:T(8,128)S(1)} %get-tuple-element.60.high, ...), custom_call_target="tpu_custom_call" | custom-call | bytes 10 | tf_op jit(solution)/shard_map/recover/pallas_call | solution.py:725
  92.7 0.0 collective-permute-done.13.rest_1_
  92.7 2.6 %collective-permute-done.14.rest_2_ = f32[5,8,2,8,128]{4,3,2,1,0:T(8,128)S(1)} collective-permute-done((f32[5,8,2,8,128]{4,3,2,1,0:T(8,128)S(1)}, f32[5,8,2,8,128]{4,3,2,1,0:T(8,128)S(1)}, u32[]{:S(2)}, u32[]{:S(2)}) %collective-permute-start.14) | collective-permute-done | bytes 327712 | tf_op jit(solution)/shard_map/ppermute | solution.py:753
  95.3 6.7 %collective-permute-done.15.rest_3_ = f32[5,8,2,8,128]{4,3,2,1,0:T(8,128)S(1)} collective-permute-done((f32[5,8,2,8,128]{4,3,2,1,0:T(8,128)S(1)}, f32[5,8,2,8,128]{4,3,2,1,0:T(8,128)S(1)}, u32[]{:S(2)}, u32[]{:S(2)}) %collective-permute-start.15) | collective-permute-done | bytes 327712 | tf_op jit(solution)/shard_map/ppermute | solution.py:753
  102.0 3.1 %collect.1 = f32[8,5,8,2,256]{4,3,2,1,0:T(2,128)} custom-call(s32[1]{0:T(128)} %bitcast.me_ref.refs_0_, s32[1,16]{1,0:T(1,128)S(1)} %copy-done.6, f32[5,8,2,8,128]{4,3,2,1,0:T(8,128)S(1)} %get-tuple-element.68.rest_0_, f32[5,8,2,8,128]{4,3,2,1,0:T(8,128)S(1)} %collective-permute-done.13.rest_1_, f32[5,8,2,8,128]{4,3,2,1,0:T(8,128)S(1)} %collective-permute-done.14.rest_2_, ...), custom_call_target="tpu_custom_call" | custom-call | bytes 2 | tf_op jit(solution)/shard_map/collect/pallas_call | solution.py:621
  (14 shorter events, 0.0 us)
Async XLA Ops:
  0.6 1.3 %copy-start = (f32[8,5,8,4,256]{4,3,2,1,0:T(4,128)S(1)}, f32[8,5,8,4,256]{4,3,2,1,0:T(4,128)}, u32[]{:S(2)}) copy-start(f32[8,5,8,4,256]{4,3,2,1,0:T(4,128)} %checkpoint.5) | copy-start | bytes 3932164
  1.9 1.3 %copy-start.2 = (f32[1,5,8,32,256]{4,3,2,1,0:T(8,128)S(1)}, f32[1,5,8,32,256]{4,3,2,1,0:T(8,128)}, u32[]{:S(2)}) copy-start(f32[1,5,8,32,256]{4,3,2,1,0:T(8,128)} %param.8) | copy-start | bytes 3932164
  3.3 1.5 %copy-start.5 = (s32[2,1,3]{2,1,0:T(1,128)S(1)}, s32[2,1,3]{2,1,0:T(1,128)}, u32[]{:S(2)}) copy-start(s32[2,1,3]{2,1,0:T(1,128)} %levels_ref.1) | copy-start | bytes 76
  3.3 1.6 %copy-start.7 = (f32[2,1]{0,1:T(1,128)S(1)}, f32[2,1]{0,1:T(1,128)}, u32[]{:S(2)}) copy-start(f32[2,1]{0,1:T(1,128)} %param.10) | copy-start | bytes 28
  3.3 5.1 %copy-start.1 = (f32[8,5,8,4,256]{4,3,2,1,0:T(4,128)S(1)}, f32[8,5,8,4,256]{4,3,2,1,0:T(4,128)}, u32[]{:S(2)}) copy-start(f32[8,5,8,4,256]{4,3,2,1,0:T(4,128)} %checkpoint.5) | copy-start | bytes 3932164
  3.3 5.1 %copy-start.4 = (s32[4,8]{1,0:T(4,128)S(1)}, s32[4,8]{1,0:T(4,128)}, u32[]{:S(2)}) copy-start(s32[4,8]{1,0:T(4,128)} %block_ref.3) | copy-start | bytes 388
  4.7 18.5 %collective-permute-start.7 = (f32[2,5,4,2,4,8,128]{6,5,4,3,2,1,0:T(8,128)S(1)}, f32[2,5,4,2,4,8,128]{6,5,4,3,2,1,0:T(8,128)}, u32[]{:S(2)}, u32[]{:S(2)}) collective-permute-start(f32[2,5,4,2,4,8,128]{6,5,4,3,2,1,0:T(8,128)S(1)} %prepare.3.refs_10_.refs_9_), channel_id=1, source_target_pairs={{0,4},{4,8},{8,12},{12,16},{16,20},{20,24},{24,28},{28,0},{1,5},{5... | collective-permute-start | bytes 3932168 | tf_op jit(solution)/shard_map/ppermute | solution.py:754
  4.9 5.7 %collective-permute-start = (f32[8]{0:T(128)S(1)}, f32[8]{0:T(128)S(1)}, u32[]{:S(2)}, u32[]{:S(2)}) collective-permute-start(f32[8]{0:T(128)S(1)} %pad_maximum_fusion), channel_id=1, source_target_pairs={{0,1},{1,0},{2,3},{3,2},{4,5},{5,4},{6,7},{7,6},{8,9},{9,8},{10,11... | collective-permute-start | bytes 104 | tf_op jit(solution)/shard_map/ppermute | solution.py:753
  5.4 5.3 %collective-permute-start.1 = (f32[8]{0:T(128)S(1)}, f32[8]{0:T(128)S(1)}, u32[]{:S(2)}, u32[]{:S(2)}) collective-permute-start(f32[8]{0:T(128)S(1)} %pad_maximum_fusion), channel_id=1, source_target_pairs={{0,2},{1,3},{2,0},{3,1},{4,6},{5,7},{6,4},{7,5},{8,10},{9,11},{10,... | collective-permute-start | bytes 104 | tf_op jit(solution)/shard_map/ppermute | solution.py:753
  8.0 3.5 %collective-permute-start.2 = (f32[8]{0:T(128)S(1)}, f32[8]{0:T(128)S(1)}, u32[]{:S(2)}, u32[]{:S(2)}) collective-permute-start(f32[8]{0:T(128)S(1)} %pad_maximum_fusion), channel_id=1, source_target_pairs={{0,3},{1,2},{2,1},{3,0},{4,7},{5,6},{6,5},{7,4},{8,11},{9,10},{10,... | collective-permute-start | bytes 104 | tf_op jit(solution)/shard_map/ppermute | solution.py:753
  11.5 26.1 %collective-permute-start.6 = (f32[3,5,8,4,256]{4,3,2,1,0:T(4,128)}, f32[3,5,8,4,256]{4,3,2,1,0:T(4,128)S(1)}, u32[]{:S(2)}, u32[]{:S(2)}) collective-permute-start(f32[3,5,8,4,256]{4,3,2,1,0:T(4,128)} %get-tuple-element.55), channel_id=1, source_target_pairs={{0,3},{3,0},{4,7},{7,4},{8,11},{11,8},{12,15},{15,12},{16,19},{19,... | collective-permute-start | bytes 1474568 | tf_op jit(solution)/shard_map/ppermute | solution.py:768
  12.2 37.9 %collective-permute-start.4 = (f32[3,5,8,4,256]{4,3,2,1,0:T(4,128)}, f32[3,5,8,4,256]{4,3,2,1,0:T(4,128)}, u32[]{:S(2)}, u32[]{:S(2)}) collective-permute-start(f32[3,5,8,4,256]{4,3,2,1,0:T(4,128)} %get-tuple-element.43), channel_id=1, source_target_pairs={{0,1},{1,0},{2,3},{3,2},{4,5},{5,4},{6,7},{7,6},{8,9},{9,8},{10,11... | collective-permute-start | bytes 1474568 | tf_op jit(solution)/shard_map/ppermute | solution.py:753
  17.6 34.1 %collective-permute-start.5 = (f32[3,5,8,4,256]{4,3,2,1,0:T(4,128)}, f32[3,5,8,4,256]{4,3,2,1,0:T(4,128)}, u32[]{:S(2)}, u32[]{:S(2)}) collective-permute-start(f32[3,5,8,4,256]{4,3,2,1,0:T(4,128)} %get-tuple-element.44), channel_id=1, source_target_pairs={{0,2},{1,3},{2,0},{3,1},{4,6},{5,7},{6,4},{7,5},{8,10},{9,11},{10,... | collective-permute-start | bytes 1474568 | tf_op jit(solution)/shard_map/ppermute | solution.py:753
  19.4 1.3 %copy-start.3 = (f32[1,5,8,32,256]{4,3,2,1,0:T(8,128)S(1)}, f32[1,5,8,32,256]{4,3,2,1,0:T(8,128)}, u32[]{:S(2)}) copy-start(f32[1,5,8,32,256]{4,3,2,1,0:T(8,128)} %param.8) | copy-start | bytes 3932164
  20.7 2.4 %copy-start.6 = (s32[1,16]{1,0:T(1,128)S(1)}, s32[1,16]{1,0:T(1,128)}, u32[]{:S(2)}) copy-start(s32[1,16]{1,0:T(1,128)} %owner_ref.3) | copy-start | bytes 196
  23.1 29.5 %collective-permute-start.3 = (f32[2,5,4,2,4,8,128]{6,5,4,3,2,1,0:T(8,128)}, f32[2,5,4,2,4,8,128]{6,5,4,3,2,1,0:T(8,128)}, u32[]{:S(2)}, u32[]{:S(2)}) collective-permute-start(f32[2,5,4,2,4,8,128]{6,5,4,3,2,1,0:T(8,128)} %prepare.2.refs_9_), channel_id=1, source_target_pairs={{4,0},{8,4},{12,8},{16,12},{20,16},{24,20},{28,24},{0,28},{5,1},{9... | collective-permute-start | bytes 3932168 | tf_op jit(solution)/shard_map/ppermute | solution.py:755
  35.1 26.9 %collective-permute-start.8 = (f32[3,5,8,4,256]{4,3,2,1,0:T(4,128)}, f32[3,5,8,4,256]{4,3,2,1,0:T(4,128)}, u32[]{:S(2)}, u32[]{:S(2)}) collective-permute-start(f32[3,5,8,4,256]{4,3,2,1,0:T(4,128)} %get-tuple-element.55), channel_id=1, source_target_pairs={{1,2},{2,1},{5,6},{6,5},{9,10},{10,9},{13,14},{14,13},{17,18},{18,... | collective-permute-start | bytes 1474568 | tf_op jit(solution)/shard_map/ppermute | solution.py:775
  51.7 15.3 %collective-permute-start.11 = (f32[5,4,2,2,8,128]{5,4,3,2,1,0:T(8,128)S(1)}, f32[5,4,2,2,8,128]{5,4,3,2,1,0:T(8,128)S(1)}, u32[]{:S(2)}, u32[]{:S(2)}) collective-permute-start(f32[5,4,2,2,8,128]{5,4,3,2,1,0:T(8,128)S(1)} %get-tuple-element.63), channel_id=1, source_target_pairs={{0,1},{1,0},{2,3},{3,2},{4,5},{5,4},{6,7},{7,6},{8,9},{9,8},{10,11... | collective-permute-start | bytes 983048 | tf_op jit(solution)/shard_map/ppermute | solution.py:753
  60.2 9.1 %collective-permute-start.12 = (f32[5,4,2,2,8,128]{5,4,3,2,1,0:T(8,128)S(1)}, f32[5,4,2,2,8,128]{5,4,3,2,1,0:T(8,128)S(1)}, u32[]{:S(2)}, u32[]{:S(2)}) collective-permute-start(f32[5,4,2,2,8,128]{5,4,3,2,1,0:T(8,128)S(1)} %get-tuple-element.65), channel_id=1, source_target_pairs={{0,1},{1,0},{2,3},{3,2},{4,5},{5,4},{6,7},{7,6},{8,9},{9,8},{10,11... | collective-permute-start | bytes 983048 | tf_op jit(solution)/shard_map/ppermute | solution.py:753
  66.4 13.5 %collective-permute-start.10 = (f32[5,4,2,4,8,128]{5,4,3,2,1,0:T(8,128)S(1)}, f32[5,4,2,4,8,128]{5,4,3,2,1,0:T(8,128)S(1)}, u32[]{:S(2)}, u32[]{:S(2)}) collective-permute-start(f32[5,4,2,4,8,128]{5,4,3,2,1,0:T(8,128)S(1)} %get-tuple-element.61.low), channel_id=1, source_target_pairs={{4,0},{8,4},{12,8},{16,12},{20,16},{24,20},{28,24},{0,28},{5,1},{9... | collective-permute-start | bytes 1966088 | tf_op jit(solution)/shard_map/ppermute | solution.py:755
  66.6 17.0 %collective-permute-start.9 = (f32[5,4,2,4,8,128]{5,4,3,2,1,0:T(8,128)S(1)}, f32[5,4,2,4,8,128]{5,4,3,2,1,0:T(8,128)S(1)}, u32[]{:S(2)}, u32[]{:S(2)}) collective-permute-start(f32[5,4,2,4,8,128]{5,4,3,2,1,0:T(8,128)S(1)} %get-tuple-element.60.high), channel_id=1, source_target_pairs={{0,4},{4,8},{8,12},{12,16},{16,20},{20,24},{24,28},{28,0},{1,5},{5... | collective-permute-start | bytes 1966088 | tf_op jit(solution)/shard_map/ppermute | solution.py:754
  70.1 22.5 %collective-permute-start.13 = (f32[5,8,2,8,128]{4,3,2,1,0:T(8,128)S(1)}, f32[5,8,2,8,128]{4,3,2,1,0:T(8,128)S(1)}, u32[]{:S(2)}, u32[]{:S(2)}) collective-permute-start(f32[5,8,2,8,128]{4,3,2,1,0:T(8,128)S(1)} %get-tuple-element.69), channel_id=1, source_target_pairs={{0,1},{1,0},{2,3},{3,2},{4,5},{5,4},{6,7},{7,6},{8,9},{9,8},{10,11... | collective-permute-start | bytes 983048 | tf_op jit(solution)/shard_map/ppermute | solution.py:753
  70.5 24.7 %collective-permute-start.14 = (f32[5,8,2,8,128]{4,3,2,1,0:T(8,128)S(1)}, f32[5,8,2,8,128]{4,3,2,1,0:T(8,128)S(1)}, u32[]{:S(2)}, u32[]{:S(2)}) collective-permute-start(f32[5,8,2,8,128]{4,3,2,1,0:T(8,128)S(1)} %get-tuple-element.70), channel_id=1, source_target_pairs={{0,2},{1,3},{2,0},{3,1},{4,6},{5,7},{6,4},{7,5},{8,10},{9,11},{10,... | collective-permute-start | bytes 983048 | tf_op jit(solution)/shard_map/ppermute | solution.py:753
  73.0 28.9 %collective-permute-start.15 = (f32[5,8,2,8,128]{4,3,2,1,0:T(8,128)S(1)}, f32[5,8,2,8,128]{4,3,2,1,0:T(8,128)S(1)}, u32[]{:S(2)}, u32[]{:S(2)}) collective-permute-start(f32[5,8,2,8,128]{4,3,2,1,0:T(8,128)S(1)} %get-tuple-element.71), channel_id=1, source_target_pairs={{0,3},{1,2},{2,1},{3,0},{4,7},{5,6},{6,5},{7,4},{8,11},{9,10},{10,... | collective-permute-start | bytes 983048 | tf_op jit(solution)/shard_map/ppermute | solution.py:753

commit v3 on v2

--- a/solution.py
+++ b/solution.py
@@ -574,6 +574,7 @@
 
 def collect_kernel(groups, tile_most, me_ref, owner_ref, *rest):
     pieces, (result, out, sems, matrix, *counts) = rest[:groups], rest[groups:]
+    pieces = (pieces[0], *pieces[:0:-1])
     count_tiles(owner_ref, groups, *counts)
     one_hot(matrix, True)
     me = me_ref[0]
@@ -628,7 +629,7 @@
         compiler_params=params(8),
         cost_estimate=cost(2),
         name="collect",
-    )(me, owner, *pieces)
+    )(me, owner, pieces[0], *pieces[:0:-1])
 
 
 def place_kernel(others, me_ref, block_ref, *rest):
@@ -650,22 +651,26 @@
                 mine = mine & (inner if number == groups - 1 else jnp.logical_not(inner))
             table[number, jnp.where(mine, rank, HELD_MOST)] = block % slots
             rank = rank + mine.astype(jnp.int32)
+    for number in range(others):
+        for slot in range(HELD_MOST):
+            block = table[number, slot]
+
+            @pl.when(block >= 0)
+            def _(number=number, slot=slot, block=block):
+                def copy(z, carry):
+                    for field in range(5):
+                        for side in (0, 1):
+                            lines[z, field, side, pl.ds(block, 4, stride=ROWS), :] = pieces[number][
+                                slot, field, z, :, pl.ds(side * LANES, LANES)
+                            ]
+                    return carry
+
+                lax.fori_loop(0, 2 * DEPTH, copy, 0)
+
     for half, out in ((0, low), (1, high)):
 
         def layer(z, carry, half=half, out=out):
-            for number in range(others):
-                for slot in range(HELD_MOST):
-                    block = table[number, slot]
-
-                    @pl.when(block >= 0)
-                    def _(number=number, slot=slot, block=block):
-                        for field in range(5):
-                            for side in (0, 1):
-                                lines[field, side, pl.ds(block, 4, stride=ROWS), :] = pieces[number][
-                                    slot, field, half * DEPTH + z, :, pl.ds(side * LANES, LANES)
-                                ]
-
-            store_lines(lines, matrix, out, z)
+            store_lines(lines.at[half * DEPTH + z], matrix, out, z)
             return carry
 
         lax.fori_loop(0, DEPTH, layer, 0)
@@ -679,11 +684,11 @@
         in_specs=[spec_smem()] * 2 + [spec_vmem()] * len(pieces),
         out_specs=[spec_vmem()] * 2,
         scratch_shapes=[
-            pltpu.VMEM((5, 2, 4 * ROWS, LANES), jnp.float32),
+            pltpu.VMEM((2 * DEPTH, 5, 2, 4 * ROWS, LANES), jnp.float32),
             one_hot_scratch(),
             pltpu.SMEM((len(pieces), HELD_MOST + 1), jnp.int32),
         ],
-        compiler_params=params(8),
+        compiler_params=params(12),
         cost_estimate=cost(3),
         name="place",
     )(me, slot_block, *pieces)
@@ -773,7 +778,7 @@
     send_low, late, carries[0] = after_all(send_low, sent[-1], carries[0])
     arrived_low = trade(send_low, 1)
     received.append(lax.ppermute(late, "buddy", [middle, middle[::-1]]))
-    send_high, keep_high = half_step(second_half_kernel, scalars, (after, high, there(received[:-1])), carries, 2 * DEPTH, True)
+    send_high, keep_high = half_step(second_half_kernel, scalars, (after, high, there(received[:1])), carries, 2 * DEPTH, True)
     arrived_high = trade(send_high, 1)
 
     keep_high, received = after_all(keep_high, received)

time: 105 us -> 103 us (0.981)
  the two profiles are of different devices: /device:TPU:10 before, /device:TPU:0 now
where the time goes in v3:
time: 103 us
  Pallas kernels  42.5 us (41%)
  waiting for transfers between devices  29.8 us (29%)
  starting transfers between devices  25.3 us (25%)
  local copies, waits for them, and re-layouts  4.14 us (4%)
    ppermute x10, waiting for transfers between devices, body(): lax.ppermute(array, 'buddy', [(i, i ^ d) for i in range(groups)])  26 us
    pallas_call x2, Pallas kernels, half_step(): pl.pallas_call(functools.partial(kernel, others), out_shape=outs, in_spec...  19.5 us
    ppermute x10, starting transfers between devices, body(): lax.ppermute(array, 'buddy', [(i, i ^ d) for i in range(groups)])  18.3 us
    pallas_call x1, Pallas kernels, recover(): pl.pallas_call(recover_kernel, out_shape=shape(5, 2 * DEPTH, 4 * ROWS, 2...  9 us
    unnamed x17, local copies, waits for them, and re-layouts  4.05 us
    pallas_call x1, Pallas kernels, place(): pl.pallas_call(functools.partial(place_kernel, len(pieces)), out_shape=[h...  4.02 us
    pallas_call x2, Pallas kernels, prepare(): pl.pallas_call(functools.partial(prepare_kernel, half, len(firsts)), out_...  3.8 us
    ppermute x1, starting transfers between devices, body(): lax.ppermute(sent[-1], 'buddy', [(i, i ^ groups - 1) for i in range(group...  3.57 us
  transfers between devices with their start and end apart: 16, of which 7 were waited for; matrix products, arithmetic and copies ran while one was open for 0% of the time, Pallas kernels for 37%

profile of v3, /device:TPU:0, one launch (start us, length us, event | category | flops | bytes accessed | tf_op | source)
XLA Modules:
  0.0 102.6 jit_solution(3079159996169548583)
XLA Ops:
  0.6 0.0 copy-start
  0.6 1.3 %copy-done = f32[8,5,8,4,256]{4,3,2,1,0:T(4,128)S(1)} copy-done((f32[8,5,8,4,256]{4,3,2,1,0:T(4,128)S(1)}, f32[8,5,8,4,256]{4,3,2,1,0:T(4,128)}, u32[]{:S(2)}) %copy-start) | copy-done | bytes 1310744
  1.9 1.3 %copy-done.2 = f32[1,5,8,32,256]{4,3,2,1,0:T(8,128)S(1)} copy-done((f32[1,5,8,32,256]{4,3,2,1,0:T(8,128)S(1)}, f32[1,5,8,32,256]{4,3,2,1,0:T(8,128)}, u32[]{:S(2)}) %copy-start.2) | copy-done | bytes 1310744
  3.3 1.4 %prepare.3.refs_10_.refs_9_ = f32[2,5,4,2,4,8,128]{6,5,4,3,2,1,0:T(8,128)S(1)} custom-call(f32[8,5,8,4,256]{4,3,2,1,0:T(4,128)S(1)} %copy-done, f32[5,8,32,256]{3,2,1,0:T(8,128)S(1)} %bitcast.4), custom_call_target="tpu_custom_call" | custom-call | bytes 1 | tf_op jit(solution)/shard_map/prepare/pallas_call | solution.py:367
  4.7 0.5 collective-permute-start.5
  5.2 0.1 reshape.14
  5.3 0.1 pad_maximum_fusion
  5.3 2.6 %collective-permute-start = (f32[8]{0:T(128)S(1)}, f32[8]{0:T(128)S(1)}, u32[]{:S(2)}, u32[]{:S(2)}) collective-permute-start(f32[8]{0:T(128)S(1)} %pad_maximum_fusion), channel_id=1, source_target_pairs={{0,1},{1,0},{2,3},{3,2},{4,5},{5,4},{6,7},{7,6},{8,9},{9,8},{10,11... | collective-permute-start | bytes 104 | tf_op jit(solution)/shard_map/ppermute | solution.py:758
  7.9 2.6 %collective-permute-start.1 = (f32[8]{0:T(128)S(1)}, f32[8]{0:T(128)S(1)}, u32[]{:S(2)}, u32[]{:S(2)}) collective-permute-start(f32[8]{0:T(128)S(1)} %pad_maximum_fusion), channel_id=1, source_target_pairs={{0,2},{1,3},{2,0},{3,1},{4,6},{5,7},{6,4},{7,5},{8,10},{9,11},{10,... | collective-permute-start | bytes 104 | tf_op jit(solution)/shard_map/ppermute | solution.py:758
  10.5 0.0 collective-permute-start.2
  10.5 2.2 %gather_slots.1 = (f32[3,5,8,4,256]{4,3,2,1,0:T(4,128)}, f32[3,5,8,4,256]{4,3,2,1,0:T(4,128)}, f32[3,5,8,4,256]{4,3,2,1,0:T(4,128)}) custom-call(s32[1]{0:T(128)} %bitcast.me_ref.refs_0_, s32[4,8]{1,0:T(4,128)S(1)} %copy-done.4, f32[8,5,8,4,256]{4,3,2,1,0:T(4,128)S(1)} %copy-done.1), custom_call_target="tpu_custom_call" | custom-call | bytes 1 | tf_op jit(solution)/shard_map/gather_slots/pallas_call | solution.py:318
  12.8 0.0 collective-permute-done.refs_0_.refs_5_
  12.8 0.0 collective-permute-done.1.refs_1_.refs_6_
  12.8 3.1 %collective-permute-done.2.refs_2_.refs_7_ = f32[8]{0:T(128)S(1)} collective-permute-done((f32[8]{0:T(128)S(1)}, f32[8]{0:T(128)S(1)}, u32[]{:S(2)}, u32[]{:S(2)}) %collective-permute-start.2) | collective-permute-done | bytes 64 | tf_op jit(solution)/shard_map/ppermute | solution.py:758
  15.9 0.0 collective-permute-start.4
  15.9 0.1 copy.9.refs_4_
  16.0 1.3 %copy-done.3 = f32[1,5,8,32,256]{4,3,2,1,0:T(8,128)S(1)} copy-done((f32[1,5,8,32,256]{4,3,2,1,0:T(8,128)S(1)}, f32[1,5,8,32,256]{4,3,2,1,0:T(8,128)}, u32[]{:S(2)}) %copy-start.3) | copy-done | bytes 1310744
  17.3 2.4 %prepare.2.refs_9_ = f32[2,5,4,2,4,8,128]{6,5,4,3,2,1,0:T(8,128)} custom-call(f32[8,5,8,4,256]{4,3,2,1,0:T(4,128)S(1)} %copy-done.1, f32[5,8,32,256]{3,2,1,0:T(8,128)S(1)} %bitcast.5, f32[8]{0:T(128)S(1)} %collective-permute-done.refs_0_.refs_5_, f32[8]{0:T(128)S(1)} %collective-permute-done.1.refs_1_.refs_6_, f32[8]{0:T(128)S(1)} %collective-permute-done.2.refs_2_.refs_7_), custom_call_target="tpu_custom_call" | custom-call | bytes 1 | tf_op jit(solution)/shard_map/prepare/pallas_call | solution.py:367
  19.7 0.9 collective-permute-start.3
  20.6 3.6 %collective-permute-start.7 = (f32[3,5,8,4,256]{4,3,2,1,0:T(4,128)}, f32[3,5,8,4,256]{4,3,2,1,0:T(4,128)}, u32[]{:S(2)}, u32[]{:S(2)}) collective-permute-start(f32[3,5,8,4,256]{4,3,2,1,0:T(4,128)} %get-tuple-element.55), channel_id=1, source_target_pairs={{0,3},{3,0},{4,7},{7,4},{8,11},{11,8},{12,15},{15,12},{16,19},{19,... | collective-permute-start | bytes 1474568 | tf_op jit(solution)/shard_map/ppermute | solution.py:773
  24.2 0.1 collective-permute-start.6
  24.3 0.0 collective-permute-done.5.refs_8_
  24.3 12.0 %first_half.1 = (f32[5,4,2,2,8,128]{5,4,3,2,1,0:T(8,128)S(1)}, f32[5,4,2,2,8,128]{5,4,3,2,1,0:T(8,128)S(1)}, f32[5,2,2,6,8,128]{5,4,3,2,1,0:T(8,128)S(1)}, f32[5...) custom-call(s32[1]{0:T(128)} %bitcast.me_ref.refs_0_, ...), custom_call_target="tpu_custom_call" | custom-call | bytes 12 | tf_op jit(solution)/shard_map/first_half/pallas_call | solution.py:500
  36.3 1.5 %collective-permute-start.8 = (f32[3,5,8,4,256]{4,3,2,1,0:T(4,128)}, f32[3,5,8,4,256]{4,3,2,1,0:T(4,128)}, u32[]{:S(2)}, u32[]{:S(2)}) collective-permute-start(f32[3,5,8,4,256]{4,3,2,1,0:T(4,128)} %get-tuple-element.55), channel_id=1, source_target_pairs={{1,2},{2,1},{5,6},{6,5},{9,10},{10,9},{13,14},{14,13},{17,18},{18,... | collective-permute-start | bytes 1474568 | tf_op jit(solution)/shard_map/ppermute | solution.py:780
  37.7 4.2 %collective-permute-done.4.refs_0_.rest_0_ = f32[3,5,8,4,256]{4,3,2,1,0:T(4,128)S(1)} collective-permute-done((f32[3,5,8,4,256]{4,3,2,1,0:T(4,128)}, f32[3,5,8,4,256]{4,3,2,1,0:T(4,128)S(1)}, u32[]{:S(2)}, u32[]{:S(2)}) %collective-permute-start.4) | collective-permute-done | bytes 491552 | tf_op jit(solution)/shard_map/ppermute | solution.py:758
  42.0 0.1 collective-permute-start.11
  42.0 0.0 collective-permute-done.3.refs_8_
  42.0 7.6 %second_half.1 = (f32[5,4,2,2,8,128]{5,4,3,2,1,0:T(8,128)S(1)}, f32[5,4,2,2,8,128]{5,4,3,2,1,0:T(8,128)S(1)}) custom-call(s32[1]{0:T(128)} %bitcast.me_ref.refs_0_, s32[4,8]{1,0:T(4,128)S(1)} %copy-done.4, s32[1,16]{1,0:T(1,128)S(1)} %copy-done.6, s32[2,1,3]{2,1,0:T(1,128)S(1)} %copy-done.5, f32[2,1]{1,0:T(2,128)S(1)} %copy.9.refs_4_, ...), custom_call_target="tpu_custom_call" | custom-call | bytes 8 | tf_op jit(solution)/shard_map/second_half/pallas_call | solution.py:500
  49.6 2.0 %collective-permute-start.12 = (f32[5,4,2,2,8,128]{5,4,3,2,1,0:T(8,128)S(1)}, f32[5,4,2,2,8,128]{5,4,3,2,1,0:T(8,128)S(1)}, u32[]{:S(2)}, u32[]{:S(2)}) collective-permute-start(f32[5,4,2,2,8,128]{5,4,3,2,1,0:T(8,128)S(1)} %get-tuple-element.65), channel_id=1, source_target_pairs={{0,1},{1,0},{2,3},{3,2},{4,5},{5,4},{6,7},{7,6},{8,9},{9,8},{10,11... | collective-permute-start | bytes 983048 | tf_op jit(solution)/shard_map/ppermute | solution.py:758
  51.6 0.0 collective-permute-done.7.rest_2_
  51.6 9.1 %collective-permute-done.6.rest_1_ = f32[3,5,8,4,256]{4,3,2,1,0:T(4,128)} collective-permute-done((f32[3,5,8,4,256]{4,3,2,1,0:T(4,128)}, f32[3,5,8,4,256]{4,3,2,1,0:T(4,128)}, u32[]{:S(2)}, u32[]{:S(2)}) %collective-permute-start.6) | collective-permute-done | bytes 491552 | tf_op jit(solution)/shard_map/ppermute | solution.py:758
  60.7 0.0 collective-permute-done.8.rest_3_
  60.7 4.0 %place.1 = (f32[5,4,2,4,8,128]{5,4,3,2,1,0:T(8,128)S(1)}, f32[5,4,2,4,8,128]{5,4,3,2,1,0:T(8,128)S(1)}) custom-call(s32[1]{0:T(128)} %bitcast.me_ref.refs_0_, s32[4,8]{1,0:T(4,128)S(1)} %copy-done.4, f32[3,5,8,4,256]{4,3,2,1,0:T(4,128)S(1)} %collective-permute-done.4.refs_0_.rest_0_, f32[3,5,8,4,256]{4,3,2,1,0:T(4,128)} %collective-permute-done.6.rest_1_, ...), custom_call_target="tpu_custom_call" | custom-call | bytes 3 | tf_op jit(solution)/shard_map/place/pallas_call | solution.py:681
  64.8 0.1 collective-permute-start.10
  64.8 0.5 collective-permute-start.9
  65.3 0.0 collective-permute-done.11.arrived_low
  65.3 0.6 collective-permute-done.12.arrived_high
  65.9 0.8 share.1
  66.8 2.6 %collective-permute-start.13 = (f32[5,8,2,8,128]{4,3,2,1,0:T(8,128)S(1)}, f32[5,8,2,8,128]{4,3,2,1,0:T(8,128)S(1)}, u32[]{:S(2)}, u32[]{:S(2)}) collective-permute-start(f32[5,8,2,8,128]{4,3,2,1,0:T(8,128)S(1)} %get-tuple-element.69), channel_id=1, source_target_pairs={{0,3},{1,2},{2,1},{3,0},{4,7},{5,6},{6,5},{7,4},{8,11},{9,10},{10,... | collective-permute-start | bytes 983048 | tf_op jit(solution)/shard_map/ppermute | solution.py:758
  69.4 7.8 %collective-permute-start.14 = (f32[5,8,2,8,128]{4,3,2,1,0:T(8,128)S(1)}, f32[5,8,2,8,128]{4,3,2,1,0:T(8,128)S(1)}, u32[]{:S(2)}, u32[]{:S(2)}) collective-permute-start(f32[5,8,2,8,128]{4,3,2,1,0:T(8,128)S(1)} %get-tuple-element.70), channel_id=1, source_target_pairs={{0,2},{1,3},{2,0},{3,1},{4,6},{5,7},{6,4},{7,5},{8,10},{9,11},{10,... | collective-permute-start | bytes 983048 | tf_op jit(solution)/shard_map/ppermute | solution.py:758
  77.2 0.5 collective-permute-start.15
  77.7 2.2 %collective-permute-done.10.after = f32[5,4,2,4,8,128]{5,4,3,2,1,0:T(8,128)S(1)} collective-permute-done((f32[5,4,2,4,8,128]{5,4,3,2,1,0:T(8,128)S(1)}, f32[5,4,2,4,8,128]{5,4,3,2,1,0:T(8,128)S(1)}, u32[]{:S(2)}, u32[]{:S(2)}) %collective-permute-start.10) | collective-permute-done | bytes 655392 | tf_op jit(solution)/shard_map/ppermute | solution.py:760
  79.9 1.6 %collective-permute-done.9.before = f32[5,4,2,4,8,128]{5,4,3,2,1,0:T(8,128)S(1)} collective-permute-done((f32[5,4,2,4,8,128]{5,4,3,2,1,0:T(8,128)S(1)}, f32[5,4,2,4,8,128]{5,4,3,2,1,0:T(8,128)S(1)}, u32[]{:S(2)}, u32[]{:S(2)}) %collective-permute-start.9) | collective-permute-done | bytes 655392 | tf_op jit(solution)/shard_map/ppermute | solution.py:759
  81.5 9.0 %recover.1 = f32[5,8,32,256]{3,2,1,0:T(8,128)} custom-call(s32[2,1,3]{2,1,0:T(1,128)S(1)} %copy-done.5, f32[5,4,2,4,8,128]{5,4,3,2,1,0:T(8,128)S(1)} %collective-permute-done.9.before, f32[5,4,2,4,8,128]{5,4,3,2,1,0:T(8,128)S(1)} %get-tuple-element.61.low, f32[5,4,2,4,8,128]{5,4,3,2,1,0:T(8,128)S(1)} %get-tuple-element.60.high, ...), custom_call_target="tpu_custom_call" | custom-call | bytes 10 | tf_op jit(solution)/shard_map/recover/pallas_call | solution.py:730
  90.5 0.0 collective-permute-done.13.rest_1_
  90.5 9.0 %collective-permute-done.14.rest_2_ = f32[5,8,2,8,128]{4,3,2,1,0:T(8,128)S(1)} collective-permute-done((f32[5,8,2,8,128]{4,3,2,1,0:T(8,128)S(1)}, f32[5,8,2,8,128]{4,3,2,1,0:T(8,128)S(1)}, u32[]{:S(2)}, u32[]{:S(2)}) %collective-permute-start.14) | collective-permute-done | bytes 327712 | tf_op jit(solution)/shard_map/ppermute | solution.py:758
  99.5 0.0 collective-permute-done.15.rest_3_
  99.5 3.1 %collect.1 = f32[8,5,8,2,256]{4,3,2,1,0:T(2,128)} custom-call(s32[1]{0:T(128)} %bitcast.me_ref.refs_0_, s32[1,16]{1,0:T(1,128)S(1)} %copy-done.6, f32[5,8,2,8,128]{4,3,2,1,0:T(8,128)S(1)} %get-tuple-element.68.rest_0_, f32[5,8,2,8,128]{4,3,2,1,0:T(8,128)S(1)} %collective-permute-done.13.rest_1_, f32[5,8,2,8,128]{4,3,2,1,0:T(8,128)S(1)} %collective-permute-done.14.rest_2_, ...), custom_call_target="tpu_custom_call" | custom-call | bytes 2 | tf_op jit(solution)/shard_map/collect/pallas_call | solution.py:622
  (14 shorter events, 0.0 us)
Async XLA Ops:
  0.6 1.3 %copy-start = (f32[8,5,8,4,256]{4,3,2,1,0:T(4,128)S(1)}, f32[8,5,8,4,256]{4,3,2,1,0:T(4,128)}, u32[]{:S(2)}) copy-start(f32[8,5,8,4,256]{4,3,2,1,0:T(4,128)} %checkpoint.5) | copy-start | bytes 3932164
  1.9 1.3 %copy-start.2 = (f32[1,5,8,32,256]{4,3,2,1,0:T(8,128)S(1)}, f32[1,5,8,32,256]{4,3,2,1,0:T(8,128)}, u32[]{:S(2)}) copy-start(f32[1,5,8,32,256]{4,3,2,1,0:T(8,128)} %param.8) | copy-start | bytes 3932164
  3.3 1.9 %copy-start.5 = (s32[2,1,3]{2,1,0:T(1,128)S(1)}, s32[2,1,3]{2,1,0:T(1,128)}, u32[]{:S(2)}) copy-start(s32[2,1,3]{2,1,0:T(1,128)} %levels_ref.1) | copy-start | bytes 76
  3.3 2.0 %copy-start.7 = (f32[2,1]{0,1:T(1,128)S(1)}, f32[2,1]{0,1:T(1,128)}, u32[]{:S(2)}) copy-start(f32[2,1]{0,1:T(1,128)} %param.10) | copy-start | bytes 28
  3.3 7.3 %copy-start.1 = (f32[8,5,8,4,256]{4,3,2,1,0:T(4,128)S(1)}, f32[8,5,8,4,256]{4,3,2,1,0:T(4,128)}, u32[]{:S(2)}) copy-start(f32[8,5,8,4,256]{4,3,2,1,0:T(4,128)} %checkpoint.5) | copy-start | bytes 3932164
  3.3 7.3 %copy-start.4 = (s32[4,8]{1,0:T(4,128)S(1)}, s32[4,8]{1,0:T(4,128)}, u32[]{:S(2)}) copy-start(s32[4,8]{1,0:T(4,128)} %block_ref.3) | copy-start | bytes 388
  4.7 19.6 %collective-permute-start.5 = (f32[2,5,4,2,4,8,128]{6,5,4,3,2,1,0:T(8,128)S(1)}, f32[2,5,4,2,4,8,128]{6,5,4,3,2,1,0:T(8,128)}, u32[]{:S(2)}, u32[]{:S(2)}) collective-permute-start(f32[2,5,4,2,4,8,128]{6,5,4,3,2,1,0:T(8,128)S(1)} %prepare.3.refs_10_.refs_9_), channel_id=1, source_target_pairs={{0,4},{4,8},{8,12},{12,16},{16,20},{20,24},{24,28},{28,0},{1,5},{5... | collective-permute-start | bytes 3932168 | tf_op jit(solution)/shard_map/ppermute | solution.py:759
  5.3 7.4 %collective-permute-start = (f32[8]{0:T(128)S(1)}, f32[8]{0:T(128)S(1)}, u32[]{:S(2)}, u32[]{:S(2)}) collective-permute-start(f32[8]{0:T(128)S(1)} %pad_maximum_fusion), channel_id=1, source_target_pairs={{0,1},{1,0},{2,3},{3,2},{4,5},{5,4},{6,7},{7,6},{8,9},{9,8},{10,11... | collective-permute-start | bytes 104 | tf_op jit(solution)/shard_map/ppermute | solution.py:758
  7.9 4.8 %collective-permute-start.1 = (f32[8]{0:T(128)S(1)}, f32[8]{0:T(128)S(1)}, u32[]{:S(2)}, u32[]{:S(2)}) collective-permute-start(f32[8]{0:T(128)S(1)} %pad_maximum_fusion), channel_id=1, source_target_pairs={{0,2},{1,3},{2,0},{3,1},{4,6},{5,7},{6,4},{7,5},{8,10},{9,11},{10,... | collective-permute-start | bytes 104 | tf_op jit(solution)/shard_map/ppermute | solution.py:758
  10.5 5.3 %collective-permute-start.2 = (f32[8]{0:T(128)S(1)}, f32[8]{0:T(128)S(1)}, u32[]{:S(2)}, u32[]{:S(2)}) collective-permute-start(f32[8]{0:T(128)S(1)} %pad_maximum_fusion), channel_id=1, source_target_pairs={{0,3},{1,2},{2,1},{3,0},{4,7},{5,6},{6,5},{7,4},{8,11},{9,10},{10,... | collective-permute-start | bytes 104 | tf_op jit(solution)/shard_map/ppermute | solution.py:758
  15.9 26.1 %collective-permute-start.4 = (f32[3,5,8,4,256]{4,3,2,1,0:T(4,128)}, f32[3,5,8,4,256]{4,3,2,1,0:T(4,128)S(1)}, u32[]{:S(2)}, u32[]{:S(2)}) collective-permute-start(f32[3,5,8,4,256]{4,3,2,1,0:T(4,128)} %get-tuple-element.43), channel_id=1, source_target_pairs={{0,1},{1,0},{2,3},{3,2},{4,5},{5,4},{6,7},{7,6},{8,9},{9,8},{10,11... | collective-permute-start | bytes 1474568 | tf_op jit(solution)/shard_map/ppermute | solution.py:758
  16.0 1.3 %copy-start.3 = (f32[1,5,8,32,256]{4,3,2,1,0:T(8,128)S(1)}, f32[1,5,8,32,256]{4,3,2,1,0:T(8,128)}, u32[]{:S(2)}) copy-start(f32[1,5,8,32,256]{4,3,2,1,0:T(8,128)} %param.8) | copy-start | bytes 3932164
  17.3 7.0 %copy-start.6 = (s32[1,16]{1,0:T(1,128)S(1)}, s32[1,16]{1,0:T(1,128)}, u32[]{:S(2)}) copy-start(s32[1,16]{1,0:T(1,128)} %owner_ref.3) | copy-start | bytes 196
  19.7 22.3 %collective-permute-start.3 = (f32[2,5,4,2,4,8,128]{6,5,4,3,2,1,0:T(8,128)}, f32[2,5,4,2,4,8,128]{6,5,4,3,2,1,0:T(8,128)}, u32[]{:S(2)}, u32[]{:S(2)}) collective-permute-start(f32[2,5,4,2,4,8,128]{6,5,4,3,2,1,0:T(8,128)} %prepare.2.refs_9_), channel_id=1, source_target_pairs={{4,0},{8,4},{12,8},{16,12},{20,16},{24,20},{28,24},{0,28},{5,1},{9... | collective-permute-start | bytes 3932168 | tf_op jit(solution)/shard_map/ppermute | solution.py:760
  20.6 31.0 %collective-permute-start.7 = (f32[3,5,8,4,256]{4,3,2,1,0:T(4,128)}, f32[3,5,8,4,256]{4,3,2,1,0:T(4,128)}, u32[]{:S(2)}, u32[]{:S(2)}) collective-permute-start(f32[3,5,8,4,256]{4,3,2,1,0:T(4,128)} %get-tuple-element.55), channel_id=1, source_target_pairs={{0,3},{3,0},{4,7},{7,4},{8,11},{11,8},{12,15},{15,12},{16,19},{19,... | collective-permute-start | bytes 1474568 | tf_op jit(solution)/shard_map/ppermute | solution.py:773
  24.2 36.5 %collective-permute-start.6 = (f32[3,5,8,4,256]{4,3,2,1,0:T(4,128)}, f32[3,5,8,4,256]{4,3,2,1,0:T(4,128)}, u32[]{:S(2)}, u32[]{:S(2)}) collective-permute-start(f32[3,5,8,4,256]{4,3,2,1,0:T(4,128)} %get-tuple-element.54), channel_id=1, source_target_pairs={{0,2},{1,3},{2,0},{3,1},{4,6},{5,7},{6,4},{7,5},{8,10},{9,11},{10,... | collective-permute-start | bytes 1474568 | tf_op jit(solution)/shard_map/ppermute | solution.py:758
  36.3 24.5 %collective-permute-start.8 = (f32[3,5,8,4,256]{4,3,2,1,0:T(4,128)}, f32[3,5,8,4,256]{4,3,2,1,0:T(4,128)}, u32[]{:S(2)}, u32[]{:S(2)}) collective-permute-start(f32[3,5,8,4,256]{4,3,2,1,0:T(4,128)} %get-tuple-element.55), channel_id=1, source_target_pairs={{1,2},{2,1},{5,6},{6,5},{9,10},{10,9},{13,14},{14,13},{17,18},{18,... | collective-permute-start | bytes 1474568 | tf_op jit(solution)/shard_map/ppermute | solution.py:780
  42.0 23.4 %collective-permute-start.11 = (f32[5,4,2,2,8,128]{5,4,3,2,1,0:T(8,128)S(1)}, f32[5,4,2,2,8,128]{5,4,3,2,1,0:T(8,128)S(1)}, u32[]{:S(2)}, u32[]{:S(2)}) collective-permute-start(f32[5,4,2,2,8,128]{5,4,3,2,1,0:T(8,128)S(1)} %get-tuple-element.63), channel_id=1, source_target_pairs={{0,1},{1,0},{2,3},{3,2},{4,5},{5,4},{6,7},{7,6},{8,9},{9,8},{10,11... | collective-permute-start | bytes 983048 | tf_op jit(solution)/shard_map/ppermute | solution.py:758
  49.6 16.3 %collective-permute-start.12 = (f32[5,4,2,2,8,128]{5,4,3,2,1,0:T(8,128)S(1)}, f32[5,4,2,2,8,128]{5,4,3,2,1,0:T(8,128)S(1)}, u32[]{:S(2)}, u32[]{:S(2)}) collective-permute-start(f32[5,4,2,2,8,128]{5,4,3,2,1,0:T(8,128)S(1)} %get-tuple-element.65), channel_id=1, source_target_pairs={{0,1},{1,0},{2,3},{3,2},{4,5},{5,4},{6,7},{7,6},{8,9},{9,8},{10,11... | collective-permute-start | bytes 983048 | tf_op jit(solution)/shard_map/ppermute | solution.py:758
  64.8 15.1 %collective-permute-start.10 = (f32[5,4,2,4,8,128]{5,4,3,2,1,0:T(8,128)S(1)}, f32[5,4,2,4,8,128]{5,4,3,2,1,0:T(8,128)S(1)}, u32[]{:S(2)}, u32[]{:S(2)}) collective-permute-start(f32[5,4,2,4,8,128]{5,4,3,2,1,0:T(8,128)S(1)} %get-tuple-element.61.low), channel_id=1, source_target_pairs={{4,0},{8,4},{12,8},{16,12},{20,16},{24,20},{28,24},{0,28},{5,1},{9... | collective-permute-start | bytes 1966088 | tf_op jit(solution)/shard_map/ppermute | solution.py:760
  64.8 16.6 %collective-permute-start.9 = (f32[5,4,2,4,8,128]{5,4,3,2,1,0:T(8,128)S(1)}, f32[5,4,2,4,8,128]{5,4,3,2,1,0:T(8,128)S(1)}, u32[]{:S(2)}, u32[]{:S(2)}) collective-permute-start(f32[5,4,2,4,8,128]{5,4,3,2,1,0:T(8,128)S(1)} %get-tuple-element.60.high), channel_id=1, source_target_pairs={{0,4},{4,8},{8,12},{12,16},{16,20},{20,24},{24,28},{28,0},{1,5},{5... | collective-permute-start | bytes 1966088 | tf_op jit(solution)/shard_map/ppermute | solution.py:759
  66.8 23.7 %collective-permute-start.13 = (f32[5,8,2,8,128]{4,3,2,1,0:T(8,128)S(1)}, f32[5,8,2,8,128]{4,3,2,1,0:T(8,128)S(1)}, u32[]{:S(2)}, u32[]{:S(2)}) collective-permute-start(f32[5,8,2,8,128]{4,3,2,1,0:T(8,128)S(1)} %get-tuple-element.69), channel_id=1, source_target_pairs={{0,3},{1,2},{2,1},{3,0},{4,7},{5,6},{6,5},{7,4},{8,11},{9,10},{10,... | collective-permute-start | bytes 983048 | tf_op jit(solution)/shard_map/ppermute | solution.py:758
  69.4 30.1 %collective-permute-start.14 = (f32[5,8,2,8,128]{4,3,2,1,0:T(8,128)S(1)}, f32[5,8,2,8,128]{4,3,2,1,0:T(8,128)S(1)}, u32[]{:S(2)}, u32[]{:S(2)}) collective-permute-start(f32[5,8,2,8,128]{4,3,2,1,0:T(8,128)S(1)} %get-tuple-element.70), channel_id=1, source_target_pairs={{0,2},{1,3},{2,0},{3,1},{4,6},{5,7},{6,4},{7,5},{8,10},{9,11},{10,... | collective-permute-start | bytes 983048 | tf_op jit(solution)/shard_map/ppermute | solution.py:758
  77.2 22.3 %collective-permute-start.15 = (f32[5,8,2,8,128]{4,3,2,1,0:T(8,128)S(1)}, f32[5,8,2,8,128]{4,3,2,1,0:T(8,128)S(1)}, u32[]{:S(2)}, u32[]{:S(2)}) collective-permute-start(f32[5,8,2,8,128]{4,3,2,1,0:T(8,128)S(1)} %get-tuple-element.71), channel_id=1, source_target_pairs={{0,1},{1,0},{2,3},{3,2},{4,5},{5,4},{6,7},{7,6},{8,9},{9,8},{10,11... | collective-permute-start | bytes 983048 | tf_op jit(solution)/shard_map/ppermute | solution.py:758

commit v4 on v3

--- a/solution.py
+++ b/solution.py
@@ -80,11 +80,9 @@
 
 def move_lanes(rows, matrix):
     top = rows.astype(jnp.bfloat16)
-    rest = rows - top.astype(jnp.float32)
-    middle = rest.astype(jnp.bfloat16)
-    low = (rest - middle.astype(jnp.float32)).astype(jnp.bfloat16)
+    rest = (rows - top.astype(jnp.float32)).astype(jnp.bfloat16)
     product = lambda part: jnp.dot(part, matrix, preferred_element_type=jnp.float32)
-    return (product(top) + product(middle)) + product(low)
+    return product(top) + product(rest)
 
 
 def one_hot_scratch():

time: 103 us -> 102 us (level)
  Pallas kernels: 42.5 us -> 41.4 us
where the time goes in v4:
time: 102 us
  Pallas kernels  41.4 us (41%)
  waiting for transfers between devices  30.3 us (30%)
  starting transfers between devices  25 us (25%)
  local copies, waits for them, and re-layouts  4.14 us (4%)
    ppermute x10, waiting for transfers between devices, body(): lax.ppermute(array, 'buddy', [(i, i ^ d) for i in range(groups)])  26.5 us
    pallas_call x2, Pallas kernels, half_step(): pl.pallas_call(functools.partial(kernel, others), out_shape=outs, in_spec...  19.5 us
    ppermute x10, starting transfers between devices, body(): lax.ppermute(array, 'buddy', [(i, i ^ d) for i in range(groups)])  18 us
    pallas_call x1, Pallas kernels, recover(): pl.pallas_call(recover_kernel, out_shape=shape(5, 2 * DEPTH, 4 * ROWS, 2...  8.75 us
    unnamed x17, local copies, waits for them, and re-layouts  4.05 us
    pallas_call x1, Pallas kernels, place(): pl.pallas_call(functools.partial(place_kernel, len(pieces)), out_shape=[h...  3.8 us
    ppermute x1, starting transfers between devices, body(): lax.ppermute(sent[-1], 'buddy', [(i, i ^ groups - 1) for i in range(group...  3.57 us
    pallas_call x2, Pallas kernels, prepare(): pl.pallas_call(functools.partial(prepare_kernel, half, len(firsts)), out_...  3.45 us
  transfers between devices with their start and end apart: 16, of which 7 were waited for; matrix products, arithmetic and copies ran while one was open for 0% of the time, Pallas kernels for 37%

profile of v4, /device:TPU:0, one launch (start us, length us, event | category | flops | bytes accessed | tf_op | source)
XLA Modules:
  0.0 101.7 jit_solution(2122184732456206532)
XLA Ops:
  0.6 0.0 copy-start
  0.6 1.3 %copy-done = f32[8,5,8,4,256]{4,3,2,1,0:T(4,128)S(1)} copy-done((f32[8,5,8,4,256]{4,3,2,1,0:T(4,128)S(1)}, f32[8,5,8,4,256]{4,3,2,1,0:T(4,128)}, u32[]{:S(2)}) %copy-start) | copy-done | bytes 1310744
  1.9 1.3 %copy-done.2 = f32[1,5,8,32,256]{4,3,2,1,0:T(8,128)S(1)} copy-done((f32[1,5,8,32,256]{4,3,2,1,0:T(8,128)S(1)}, f32[1,5,8,32,256]{4,3,2,1,0:T(8,128)}, u32[]{:S(2)}) %copy-start.2) | copy-done | bytes 1310744
  3.3 1.2 %prepare.3.refs_10_.refs_9_ = f32[2,5,4,2,4,8,128]{6,5,4,3,2,1,0:T(8,128)S(1)} custom-call(f32[8,5,8,4,256]{4,3,2,1,0:T(4,128)S(1)} %copy-done, f32[5,8,32,256]{3,2,1,0:T(8,128)S(1)} %bitcast.4), custom_call_target="tpu_custom_call" | custom-call | bytes 1 | tf_op jit(solution)/shard_map/prepare/pallas_call | solution.py:365
  4.5 0.5 collective-permute-start.5
  5.0 0.1 reshape.14
  5.1 0.1 pad_maximum_fusion
  5.2 2.6 %collective-permute-start = (f32[8]{0:T(128)S(1)}, f32[8]{0:T(128)S(1)}, u32[]{:S(2)}, u32[]{:S(2)}) collective-permute-start(f32[8]{0:T(128)S(1)} %pad_maximum_fusion), channel_id=1, source_target_pairs={{0,1},{1,0},{2,3},{3,2},{4,5},{5,4},{6,7},{7,6},{8,9},{9,8},{10,11... | collective-permute-start | bytes 104 | tf_op jit(solution)/shard_map/ppermute | solution.py:756
  7.8 2.6 %collective-permute-start.1 = (f32[8]{0:T(128)S(1)}, f32[8]{0:T(128)S(1)}, u32[]{:S(2)}, u32[]{:S(2)}) collective-permute-start(f32[8]{0:T(128)S(1)} %pad_maximum_fusion), channel_id=1, source_target_pairs={{0,2},{1,3},{2,0},{3,1},{4,6},{5,7},{6,4},{7,5},{8,10},{9,11},{10,... | collective-permute-start | bytes 104 | tf_op jit(solution)/shard_map/ppermute | solution.py:756
  10.4 0.0 collective-permute-start.2
  10.4 2.2 %gather_slots.1 = (f32[3,5,8,4,256]{4,3,2,1,0:T(4,128)}, f32[3,5,8,4,256]{4,3,2,1,0:T(4,128)}, f32[3,5,8,4,256]{4,3,2,1,0:T(4,128)}) custom-call(s32[1]{0:T(128)} %bitcast.me_ref.refs_0_, s32[4,8]{1,0:T(4,128)S(1)} %copy-done.4, f32[8,5,8,4,256]{4,3,2,1,0:T(4,128)S(1)} %copy-done.1), custom_call_target="tpu_custom_call" | custom-call | bytes 1 | tf_op jit(solution)/shard_map/gather_slots/pallas_call | solution.py:316
  12.6 0.0 collective-permute-done.refs_0_.refs_5_
  12.6 0.0 collective-permute-done.1.refs_1_.refs_6_
  12.6 3.1 %collective-permute-done.2.refs_2_.refs_7_ = f32[8]{0:T(128)S(1)} collective-permute-done((f32[8]{0:T(128)S(1)}, f32[8]{0:T(128)S(1)}, u32[]{:S(2)}, u32[]{:S(2)}) %collective-permute-start.2) | collective-permute-done | bytes 64 | tf_op jit(solution)/shard_map/ppermute | solution.py:756
  15.7 0.0 collective-permute-start.4
  15.7 0.1 copy.9.refs_4_
  15.8 1.3 %copy-done.3 = f32[1,5,8,32,256]{4,3,2,1,0:T(8,128)S(1)} copy-done((f32[1,5,8,32,256]{4,3,2,1,0:T(8,128)S(1)}, f32[1,5,8,32,256]{4,3,2,1,0:T(8,128)}, u32[]{:S(2)}) %copy-start.3) | copy-done | bytes 1310744
  17.1 2.3 %prepare.2.refs_9_ = f32[2,5,4,2,4,8,128]{6,5,4,3,2,1,0:T(8,128)} custom-call(f32[8,5,8,4,256]{4,3,2,1,0:T(4,128)S(1)} %copy-done.1, f32[5,8,32,256]{3,2,1,0:T(8,128)S(1)} %bitcast.5, f32[8]{0:T(128)S(1)} %collective-permute-done.refs_0_.refs_5_, f32[8]{0:T(128)S(1)} %collective-permute-done.1.refs_1_.refs_6_, f32[8]{0:T(128)S(1)} %collective-permute-done.2.refs_2_.refs_7_), custom_call_target="tpu_custom_call" | custom-call | bytes 1 | tf_op jit(solution)/shard_map/prepare/pallas_call | solution.py:365
  19.4 0.9 collective-permute-start.3
  20.3 3.6 %collective-permute-start.7 = (f32[3,5,8,4,256]{4,3,2,1,0:T(4,128)}, f32[3,5,8,4,256]{4,3,2,1,0:T(4,128)}, u32[]{:S(2)}, u32[]{:S(2)}) collective-permute-start(f32[3,5,8,4,256]{4,3,2,1,0:T(4,128)} %get-tuple-element.55), channel_id=1, source_target_pairs={{0,3},{3,0},{4,7},{7,4},{8,11},{11,8},{12,15},{15,12},{16,19},{19,... | collective-permute-start | bytes 1474568 | tf_op jit(solution)/shard_map/ppermute | solution.py:771
  23.9 0.1 collective-permute-start.6
  23.9 0.0 collective-permute-done.5.refs_8_
  24.0 12.0 %first_half.1 = (f32[5,4,2,2,8,128]{5,4,3,2,1,0:T(8,128)S(1)}, f32[5,4,2,2,8,128]{5,4,3,2,1,0:T(8,128)S(1)}, f32[5,2,2,6,8,128]{5,4,3,2,1,0:T(8,128)S(1)}, f32[5...) custom-call(s32[1]{0:T(128)} %bitcast.me_ref.refs_0_, ...), custom_call_target="tpu_custom_call" | custom-call | bytes 12 | tf_op jit(solution)/shard_map/first_half/pallas_call | solution.py:498
  35.9 1.5 %collective-permute-start.8 = (f32[3,5,8,4,256]{4,3,2,1,0:T(4,128)}, f32[3,5,8,4,256]{4,3,2,1,0:T(4,128)}, u32[]{:S(2)}, u32[]{:S(2)}) collective-permute-start(f32[3,5,8,4,256]{4,3,2,1,0:T(4,128)} %get-tuple-element.55), channel_id=1, source_target_pairs={{1,2},{2,1},{5,6},{6,5},{9,10},{10,9},{13,14},{14,13},{17,18},{18,... | collective-permute-start | bytes 1474568 | tf_op jit(solution)/shard_map/ppermute | solution.py:778
  37.4 4.6 %collective-permute-done.4.refs_0_.rest_0_ = f32[3,5,8,4,256]{4,3,2,1,0:T(4,128)S(1)} collective-permute-done((f32[3,5,8,4,256]{4,3,2,1,0:T(4,128)}, f32[3,5,8,4,256]{4,3,2,1,0:T(4,128)S(1)}, u32[]{:S(2)}, u32[]{:S(2)}) %collective-permute-start.4) | collective-permute-done | bytes 491552 | tf_op jit(solution)/shard_map/ppermute | solution.py:756
  42.0 0.1 collective-permute-start.11
  42.0 0.0 collective-permute-done.3.refs_8_
  42.0 7.6 %second_half.1 = (f32[5,4,2,2,8,128]{5,4,3,2,1,0:T(8,128)S(1)}, f32[5,4,2,2,8,128]{5,4,3,2,1,0:T(8,128)S(1)}) custom-call(s32[1]{0:T(128)} %bitcast.me_ref.refs_0_, s32[4,8]{1,0:T(4,128)S(1)} %copy-done.4, s32[1,16]{1,0:T(1,128)S(1)} %copy-done.6, s32[2,1,3]{2,1,0:T(1,128)S(1)} %copy-done.5, f32[2,1]{1,0:T(2,128)S(1)} %copy.9.refs_4_, ...), custom_call_target="tpu_custom_call" | custom-call | bytes 8 | tf_op jit(solution)/shard_map/second_half/pallas_call | solution.py:498
  49.6 2.0 %collective-permute-start.12 = (f32[5,4,2,2,8,128]{5,4,3,2,1,0:T(8,128)S(1)}, f32[5,4,2,2,8,128]{5,4,3,2,1,0:T(8,128)S(1)}, u32[]{:S(2)}, u32[]{:S(2)}) collective-permute-start(f32[5,4,2,2,8,128]{5,4,3,2,1,0:T(8,128)S(1)} %get-tuple-element.65), channel_id=1, source_target_pairs={{0,1},{1,0},{2,3},{3,2},{4,5},{5,4},{6,7},{7,6},{8,9},{9,8},{10,11... | collective-permute-start | bytes 983048 | tf_op jit(solution)/shard_map/ppermute | solution.py:756
  51.6 0.0 collective-permute-done.7.rest_2_
  51.6 8.8 %collective-permute-done.6.rest_1_ = f32[3,5,8,4,256]{4,3,2,1,0:T(4,128)} collective-permute-done((f32[3,5,8,4,256]{4,3,2,1,0:T(4,128)}, f32[3,5,8,4,256]{4,3,2,1,0:T(4,128)}, u32[]{:S(2)}, u32[]{:S(2)}) %collective-permute-start.6) | collective-permute-done | bytes 491552 | tf_op jit(solution)/shard_map/ppermute | solution.py:756
  60.4 0.0 collective-permute-done.8.rest_3_
  60.4 3.8 %place.1 = (f32[5,4,2,4,8,128]{5,4,3,2,1,0:T(8,128)S(1)}, f32[5,4,2,4,8,128]{5,4,3,2,1,0:T(8,128)S(1)}) custom-call(s32[1]{0:T(128)} %bitcast.me_ref.refs_0_, s32[4,8]{1,0:T(4,128)S(1)} %copy-done.4, f32[3,5,8,4,256]{4,3,2,1,0:T(4,128)S(1)} %collective-permute-done.4.refs_0_.rest_0_, f32[3,5,8,4,256]{4,3,2,1,0:T(4,128)} %collective-permute-done.6.rest_1_, ...), custom_call_target="tpu_custom_call" | custom-call | bytes 3 | tf_op jit(solution)/shard_map/place/pallas_call | solution.py:679
  64.2 0.1 collective-permute-start.10
  64.3 0.5 collective-permute-start.9
  64.8 0.0 collective-permute-done.11.arrived_low
  64.8 0.9 collective-permute-done.12.arrived_high
  65.7 0.8 share.1
  66.6 2.6 %collective-permute-start.13 = (f32[5,8,2,8,128]{4,3,2,1,0:T(8,128)S(1)}, f32[5,8,2,8,128]{4,3,2,1,0:T(8,128)S(1)}, u32[]{:S(2)}, u32[]{:S(2)}) collective-permute-start(f32[5,8,2,8,128]{4,3,2,1,0:T(8,128)S(1)} %get-tuple-element.69), channel_id=1, source_target_pairs={{0,3},{1,2},{2,1},{3,0},{4,7},{5,6},{6,5},{7,4},{8,11},{9,10},{10,... | collective-permute-start | bytes 983048 | tf_op jit(solution)/shard_map/ppermute | solution.py:756
  69.2 7.5 %collective-permute-start.14 = (f32[5,8,2,8,128]{4,3,2,1,0:T(8,128)S(1)}, f32[5,8,2,8,128]{4,3,2,1,0:T(8,128)S(1)}, u32[]{:S(2)}, u32[]{:S(2)}) collective-permute-start(f32[5,8,2,8,128]{4,3,2,1,0:T(8,128)S(1)} %get-tuple-element.70), channel_id=1, source_target_pairs={{0,2},{1,3},{2,0},{3,1},{4,6},{5,7},{6,4},{7,5},{8,10},{9,11},{10,... | collective-permute-start | bytes 983048 | tf_op jit(solution)/shard_map/ppermute | solution.py:756
  76.7 0.5 collective-permute-start.15
  77.2 2.2 %collective-permute-done.10.after = f32[5,4,2,4,8,128]{5,4,3,2,1,0:T(8,128)S(1)} collective-permute-done((f32[5,4,2,4,8,128]{5,4,3,2,1,0:T(8,128)S(1)}, f32[5,4,2,4,8,128]{5,4,3,2,1,0:T(8,128)S(1)}, u32[]{:S(2)}, u32[]{:S(2)}) %collective-permute-start.10) | collective-permute-done | bytes 655392 | tf_op jit(solution)/shard_map/ppermute | solution.py:758
  79.4 1.6 %collective-permute-done.9.before = f32[5,4,2,4,8,128]{5,4,3,2,1,0:T(8,128)S(1)} collective-permute-done((f32[5,4,2,4,8,128]{5,4,3,2,1,0:T(8,128)S(1)}, f32[5,4,2,4,8,128]{5,4,3,2,1,0:T(8,128)S(1)}, u32[]{:S(2)}, u32[]{:S(2)}) %collective-permute-start.9) | collective-permute-done | bytes 655392 | tf_op jit(solution)/shard_map/ppermute | solution.py:757
  81.0 8.8 %recover.1 = f32[5,8,32,256]{3,2,1,0:T(8,128)} custom-call(s32[2,1,3]{2,1,0:T(1,128)S(1)} %copy-done.5, f32[5,4,2,4,8,128]{5,4,3,2,1,0:T(8,128)S(1)} %collective-permute-done.9.before, f32[5,4,2,4,8,128]{5,4,3,2,1,0:T(8,128)S(1)} %get-tuple-element.61.low, f32[5,4,2,4,8,128]{5,4,3,2,1,0:T(8,128)S(1)} %get-tuple-element.60.high, ...), custom_call_target="tpu_custom_call" | custom-call | bytes 10 | tf_op jit(solution)/shard_map/recover/pallas_call | solution.py:728
  89.7 0.0 collective-permute-done.13.rest_1_
  89.8 9.1 %collective-permute-done.14.rest_2_ = f32[5,8,2,8,128]{4,3,2,1,0:T(8,128)S(1)} collective-permute-done((f32[5,8,2,8,128]{4,3,2,1,0:T(8,128)S(1)}, f32[5,8,2,8,128]{4,3,2,1,0:T(8,128)S(1)}, u32[]{:S(2)}, u32[]{:S(2)}) %collective-permute-start.14) | collective-permute-done | bytes 327712 | tf_op jit(solution)/shard_map/ppermute | solution.py:756
  98.9 0.0 collective-permute-done.15.rest_3_
  98.9 2.8 %collect.1 = f32[8,5,8,2,256]{4,3,2,1,0:T(2,128)} custom-call(s32[1]{0:T(128)} %bitcast.me_ref.refs_0_, s32[1,16]{1,0:T(1,128)S(1)} %copy-done.6, f32[5,8,2,8,128]{4,3,2,1,0:T(8,128)S(1)} %get-tuple-element.68.rest_0_, f32[5,8,2,8,128]{4,3,2,1,0:T(8,128)S(1)} %collective-permute-done.13.rest_1_, f32[5,8,2,8,128]{4,3,2,1,0:T(8,128)S(1)} %collective-permute-done.14.rest_2_, ...), custom_call_target="tpu_custom_call" | custom-call | bytes 2 | tf_op jit(solution)/shard_map/collect/pallas_call | solution.py:620
  (14 shorter events, 0.0 us)
Async XLA Ops:
  0.6 1.3 %copy-start = (f32[8,5,8,4,256]{4,3,2,1,0:T(4,128)S(1)}, f32[8,5,8,4,256]{4,3,2,1,0:T(4,128)}, u32[]{:S(2)}) copy-start(f32[8,5,8,4,256]{4,3,2,1,0:T(4,128)} %checkpoint.5) | copy-start | bytes 3932164
  1.9 1.3 %copy-start.2 = (f32[1,5,8,32,256]{4,3,2,1,0:T(8,128)S(1)}, f32[1,5,8,32,256]{4,3,2,1,0:T(8,128)}, u32[]{:S(2)}) copy-start(f32[1,5,8,32,256]{4,3,2,1,0:T(8,128)} %param.8) | copy-start | bytes 3932164
  3.3 1.7 %copy-start.5 = (s32[2,1,3]{2,1,0:T(1,128)S(1)}, s32[2,1,3]{2,1,0:T(1,128)}, u32[]{:S(2)}) copy-start(s32[2,1,3]{2,1,0:T(1,128)} %levels_ref.1) | copy-start | bytes 76
  3.3 1.8 %copy-start.7 = (f32[2,1]{0,1:T(1,128)S(1)}, f32[2,1]{0,1:T(1,128)}, u32[]{:S(2)}) copy-start(f32[2,1]{0,1:T(1,128)} %param.10) | copy-start | bytes 28
  3.3 7.1 %copy-start.1 = (f32[8,5,8,4,256]{4,3,2,1,0:T(4,128)S(1)}, f32[8,5,8,4,256]{4,3,2,1,0:T(4,128)}, u32[]{:S(2)}) copy-start(f32[8,5,8,4,256]{4,3,2,1,0:T(4,128)} %checkpoint.5) | copy-start | bytes 3932164
  3.3 7.1 %copy-start.4 = (s32[4,8]{1,0:T(4,128)S(1)}, s32[4,8]{1,0:T(4,128)}, u32[]{:S(2)}) copy-start(s32[4,8]{1,0:T(4,128)} %block_ref.3) | copy-start | bytes 388
  4.5 19.5 %collective-permute-start.5 = (f32[2,5,4,2,4,8,128]{6,5,4,3,2,1,0:T(8,128)S(1)}, f32[2,5,4,2,4,8,128]{6,5,4,3,2,1,0:T(8,128)}, u32[]{:S(2)}, u32[]{:S(2)}) collective-permute-start(f32[2,5,4,2,4,8,128]{6,5,4,3,2,1,0:T(8,128)S(1)} %prepare.3.refs_10_.refs_9_), channel_id=1, source_target_pairs={{0,4},{4,8},{8,12},{12,16},{16,20},{20,24},{24,28},{28,0},{1,5},{5... | collective-permute-start | bytes 3932168 | tf_op jit(solution)/shard_map/ppermute | solution.py:757
  5.2 7.4 %collective-permute-start = (f32[8]{0:T(128)S(1)}, f32[8]{0:T(128)S(1)}, u32[]{:S(2)}, u32[]{:S(2)}) collective-permute-start(f32[8]{0:T(128)S(1)} %pad_maximum_fusion), channel_id=1, source_target_pairs={{0,1},{1,0},{2,3},{3,2},{4,5},{5,4},{6,7},{7,6},{8,9},{9,8},{10,11... | collective-permute-start | bytes 104 | tf_op jit(solution)/shard_map/ppermute | solution.py:756
  7.8 4.8 %collective-permute-start.1 = (f32[8]{0:T(128)S(1)}, f32[8]{0:T(128)S(1)}, u32[]{:S(2)}, u32[]{:S(2)}) collective-permute-start(f32[8]{0:T(128)S(1)} %pad_maximum_fusion), channel_id=1, source_target_pairs={{0,2},{1,3},{2,0},{3,1},{4,6},{5,7},{6,4},{7,5},{8,10},{9,11},{10,... | collective-permute-start | bytes 104 | tf_op jit(solution)/shard_map/ppermute | solution.py:756
  10.4 5.3 %collective-permute-start.2 = (f32[8]{0:T(128)S(1)}, f32[8]{0:T(128)S(1)}, u32[]{:S(2)}, u32[]{:S(2)}) collective-permute-start(f32[8]{0:T(128)S(1)} %pad_maximum_fusion), channel_id=1, source_target_pairs={{0,3},{1,2},{2,1},{3,0},{4,7},{5,6},{6,5},{7,4},{8,11},{9,10},{10,... | collective-permute-start | bytes 104 | tf_op jit(solution)/shard_map/ppermute | solution.py:756
  15.7 26.3 %collective-permute-start.4 = (f32[3,5,8,4,256]{4,3,2,1,0:T(4,128)}, f32[3,5,8,4,256]{4,3,2,1,0:T(4,128)S(1)}, u32[]{:S(2)}, u32[]{:S(2)}) collective-permute-start(f32[3,5,8,4,256]{4,3,2,1,0:T(4,128)} %get-tuple-element.43), channel_id=1, source_target_pairs={{0,1},{1,0},{2,3},{3,2},{4,5},{5,4},{6,7},{7,6},{8,9},{9,8},{10,11... | collective-permute-start | bytes 1474568 | tf_op jit(solution)/shard_map/ppermute | solution.py:756
  15.8 1.3 %copy-start.3 = (f32[1,5,8,32,256]{4,3,2,1,0:T(8,128)S(1)}, f32[1,5,8,32,256]{4,3,2,1,0:T(8,128)}, u32[]{:S(2)}) copy-start(f32[1,5,8,32,256]{4,3,2,1,0:T(8,128)} %param.8) | copy-start | bytes 3932164
  17.1 6.8 %copy-start.6 = (s32[1,16]{1,0:T(1,128)S(1)}, s32[1,16]{1,0:T(1,128)}, u32[]{:S(2)}) copy-start(s32[1,16]{1,0:T(1,128)} %owner_ref.3) | copy-start | bytes 196
  19.4 22.7 %collective-permute-start.3 = (f32[2,5,4,2,4,8,128]{6,5,4,3,2,1,0:T(8,128)}, f32[2,5,4,2,4,8,128]{6,5,4,3,2,1,0:T(8,128)}, u32[]{:S(2)}, u32[]{:S(2)}) collective-permute-start(f32[2,5,4,2,4,8,128]{6,5,4,3,2,1,0:T(8,128)} %prepare.2.refs_9_), channel_id=1, source_target_pairs={{4,0},{8,4},{12,8},{16,12},{20,16},{24,20},{28,24},{0,28},{5,1},{9... | collective-permute-start | bytes 3932168 | tf_op jit(solution)/shard_map/ppermute | solution.py:758
  20.3 31.4 %collective-permute-start.7 = (f32[3,5,8,4,256]{4,3,2,1,0:T(4,128)}, f32[3,5,8,4,256]{4,3,2,1,0:T(4,128)}, u32[]{:S(2)}, u32[]{:S(2)}) collective-permute-start(f32[3,5,8,4,256]{4,3,2,1,0:T(4,128)} %get-tuple-element.55), channel_id=1, source_target_pairs={{0,3},{3,0},{4,7},{7,4},{8,11},{11,8},{12,15},{15,12},{16,19},{19,... | collective-permute-start | bytes 1474568 | tf_op jit(solution)/shard_map/ppermute | solution.py:771
  23.9 36.6 %collective-permute-start.6 = (f32[3,5,8,4,256]{4,3,2,1,0:T(4,128)}, f32[3,5,8,4,256]{4,3,2,1,0:T(4,128)}, u32[]{:S(2)}, u32[]{:S(2)}) collective-permute-start(f32[3,5,8,4,256]{4,3,2,1,0:T(4,128)} %get-tuple-element.54), channel_id=1, source_target_pairs={{0,2},{1,3},{2,0},{3,1},{4,6},{5,7},{6,4},{7,5},{8,10},{9,11},{10,... | collective-permute-start | bytes 1474568 | tf_op jit(solution)/shard_map/ppermute | solution.py:756
  35.9 24.5 %collective-permute-start.8 = (f32[3,5,8,4,256]{4,3,2,1,0:T(4,128)}, f32[3,5,8,4,256]{4,3,2,1,0:T(4,128)}, u32[]{:S(2)}, u32[]{:S(2)}) collective-permute-start(f32[3,5,8,4,256]{4,3,2,1,0:T(4,128)} %get-tuple-element.55), channel_id=1, source_target_pairs={{1,2},{2,1},{5,6},{6,5},{9,10},{10,9},{13,14},{14,13},{17,18},{18,... | collective-permute-start | bytes 1474568 | tf_op jit(solution)/shard_map/ppermute | solution.py:778
  42.0 22.8 %collective-permute-start.11 = (f32[5,4,2,2,8,128]{5,4,3,2,1,0:T(8,128)S(1)}, f32[5,4,2,2,8,128]{5,4,3,2,1,0:T(8,128)S(1)}, u32[]{:S(2)}, u32[]{:S(2)}) collective-permute-start(f32[5,4,2,2,8,128]{5,4,3,2,1,0:T(8,128)S(1)} %get-tuple-element.63), channel_id=1, source_target_pairs={{0,1},{1,0},{2,3},{3,2},{4,5},{5,4},{6,7},{7,6},{8,9},{9,8},{10,11... | collective-permute-start | bytes 983048 | tf_op jit(solution)/shard_map/ppermute | solution.py:756
  49.6 16.1 %collective-permute-start.12 = (f32[5,4,2,2,8,128]{5,4,3,2,1,0:T(8,128)S(1)}, f32[5,4,2,2,8,128]{5,4,3,2,1,0:T(8,128)S(1)}, u32[]{:S(2)}, u32[]{:S(2)}) collective-permute-start(f32[5,4,2,2,8,128]{5,4,3,2,1,0:T(8,128)S(1)} %get-tuple-element.65), channel_id=1, source_target_pairs={{0,1},{1,0},{2,3},{3,2},{4,5},{5,4},{6,7},{7,6},{8,9},{9,8},{10,11... | collective-permute-start | bytes 983048 | tf_op jit(solution)/shard_map/ppermute | solution.py:756
  64.2 15.1 %collective-permute-start.10 = (f32[5,4,2,4,8,128]{5,4,3,2,1,0:T(8,128)S(1)}, f32[5,4,2,4,8,128]{5,4,3,2,1,0:T(8,128)S(1)}, u32[]{:S(2)}, u32[]{:S(2)}) collective-permute-start(f32[5,4,2,4,8,128]{5,4,3,2,1,0:T(8,128)S(1)} %get-tuple-element.61.low), channel_id=1, source_target_pairs={{4,0},{8,4},{12,8},{16,12},{20,16},{24,20},{28,24},{0,28},{5,1},{9... | collective-permute-start | bytes 1966088 | tf_op jit(solution)/shard_map/ppermute | solution.py:758
  64.3 16.7 %collective-permute-start.9 = (f32[5,4,2,4,8,128]{5,4,3,2,1,0:T(8,128)S(1)}, f32[5,4,2,4,8,128]{5,4,3,2,1,0:T(8,128)S(1)}, u32[]{:S(2)}, u32[]{:S(2)}) collective-permute-start(f32[5,4,2,4,8,128]{5,4,3,2,1,0:T(8,128)S(1)} %get-tuple-element.60.high), channel_id=1, source_target_pairs={{0,4},{4,8},{8,12},{12,16},{16,20},{20,24},{24,28},{28,0},{1,5},{5... | collective-permute-start | bytes 1966088 | tf_op jit(solution)/shard_map/ppermute | solution.py:757
  66.6 23.2 %collective-permute-start.13 = (f32[5,8,2,8,128]{4,3,2,1,0:T(8,128)S(1)}, f32[5,8,2,8,128]{4,3,2,1,0:T(8,128)S(1)}, u32[]{:S(2)}, u32[]{:S(2)}) collective-permute-start(f32[5,8,2,8,128]{4,3,2,1,0:T(8,128)S(1)} %get-tuple-element.69), channel_id=1, source_target_pairs={{0,3},{1,2},{2,1},{3,0},{4,7},{5,6},{6,5},{7,4},{8,11},{9,10},{10,... | collective-permute-start | bytes 983048 | tf_op jit(solution)/shard_map/ppermute | solution.py:756
  69.2 29.7 %collective-permute-start.14 = (f32[5,8,2,8,128]{4,3,2,1,0:T(8,128)S(1)}, f32[5,8,2,8,128]{4,3,2,1,0:T(8,128)S(1)}, u32[]{:S(2)}, u32[]{:S(2)}) collective-permute-start(f32[5,8,2,8,128]{4,3,2,1,0:T(8,128)S(1)} %get-tuple-element.70), channel_id=1, source_target_pairs={{0,2},{1,3},{2,0},{3,1},{4,6},{5,7},{6,4},{7,5},{8,10},{9,11},{10,... | collective-permute-start | bytes 983048 | tf_op jit(solution)/shard_map/ppermute | solution.py:756
  76.7 22.2 %collective-permute-start.15 = (f32[5,8,2,8,128]{4,3,2,1,0:T(8,128)S(1)}, f32[5,8,2,8,128]{4,3,2,1,0:T(8,128)S(1)}, u32[]{:S(2)}, u32[]{:S(2)}) collective-permute-start(f32[5,8,2,8,128]{4,3,2,1,0:T(8,128)S(1)} %get-tuple-element.71), channel_id=1, source_target_pairs={{0,1},{1,0},{2,3},{3,2},{4,5},{5,4},{6,7},{7,6},{8,9},{9,8},{10,11... | collective-permute-start | bytes 983048 | tf_op jit(solution)/shard_map/ppermute | solution.py:756
